TPU v7x, 512 devices: a whole 4x4x16 slice. The times are simulated.
512 devices in a mesh: mp: 32 (over y, x, core), dp: 16 (over z).
Axes of the slice: x: 4, y: 4, z: 16, core: 2. Of those that a mesh axis runs over, the one named last changes fastest.
Arguments:
- momentum: float32 [8192, 14336], P('mp', 'dp'), may hold values from -120 to 120
- gradient: bfloat16 [8192, 14336], P('mp', 'dp'), may hold values from -6 to 6
- weight: bfloat16 [8192, 14336], P('mp', 'dp'), may hold values from -6 to 6
- right_basis: float32 [14336, 256], P('dp'), may hold values from -0.046875 to 0.046875
Outputs:
- new_weight: bfloat16 [8192, 14336], P('mp', 'dp')
- new_momentum: float32 [8192, 14336], P('mp', 'dp')
- new_basis: float32 [14336, 256], P('dp')
All inputs are finite; a program needn't handle non-finite values.
Results may differ from a plain program's by a relative error of at most 0.001.
Values sent between devices are 32-bit elements; how exact they have to be, the bound alone decides.
No kernel may reach another device: no remote copies, remote signals or barrier semaphores. Data moves between devices by JAX's collectives and lax.ppermute only.
A program may use at most 64 MiB of HBM per device.

v0:
```python
import math

import jax
import jax.numpy as jnp
from jax import lax
from jax.sharding import PartitionSpec as P

ROWS = 8192
COLS = 14336
RANK = 256
ITERS = 2


highest = lax.Precision.HIGHEST
retain = 0.95
step_size = 0.5
norm_eps = 1e-06


def product(first, second):
    return jnp.dot(first, second, precision=highest, preferred_element_type=jnp.float32)


def inner_rows(first, second):
    return lax.dot_general(
        first,
        second,
        (((0,), (0,)), ((), ())),
        precision=highest,
        preferred_element_type=jnp.float32,
    )


def outer_rows(first, second):
    return lax.dot_general(
        first,
        second,
        (((1,), (1,)), ((), ())),
        precision=highest,
        preferred_element_type=jnp.float32,
    )


def orthonormal(left_part, gram):
    factor = jnp.linalg.cholesky(gram)
    return lax.linalg.triangular_solve(
        factor, left_part, left_side=False, lower=True, transpose_a=True
    )


def body(momentum, gradient, weight, right_basis):
    buffer = momentum + gradient.astype(jnp.float32)
    basis = right_basis
    left = None
    right = None
    own_squares = None
    for turn_index in range(ITERS):
        left = lax.psum(product(buffer, basis), "dp")
        gram = lax.psum(inner_rows(left, left), "mp")
        left = orthonormal(left, gram)
        right = lax.psum(inner_rows(buffer, left), "mp")
        own_squares = jnp.sum(right * right, axis=0)
        squares = lax.psum(own_squares, "dp")
        basis = right / (jnp.sqrt(squares) + norm_eps)
    new_momentum = buffer - (1.0 - retain) * outer_rows(left, right)
    update = outer_rows(left, basis)
    scale = step_size * math.sqrt(ROWS * COLS / RANK)
    new_weight = (weight.astype(jnp.float32) - scale * update).astype(jnp.bfloat16)
    return (new_weight, new_momentum, basis)


def solution(mesh):
    in_specs = (P("mp", "dp"), P("mp", "dp"), P("mp", "dp"), P("dp", None))
    out_specs = (P("mp", "dp"), P("mp", "dp"), P("dp", None))
    return jax.shard_map(body, mesh=mesh, in_specs=in_specs, out_specs=out_specs, check_vma=False)
```

profile of v0, /device:TPU:1, one launch (start us, length us, event | category | flops | bytes accessed | tf_op | source)
XLA Modules:
  0.0 1023.0 jit_solution(4047198545692508839)
XLA Ops:
  8.3 3.0 fusion.35
  11.5 131.7 %all-reduce.8.cloned.1.call-done = f32[256,256]{1,0:T(8,128)} async-done(((f32[256,256]{1,0:T(8,128)}), f32[256,256]{1,0:T(8,128)}) %all-reduce.8.cloned.1.call-update) | async-done | bytes 262160 | tf_op jit(solution)/shard_map/psum | solution.py:58
  145.5 139.9 %all-reduce.10.cloned.1.call-done = f32[256,256]{0,1:T(8,128)} async-done(((f32[256,256]{0,1:T(8,128)}), f32[256,256]{0,1:T(8,128)}) %all-reduce.10.cloned.1.call-update) | async-done | bytes 262160 | tf_op jit(solution)/shard_map/psum | solution.py:59
  286.6 11.7 %cholesky.130 = f32[128,128]{1,0:T(8,128)S(1)} custom-call(f32[128,128]{1,0:T(8,128)S(1)} %cholesky.194), custom_call_target="Cholesky" | custom-call | tf_op jit(solution)/shard_map/jit(cholesky)/cholesky | solution.py:45
  298.4 9.8 custom-call.13
  308.7 11.7 %cholesky.147 = f32[128,128]{1,0:T(8,128)S(1)} custom-call(f32[128,128]{1,0:T(8,128)S(1)} %convolution_subtract_fusion.3), custom_call_target="Cholesky" | custom-call | tf_op jit(solution)/shard_map/jit(cholesky)/cholesky | solution.py:45
  322.6 4.1 while.4
  326.7 19.7 %custom-call.14 = f32[2,128,128]{1,2,0:T(8,128)S(1)} custom-call(f32[2,128,128]{2,1,0:T(8,128)S(1)} %get-tuple-element.19), custom_call_target="InvertDiagBlocksLowerTriangular" | custom-call | tf_op jit(solution)/shard_map/triangular_solve/custom-call.0 | solution.py:46
  347.4 2.5 fusion.6
  350.0 134.7 %all-reduce.12.cloned.1.call-done = f32[896,256]{1,0:T(8,128)} async-done(((f32[896,256]{1,0:T(8,128)}), f32[896,256]{1,0:T(8,128)}) %all-reduce.12.cloned.1.call-update) | async-done | bytes 917520 | tf_op jit(solution)/shard_map/psum | solution.py:61
  486.2 24.3 %psum.59 = f32[256]{0:T(256)S(1)} all-reduce(f32[256]{0:T(256)S(1)} %multiply_reduce_fusion.1), channel_id=1, replica_groups=mesh['mp'=32,'dp'=16] {'dp'}, use_global_device_ids=true, to_apply=%region_8.11 | all-reduce | flops 256 | bytes 2048 | tf_op jit(solution)/shard_map/psum | solution.py:63
  512.4 129.2 %all-reduce.14.cloned.1.call-done = f32[256,256]{1,0:T(8,128)} async-done(((f32[256,256]{1,0:T(8,128)}), f32[256,256]{1,0:T(8,128)}) %all-reduce.14.cloned.1.call-update) | async-done | bytes 262160 | tf_op jit(solution)/shard_map/psum | solution.py:58
  641.5 2.3 fusion.39
  644.2 139.5 %all-reduce.16.cloned.1.call-done = f32[256,256]{0,1:T(8,128)} async-done(((f32[256,256]{0,1:T(8,128)}), f32[256,256]{0,1:T(8,128)}) %all-reduce.16.cloned.1.call-update) | async-done | bytes 262160 | tf_op jit(solution)/shard_map/psum | solution.py:59
  784.9 11.7 %cholesky.164 = f32[128,128]{1,0:T(8,128)S(1)} custom-call(f32[128,128]{1,0:T(8,128)S(1)} %cholesky.197), custom_call_target="Cholesky" | custom-call | tf_op jit(solution)/shard_map/jit(cholesky)/cholesky | solution.py:45
  797.3 9.8 custom-call.15
  807.6 11.7 %cholesky.181 = f32[128,128]{1,0:T(8,128)S(1)} custom-call(f32[128,128]{1,0:T(8,128)S(1)} %convolution_subtract_fusion.2), custom_call_target="Cholesky" | custom-call | tf_op jit(solution)/shard_map/jit(cholesky)/cholesky | solution.py:45
  821.4 4.3 while.5
  825.6 19.7 %custom-call.16 = f32[2,128,128]{1,2,0:T(8,128)S(1)} custom-call(f32[2,128,128]{2,1,0:T(8,128)S(1)} %get-tuple-element.20), custom_call_target="InvertDiagBlocksLowerTriangular" | custom-call | tf_op jit(solution)/shard_map/triangular_solve/custom-call.0 | solution.py:46
  846.3 2.5 fusion.12
  848.9 134.8 %all-reduce.18.cloned.1.call-done = f32[896,256]{1,0:T(8,128)} async-done(((f32[896,256]{1,0:T(8,128)}), f32[896,256]{1,0:T(8,128)}) %all-reduce.18.cloned.1.call-update) | async-done | bytes 917520 | tf_op jit(solution)/shard_map/psum | solution.py:61
  985.1 24.3 %psum.63 = f32[256]{0:T(256)S(1)} all-reduce(f32[256]{0:T(256)S(1)} %multiply_reduce_fusion), channel_id=1, replica_groups=mesh['mp'=32,'dp'=16] {'dp'}, use_global_device_ids=true, to_apply=%region_13.16 | all-reduce | flops 256 | bytes 2048 | tf_op jit(solution)/shard_map/psum | solution.py:63
  1010.4 2.6 fusion.2
  1013.0 2.7 fusion
  (84 shorter events, 25.2 us)
Async XLA Ops:
  7.2 1.2 copy-start
  7.2 135.9 %all-reduce.8.cloned.1.call-start = ((), (), s32[]{:S(2)}) async-start(), calls=%async_computation | async-start | bytes 524288 | tf_op jit(solution)/shard_map/psum | solution.py:58
  11.4 274.0 %all-reduce.10.cloned.1.call-start = ((), (), s32[]{:S(2)}) async-start(), calls=%async_computation.1 | async-start | bytes 524288 | tf_op jit(solution)/shard_map/psum | solution.py:59
  145.5 339.3 %all-reduce.12.cloned.1.call-start = ((), (), s32[]{:S(2)}) async-start(), calls=%async_computation.2 | async-start | bytes 1835008 | tf_op jit(solution)/shard_map/psum | solution.py:61
  285.4 1.2 copy-start.7
  322.4 24.0 %copy-start.5 = (f32[256,256]{1,0:T(8,128)S(1)}, f32[256,256]{1,0:T(8,128)}, u32[]{:S(2)}) copy-start(f32[256,256]{1,0:T(8,128)} %all-reduce.8.cloned.1.call-done) | copy-start | bytes 786436
  322.5 24.9 %copy-start.3 = (bf16[256,896]{1,0:T(8,128)(2,1)S(1)}, bf16[256,896]{1,0:T(8,128)(2,1)}, u32[]{:S(2)}) copy-start(bf16[256,896]{1,0:T(8,128)(2,1)} %param.8) | copy-start | bytes 1376260
  322.6 24.9 %copy-start.1 = (f32[256,896]{1,0:T(8,128)S(1)}, f32[256,896]{1,0:T(8,128)}, u32[]{:S(2)}) copy-start(f32[256,896]{1,0:T(8,128)} %param.7) | copy-start | bytes 2752516
  350.0 291.5 %all-reduce.14.cloned.1.call-start = ((), (), s32[]{:S(2)}) async-start(), calls=%async_computation.3 | async-start | bytes 524288 | tf_op jit(solution)/shard_map/psum | solution.py:58
  484.8 25.7 %copy-start.9 = (f32[896,256]{1,0:T(8,128)S(1)}, f32[896,256]{1,0:T(8,128)}, u32[]{:S(2)}) copy-start(f32[896,256]{1,0:T(8,128)} %all-reduce.12.cloned.1.call-done) | copy-start | bytes 2752516
  512.3 271.3 %all-reduce.16.cloned.1.call-start = ((), (), s32[]{:S(2)}) async-start(), calls=%async_computation.4 | async-start | bytes 524288 | tf_op jit(solution)/shard_map/psum | solution.py:59
  643.9 339.8 %all-reduce.18.cloned.1.call-start = ((), (), s32[]{:S(2)}) async-start(), calls=%async_computation.5 | async-start | bytes 1835008 | tf_op jit(solution)/shard_map/psum | solution.py:61
  783.7 1.2 copy-start.8
  821.3 24.0 %copy-start.6 = (f32[256,256]{1,0:T(8,128)S(1)}, f32[256,256]{1,0:T(8,128)}, u32[]{:S(2)}) copy-start(f32[256,256]{1,0:T(8,128)} %all-reduce.14.cloned.1.call-done) | copy-start | bytes 786436
  983.7 25.7 %copy-start.2 = (f32[896,256]{1,0:T(8,128)S(1)}, f32[896,256]{1,0:T(8,128)}, u32[]{:S(2)}) copy-start(f32[896,256]{1,0:T(8,128)} %all-reduce.18.cloned.1.call-done) | copy-start | bytes 2752516
  1009.4 1.0 copy-start.10
  1010.4 2.6 copy-start.4
Sparse Core Ops, SparseCore 0:
  11.5 131.5 all-reduce.7
  147.2 138.0 all-reduce.9
  350.1 134.5 all-reduce.11
  512.4 129.0 all-reduce.13
  645.5 138.0 all-reduce.15
  849.0 134.5 all-reduce.17
where the time goes:
time: 1040 us; the launch traced here: 1020 us
  waiting for transfers between devices  810 us (78%)
  other arithmetic  111 us (11%)
  blocking collectives  48.7 us (5%)
  matrix products  22.8 us (2%)
  between operations  17.4 us (2%)
  local copies, waits for them, and re-layouts  12.4 us (1%)
    psum x2, waiting for transfers between devices, body(): gram = lax.psum(inner_rows(left, left), 'mp')  279 us
    psum x2, waiting for transfers between devices, body(): right = lax.psum(inner_rows(buffer, left), 'mp')  269 us
    psum x2, waiting for transfers between devices, body(): left = lax.psum(product(buffer, basis), 'dp')  261 us
    another operation x13, other arithmetic, orthonormal(): factor = jnp.linalg.cholesky(gram)  68.6 us
    psum x2, blocking collectives, body(): squares = lax.psum(own_squares, 'dp')  48.7 us
    another operation x5, other arithmetic, orthonormal(): lax.linalg.triangular_solve(factor, left_part, left_side=False, lower=Tru...  39.4 us
  transfers between devices with their start and end apart: 6, of which 6 were waited for; matrix products, arithmetic and copies ran while one was open for 0% of the time, Pallas kernels for 0%

commit v1 on v0

v1 whole, which is shorter than its diff:
```python
import math

import jax
import jax.numpy as jnp
from jax import lax
from jax.sharding import PartitionSpec as P

ROWS = 8192
COLS = 14336
RANK = 256
ITERS = 2

highest = lax.Precision.HIGHEST
retain = 0.95
step_size = 0.5
norm_eps = 1e-06

MP = 32
DP = 16
HALF = RANK // 2
SAME_CORE = [[c + 2 * i for i in range(MP // 2)] for c in range(2)]
CORE_PAIRS = [(i, i ^ 1) for i in range(MP)]


def product(first, second):
    return jnp.dot(first, second, precision=highest, preferred_element_type=jnp.float32)


def inner_rows(first, second):
    return lax.dot_general(
        first,
        second,
        (((0,), (0,)), ((), ())),
        precision=highest,
        preferred_element_type=jnp.float32,
    )


def outer_rows(first, second):
    return lax.dot_general(
        first,
        second,
        (((1,), (1,)), ((), ())),
        precision=highest,
        preferred_element_type=jnp.float32,
    )


def scatter_sum(values, axis, count, groups=None):
    rows, columns = values.shape
    parts = lax.all_to_all(values, axis, 0, 0, axis_index_groups=groups, tiled=True)
    return jnp.sum(parts.reshape(count, rows // count, columns), axis=0)


def gather(values, axis, count, groups=None):
    rows, columns = values.shape
    copies = jnp.broadcast_to(values[None], (count, rows, columns))
    return lax.all_to_all(
        copies.reshape(count * rows, columns), axis, 0, 0, axis_index_groups=groups, tiled=True
    )


def sum_over_mp(values):
    core = lax.axis_index("mp") % 2
    first, second = values[:, :HALF], values[:, HALF:]
    own = jnp.where(core == 0, first, second)
    other = jnp.where(core == 0, second, first)
    own = own + lax.ppermute(other, "mp", CORE_PAIRS)
    own = scatter_sum(own, "mp", MP // 2, SAME_CORE)
    own = gather(own, "mp", MP // 2, SAME_CORE)
    other = lax.ppermute(own, "mp", CORE_PAIRS)
    return jnp.concatenate(
        [jnp.where(core == 0, own, other), jnp.where(core == 0, other, own)], axis=1
    )


def scaled_inverse_factor(gram):
    scale = lax.rsqrt(jnp.diagonal(gram))
    factor = jnp.linalg.cholesky(gram * scale[:, None] * scale[None, :])
    inverse = lax.linalg.triangular_solve(
        factor, jnp.eye(RANK, dtype=jnp.float32), left_side=True, lower=True
    )
    return scale, inverse


def body(momentum, gradient, weight, right_basis):
    buffer = momentum + gradient.astype(jnp.float32)
    share = buffer.shape[1]
    own_rows = buffer.shape[0] // DP

    left = scatter_sum(product(buffer, right_basis), "dp", DP)
    left = gather(left, "dp", DP)
    sums = sum_over_mp(jnp.concatenate([inner_rows(buffer, left), inner_rows(left, left)], axis=0))
    scale, inverse = scaled_inverse_factor(sums[share:])
    raw = sums[:share] * scale[None, :]
    left = scatter_sum(product(buffer, raw), "dp", DP)
    right = outer_rows(raw, inverse)
    own_squares = jnp.sum(right * right, axis=0, keepdims=True)
    sent = jnp.concatenate([left, jnp.broadcast_to(own_squares, (8, RANK))], axis=0)
    came = gather(sent, "dp", DP).reshape(DP, own_rows + 8, RANK)
    left = came[:, :own_rows].reshape(DP * own_rows, RANK)
    squares = jnp.sum(came[:, own_rows], axis=0)

    left = outer_rows(left, inverse) / (jnp.sqrt(squares) + norm_eps)[None, :]
    sums = sum_over_mp(jnp.concatenate([inner_rows(buffer, left), inner_rows(left, left)], axis=0))
    scale, inverse = scaled_inverse_factor(sums[share:])
    right = outer_rows(sums[:share] * scale[None, :], inverse)
    left = outer_rows(left * scale[None, :], inverse)
    own_squares = jnp.sum(right * right, axis=0, keepdims=True)
    squares = jnp.sum(gather(own_squares, "dp", DP), axis=0)
    new_momentum = buffer - (1.0 - retain) * outer_rows(left, right)
    basis = right / (jnp.sqrt(squares) + norm_eps)[None, :]
    update = outer_rows(left, basis)
    step = step_size * math.sqrt(ROWS * COLS / RANK)
    new_weight = (weight.astype(jnp.float32) - step * update).astype(jnp.bfloat16)
    return (new_weight, new_momentum, basis)


def solution(mesh):
    in_specs = (P("mp", "dp"), P("mp", "dp"), P("mp", "dp"), P("dp", None))
    out_specs = (P("mp", "dp"), P("mp", "dp"), P("dp", None))
    return jax.shard_map(body, mesh=mesh, in_specs=in_specs, out_specs=out_specs, check_vma=False)
```

time: 1040 us -> 379 us (0.36)
  waiting for transfers between devices: 810 us -> 40.5 us
  starting transfers between devices: 0.46 us -> 64.1 us
  blocking collectives: 48.7 us -> 90.8 us
  local copies, waits for them, and re-layouts: 12.4 us -> 28.3 us
  between operations: 17.4 us -> 4.03 us
    psum x6 -> x0, waiting for transfers between devices: 810 us -> none  [the longest x2 279 us: body(): gram = lax.psum(inner_rows(left, left), 'mp')]
    all_to_all x0 -> x5, blocking collectives: none -> 90.8 us  [the longest x3 57.6 us: gather(): lax.all_to_all(copies.reshape(count * rows, columns), axis, 0, 0, axis_in...]
    psum x2 -> x0, blocking collectives: 48.7 us -> none  [body(): squares = lax.psum(own_squares, 'dp')]
    all_to_all x0 -> x4, starting transfers between devices: none -> 38.9 us  [the longest x2 21.9 us: scatter_sum(): lax.all_to_all(values, axis, 0, 0, axis_index_groups=groups, tiled=True)]
    all_to_all x0 -> x4, waiting for transfers between devices: none -> 34.6 us  [the longest x2 21.5 us: gather(): lax.all_to_all(copies.reshape(count * rows, columns), axis, 0, 0, axis_in...]
    ppermute x0 -> x4, starting transfers between devices: none -> 25.2 us  [the longest x2 16.4 us: sum_over_mp(): own = own + lax.ppermute(other, 'mp', CORE_PAIRS)]
  transfers between devices with their start and end apart: 6 -> 8, of which waited for: 6 -> 7; matrix products, arithmetic and copies ran while one was open for 0% -> 20% of each run, Pallas kernels for 0% -> 0%
where the time goes in v1:
time: 379 us; the launch traced here: 372 us
  other arithmetic  115 us (30%)
  blocking collectives  90.8 us (24%)
  starting transfers between devices  64.1 us (17%)
  waiting for transfers between devices  40.5 us (11%)
  matrix products  29.2 us (8%)
  local copies, waits for them, and re-layouts  28.3 us (7%)
  between operations  4.03 us (1%)
    another operation x13, other arithmetic, scaled_inverse_factor(): factor = jnp.linalg.cholesky(gram * scale[:, None] * scale[None, :])  68.7 us
    all_to_all x3, blocking collectives, gather(): lax.all_to_all(copies.reshape(count * rows, columns), axis, 0, 0, axis_in...  57.6 us
    another operation x5, other arithmetic, scaled_inverse_factor(): lax.linalg.triangular_solve(factor, jnp.eye(RANK, dtype=jnp.float32), lef...  41.9 us
    all_to_all x2, blocking collectives, scatter_sum(): lax.all_to_all(values, axis, 0, 0, axis_index_groups=groups, tiled=True)  33.2 us
    all_to_all x2, starting transfers between devices, scatter_sum(): lax.all_to_all(values, axis, 0, 0, axis_index_groups=groups, tiled=True)  21.9 us
    all_to_all x2, waiting for transfers between devices, gather(): lax.all_to_all(copies.reshape(count * rows, columns), axis, 0, 0, axis_in...  21.5 us
    all_to_all x2, starting transfers between devices, gather(): lax.all_to_all(copies.reshape(count * rows, columns), axis, 0, 0, axis_in...  17 us
    ppermute x2, starting transfers between devices, sum_over_mp(): own = own + lax.ppermute(other, 'mp', CORE_PAIRS)  16.4 us
  transfers between devices with their start and end apart: 8, of which 7 were waited for; matrix products, arithmetic and copies ran while one was open for 20% of the time, Pallas kernels for 0%

profile of v1, /device:TPU:1, one launch (start us, length us, event | category | flops | bytes accessed | tf_op | source)
XLA Modules:
  0.0 372.1 jit_solution(13258852741634421613)
XLA Ops:
  4.9 15.9 %all-to-all-start = ((f32[16,16,256]{2,1,0:T(8,128)}), f32[16,16,256]{2,1,0:T(8,128)S(1)}, u32[]{:S(2)}, u32[]{:S(2)}) async-start(f32[16,16,256]{2,1,0:T(8,128)} %bitcast), calls=%async_computation | async-start | bytes 524288 | tf_op jit(solution)/shard_map/all_to_all | solution.py:51
  20.7 13.1 %all-to-all-done = f32[16,16,256]{2,1,0:T(8,128)S(1)} async-done(((f32[16,16,256]{2,1,0:T(8,128)}), f32[16,16,256]{2,1,0:T(8,128)S(1)}, u32[]{:S(2)}, u32[]{:S(2)}) %all-to-all-start) | async-done | bytes 262176 | tf_op jit(solution)/shard_map/all_to_all | solution.py:51
  34.6 10.9 %all-to-all-start.1 = ((f32[16,16,256]{2,1,0:T(8,128)}), f32[16,16,256]{2,1,0:T(8,128)S(1)}, u32[]{:S(2)}, u32[]{:S(2)}) async-start(f32[16,16,256]{2,1,0:T(8,128)} %broadcast_in_dim.17), calls=%async_computation.1 | async-start | bytes 524288 | tf_op jit(solution)/shard_map/all_to_all | solution.py:58
  45.6 13.1 %all-to-all-done.1 = f32[16,16,256]{2,1,0:T(8,128)S(1)} async-done(((f32[16,16,256]{2,1,0:T(8,128)}), f32[16,16,256]{2,1,0:T(8,128)S(1)}, u32[]{:S(2)}, u32[]{:S(2)}) %all-to-all-start.1) | async-done | bytes 262176 | tf_op jit(solution)/shard_map/all_to_all | solution.py:58
  60.5 8.3 %collective-permute-start = (f32[1152,128]{0,1:T(8,128)S(1)}, f32[1152,128]{0,1:T(8,128)S(1)}, u32[]{:S(2)}, u32[]{:S(2)}) collective-permute-start(f32[1152,128]{0,1:T(8,128)S(1)} %broadcast_select_fusion.5), channel_id=1, source_target_pairs={{0,16},{16,0},{32,48},{48,32},{64,80},{80,64},{96,112},{112,96},{1... | collective-permute-start | bytes 1769480 | tf_op jit(solution)/shard_map/ppermute | solution.py:68
  70.7 18.0 %all_to_all.78 = f32[16,72,128]{2,1,0:T(8,128)S(1)} all-to-all(f32[16,72,128]{2,1,0:T(8,128)S(1)} %bitcast.88), channel_id=1, replica_groups={{0,32,64,96,128,160,192,224,256,288,320,352,384,416,448,480},{16,48,80,..., dimensions={0} | all-to-all | bytes 1179648 | tf_op jit(solution)/shard_map/all_to_all | solution.py:51
  88.7 13.8 %all_to_all.75 = f32[16,72,128]{2,1,0:T(8,128)S(1)} all-to-all(f32[16,72,128]{2,1,0:T(8,128)S(1)} %broadcast_in_dim.18), channel_id=1, replica_groups={{0,32,64,96,128,160,192,224,256,288,320,352,384,416,448,480},{16,48,80,..., dimensions={0} | all-to-all | bytes 1179648 | tf_op jit(solution)/shard_map/all_to_all | solution.py:58
  102.7 4.6 %collective-permute-start.1 = (f32[1152,128]{0,1:T(8,128)S(1)}, f32[1152,128]{0,1:T(8,128)}, u32[]{:S(2)}, u32[]{:S(2)}) collective-permute-start(f32[1152,128]{0,1:T(8,128)S(1)} %copy.64), channel_id=1, source_target_pairs={{0,16},{16,0},{32,48},{48,32},{64,80},{80,64},{96,112},{112,96},{1... | collective-permute-start | bytes 1769480 | tf_op jit(solution)/shard_map/ppermute | solution.py:71
  117.1 6.0 %all-to-all-start.4 = ((f32[16,16,256]{2,1,0:T(8,128)}), f32[16,16,256]{2,1,0:T(8,128)}, u32[]{:S(2)}, u32[]{:S(2)}) async-start(f32[16,16,256]{2,1,0:T(8,128)} %bitcast.6), calls=%async_computation.4 | async-start | bytes 524288 | tf_op jit(solution)/shard_map/all_to_all | solution.py:51
  125.1 11.7 %cholesky.130 = f32[128,128]{1,0:T(8,128)S(1)} custom-call(f32[128,128]{1,0:T(8,128)S(1)} %cholesky.194), custom_call_target="Cholesky" | custom-call | tf_op jit(solution)/shard_map/jit(cholesky)/cholesky | solution.py:79
  136.8 9.8 %custom-call.17 = f32[1,128,128]{1,2,0:T(8,128)S(1)} custom-call(f32[1,128,128]{2,1,0:T(8,128)S(1)} %get-tuple-element.52), custom_call_target="InvertDiagBlocksLowerTriangular" | custom-call | tf_op jit(solution)/shard_map/jit(cholesky)/cholesky | solution.py:79
  148.8 11.7 %cholesky.147 = f32[128,128]{1,0:T(8,128)S(1)} custom-call(f32[128,128]{1,0:T(8,128)S(1)} %convolution_subtract_fusion.3), custom_call_target="Cholesky" | custom-call | tf_op jit(solution)/shard_map/jit(cholesky)/cholesky | solution.py:79
  164.0 7.0 %while.4 = (s32[]{:T(128)}, f32[256,256]{1,0:T(8,128)}, s32[2,2]{1,0:T(2,128)S(1)}, f32[2,128,128]{2,1,0:T(8,128)}, s32[]{:T(128)}) while((s32[]{:T(128)}, f32[256,256]{1,0:T(8,128)}, s32[2,2]{1,0:T(2,128)S(1)}, f32[2,128,128]{2,1,0:T(8,128)}, s32[]{:T(128)}) %tuple.50), condition=%wide.while_cond, body=%wide.while_body.sunk | while | flops 2 | bytes 132705 | solution.py:80
  171.0 21.2 %custom-call.18 = f32[2,128,128]{1,2,0:T(8,128)} custom-call(f32[2,128,128]{2,1,0:T(8,128)} %get-tuple-element.19), custom_call_target="InvertDiagBlocksLowerTriangular" | custom-call | tf_op jit(solution)/shard_map/triangular_solve/custom-call.0 | solution.py:80
  199.4 29.6 %all_to_all.76 = f32[16,24,256]{2,1,0:T(8,128)S(1)} all-to-all(f32[16,24,256]{2,1,0:T(8,128)S(1)} %broadcast_in_dim.20), channel_id=1, replica_groups=mesh['mp'=32,'dp'=16] {'dp'}, dimensions={0} | all-to-all | bytes 786432 | tf_op jit(solution)/shard_map/all_to_all | solution.py:58
  231.1 8.2 %collective-permute-start.2 = (f32[1152,128]{0,1:T(8,128)S(1)}, f32[1152,128]{0,1:T(8,128)S(1)}, u32[]{:S(2)}, u32[]{:S(2)}) collective-permute-start(f32[1152,128]{0,1:T(8,128)S(1)} %broadcast_select_fusion.2), channel_id=1, source_target_pairs={{0,16},{16,0},{32,48},{48,32},{64,80},{80,64},{96,112},{112,96},{1... | collective-permute-start | bytes 1769480 | tf_op jit(solution)/shard_map/ppermute | solution.py:68
  242.0 15.2 %all_to_all.79 = f32[16,72,128]{2,1,0:T(8,128)S(1)} all-to-all(f32[16,72,128]{2,1,0:T(8,128)} %bitcast.90), channel_id=1, replica_groups={{0,32,64,96,128,160,192,224,256,288,320,352,384,416,448,480},{16,48,80,..., dimensions={0} | all-to-all | bytes 1179648 | tf_op jit(solution)/shard_map/all_to_all | solution.py:51
  257.3 14.3 %all_to_all.77 = f32[16,72,128]{2,1,0:T(8,128)} all-to-all(f32[16,72,128]{2,1,0:T(8,128)S(1)} %broadcast_in_dim.21), channel_id=1, replica_groups={{0,32,64,96,128,160,192,224,256,288,320,352,384,416,448,480},{16,48,80,..., dimensions={0} | all-to-all | bytes 1179648 | tf_op jit(solution)/shard_map/all_to_all | solution.py:58
  283.4 11.7 %cholesky.164 = f32[128,128]{1,0:T(8,128)S(1)} custom-call(f32[128,128]{1,0:T(8,128)S(1)} %cholesky.197), custom_call_target="Cholesky" | custom-call | tf_op jit(solution)/shard_map/jit(cholesky)/cholesky | solution.py:79
  295.2 9.8 %custom-call.19 = f32[1,128,128]{1,2,0:T(8,128)S(1)} custom-call(f32[1,128,128]{2,1,0:T(8,128)S(1)} %get-tuple-element.48), custom_call_target="InvertDiagBlocksLowerTriangular" | custom-call | tf_op jit(solution)/shard_map/jit(cholesky)/cholesky | solution.py:79
  307.2 11.7 %cholesky.181 = f32[128,128]{1,0:T(8,128)S(1)} custom-call(f32[128,128]{1,0:T(8,128)S(1)} %convolution_subtract_fusion.2), custom_call_target="Cholesky" | custom-call | tf_op jit(solution)/shard_map/jit(cholesky)/cholesky | solution.py:79
  325.7 19.9 %custom-call.20 = f32[2,128,128]{1,2,0:T(8,128)S(1)} custom-call(f32[2,128,128]{2,1,0:T(8,128)S(1)} %get-tuple-element.20), custom_call_target="InvertDiagBlocksLowerTriangular" | custom-call | tf_op jit(solution)/shard_map/triangular_solve/custom-call.0 | solution.py:80
  351.4 6.1 %all-to-all-start.8 = ((f32[16,1,256]{2,1,0:T(1,128)}), f32[16,1,256]{2,1,0:T(1,128)S(1)}, u32[]{:S(2)}, u32[]{:S(2)}) async-start(f32[16,1,256]{2,1,0:T(1,128)} %reshape.97), calls=%async_computation.8 | async-start | bytes 32768 | tf_op jit(solution)/shard_map/all_to_all | solution.py:58
  360.5 8.4 %all-to-all-done.8 = f32[16,1,256]{2,1,0:T(1,128)S(1)} async-done(((f32[16,1,256]{2,1,0:T(1,128)}), f32[16,1,256]{2,1,0:T(1,128)S(1)}, u32[]{:S(2)}, u32[]{:S(2)}) %all-to-all-start.8) | async-done | bytes 16416 | tf_op jit(solution)/shard_map/all_to_all | solution.py:58
  (133 shorter events, 79.0 us)
Async XLA Ops:
  0.6 1.2 copy-start
  4.9 53.8 %copy-start.1 = (f32[256,896]{1,0:T(8,128)S(1)}, f32[256,896]{1,0:T(8,128)}, u32[]{:S(2)}) copy-start(f32[256,896]{1,0:T(8,128)} %param.7) | copy-start | bytes 2752516
  4.9 53.8 %copy-start.2 = (bf16[256,896]{1,0:T(8,128)(2,1)S(1)}, bf16[256,896]{1,0:T(8,128)(2,1)}, u32[]{:S(2)}) copy-start(bf16[256,896]{1,0:T(8,128)(2,1)} %param.8) | copy-start | bytes 1376260
  4.9 29.0 %all-to-all-start = ((f32[16,16,256]{2,1,0:T(8,128)}), f32[16,16,256]{2,1,0:T(8,128)S(1)}, u32[]{:S(2)}, u32[]{:S(2)}) async-start(f32[16,16,256]{2,1,0:T(8,128)} %bitcast), calls=%async_computation | async-start | bytes 524288 | tf_op jit(solution)/shard_map/all_to_all | solution.py:51
  34.6 24.0 %all-to-all-start.1 = ((f32[16,16,256]{2,1,0:T(8,128)}), f32[16,16,256]{2,1,0:T(8,128)S(1)}, u32[]{:S(2)}, u32[]{:S(2)}) async-start(f32[16,16,256]{2,1,0:T(8,128)} %broadcast_in_dim.17), calls=%async_computation.1 | async-start | bytes 524288 | tf_op jit(solution)/shard_map/all_to_all | solution.py:58
  60.5 9.9 %collective-permute-start = (f32[1152,128]{0,1:T(8,128)S(1)}, f32[1152,128]{0,1:T(8,128)S(1)}, u32[]{:S(2)}, u32[]{:S(2)}) collective-permute-start(f32[1152,128]{0,1:T(8,128)S(1)} %broadcast_select_fusion.5), channel_id=1, source_target_pairs={{0,16},{16,0},{32,48},{48,32},{64,80},{80,64},{96,112},{112,96},{1... | collective-permute-start | bytes 1769480 | tf_op jit(solution)/shard_map/ppermute | solution.py:68
  102.7 6.4 %collective-permute-start.1 = (f32[1152,128]{0,1:T(8,128)S(1)}, f32[1152,128]{0,1:T(8,128)}, u32[]{:S(2)}, u32[]{:S(2)}) collective-permute-start(f32[1152,128]{0,1:T(8,128)S(1)} %copy.64), channel_id=1, source_target_pairs={{0,16},{16,0},{32,48},{48,32},{64,80},{80,64},{96,112},{112,96},{1... | collective-permute-start | bytes 1769480 | tf_op jit(solution)/shard_map/ppermute | solution.py:71
  110.2 0.8 copy-start.3
  117.1 81.2 %all-to-all-start.4 = ((f32[16,16,256]{2,1,0:T(8,128)}), f32[16,16,256]{2,1,0:T(8,128)}, u32[]{:S(2)}, u32[]{:S(2)}) async-start(f32[16,16,256]{2,1,0:T(8,128)} %bitcast.6), calls=%async_computation.4 | async-start | bytes 524288 | tf_op jit(solution)/shard_map/all_to_all | solution.py:51
  124.3 0.7 copy-start.10
  164.0 32.6 %copy-start.4 = (f32[1152,128]{0,1:T(8,128)S(1)}, f32[1152,128]{0,1:T(8,128)}, u32[]{:S(2)}) copy-start(f32[1152,128]{0,1:T(8,128)} %copy-done.3) | copy-start | bytes 1769476
  193.5 2.4 copy-start.12
  199.3 29.7 %copy-start.13 = (f32[128,256]{1,0:T(8,128)S(1)}, f32[128,256]{1,0:T(8,128)}, u32[]{:S(2)}) copy-start(f32[128,256]{1,0:T(8,128)} %copy-done.12) | copy-start | bytes 393220
  199.3 29.7 %copy-start.16 = (f32[128,256]{1,0:T(8,128)S(1)}, f32[128,256]{1,0:T(8,128)}, u32[]{:S(2)}) copy-start(f32[128,256]{1,0:T(8,128)} %copy-done.15) | copy-start | bytes 393220
  231.1 9.8 %collective-permute-start.2 = (f32[1152,128]{0,1:T(8,128)S(1)}, f32[1152,128]{0,1:T(8,128)S(1)}, u32[]{:S(2)}, u32[]{:S(2)}) collective-permute-start(f32[1152,128]{0,1:T(8,128)S(1)} %broadcast_select_fusion.2), channel_id=1, source_target_pairs={{0,16},{16,0},{32,48},{48,32},{64,80},{80,64},{96,112},{112,96},{1... | collective-permute-start | bytes 1769480 | tf_op jit(solution)/shard_map/ppermute | solution.py:68
  272.9 5.7 %collective-permute-start.3 = (f32[1152,128]{0,1:T(8,128)S(1)}, f32[1152,128]{0,1:T(8,128)S(1)}, u32[]{:S(2)}, u32[]{:S(2)}) collective-permute-start(f32[1152,128]{0,1:T(8,128)S(1)} %copy.73), channel_id=1, source_target_pairs={{0,16},{16,0},{32,48},{48,32},{64,80},{80,64},{96,112},{112,96},{1... | collective-permute-start | bytes 1769480 | tf_op jit(solution)/shard_map/ppermute | solution.py:71
  278.7 0.8 copy-start.5
  278.7 1.0 copy-start.6
  282.7 0.7 copy-start.11
  306.0 39.6 %copy-start.8 = (f32[256,256]{1,0:T(8,128)S(1)}, f32[256,256]{1,0:T(8,128)}, u32[]{:S(2)}) copy-start(f32[256,256]{1,0:T(8,128)} %fusion.17) | copy-start | bytes 786436
  351.4 17.5 %all-to-all-start.8 = ((f32[16,1,256]{2,1,0:T(1,128)}), f32[16,1,256]{2,1,0:T(1,128)S(1)}, u32[]{:S(2)}, u32[]{:S(2)}) async-start(f32[16,1,256]{2,1,0:T(1,128)} %reshape.97), calls=%async_computation.8 | async-start | bytes 32768 | tf_op jit(solution)/shard_map/all_to_all | solution.py:58
  368.9 1.0 copy-start.9
  369.0 1.1 copy-start.14
  370.1 1.8 copy-start.7
  (1 other events, 0.7 us)

commit v2 on v1

--- a/solution.py
+++ b/solution.py
@@ -1,8 +1,11 @@
+import functools
 import math
 
 import jax
 import jax.numpy as jnp
 from jax import lax
+from jax.experimental import pallas as pl
+from jax.experimental.pallas import tpu as pltpu
 from jax.sharding import PartitionSpec as P
 
 ROWS = 8192
@@ -18,6 +21,7 @@
 MP = 32
 DP = 16
 HALF = RANK // 2
+PANEL = 16
 SAME_CORE = [[c + 2 * i for i in range(MP // 2)] for c in range(2)]
 CORE_PAIRS = [(i, i ^ 1) for i in range(MP)]
 
@@ -74,13 +78,61 @@
     )
 
 
-def scaled_inverse_factor(gram):
-    scale = lax.rsqrt(jnp.diagonal(gram))
-    factor = jnp.linalg.cholesky(gram * scale[:, None] * scale[None, :])
-    inverse = lax.linalg.triangular_solve(
-        factor, jnp.eye(RANK, dtype=jnp.float32), left_side=True, lower=True
-    )
-    return scale, inverse
+def inverse_factor_kernel(gram_ref, out_ref, *, unscale):
+    gram = gram_ref[...]
+    row = lax.broadcasted_iota(jnp.int32, (RANK, RANK), 0)
+    column = lax.broadcasted_iota(jnp.int32, (RANK, RANK), 1)
+    diagonal = jnp.where(row == column, gram, 0.0)
+    scale_row = lax.rsqrt(jnp.sum(diagonal, axis=0, keepdims=True))
+    scale_column = lax.rsqrt(jnp.sum(diagonal, axis=1, keepdims=True))
+    rest = gram * scale_column * scale_row
+    lane = lax.broadcasted_iota(jnp.int32, (PANEL, RANK), 1)
+    place = lax.broadcasted_iota(jnp.int32, (PANEL, RANK), 0)
+    short = place[:, :HALF]
+    panel, rest = rest[:PANEL], rest[PANEL:]
+    for start in range(0, RANK, PANEL):
+        own = [
+            jnp.broadcast_to(panel[:, start + t : start + t + 1], (PANEL, HALF))
+            for t in range(PANEL)
+        ]
+        inside = (lane >= start) & (lane < start + PANEL)
+        panel = jnp.where(inside, jnp.where(lane - start == place, 1.0, 0.0), panel)
+        pivots = own[0]
+        for t in range(PANEL):
+            if t > 0:
+                pivots = jnp.where(short == t, own[t], pivots)
+            if t < PANEL - 1:
+                factor = jnp.where(short > t, own[t] * (1.0 / own[t][t : t + 1]), 0.0)
+                for later in range(t + 1, PANEL):
+                    own[later] = own[later] - factor * own[later][t : t + 1]
+                panel = panel - jnp.concatenate([factor, factor], axis=1) * panel[t : t + 1]
+        root = lax.rsqrt(pivots)
+        done = panel * jnp.concatenate([root, root], axis=1)
+        result = jnp.where(lane < start + PANEL, done, 0.0)
+        out_ref[start : start + PANEL, :] = result * scale_row if unscale else result
+        if start + PANEL < RANK:
+            turned = done.T
+            kept = jnp.where(inside, 0.0, 1.0)[:1]
+            panel = rest[:PANEL] * kept - product(turned[start + PANEL : start + 2 * PANEL], done)
+            if start + 2 * PANEL < RANK:
+                rest = rest[PANEL:] * kept - product(turned[start + 2 * PANEL :], done)
+
+
+def inverse_factor(gram, unscale):
+    return pl.pallas_call(
+        functools.partial(inverse_factor_kernel, unscale=unscale),
+        out_shape=jax.ShapeDtypeStruct((RANK, RANK), jnp.float32),
+        cost_estimate=pl.CostEstimate(
+            flops=RANK**3 * 12, bytes_accessed=2 * 4 * RANK**2, transcendentals=2 * RANK
+        ),
+        compiler_params=pltpu.CompilerParams(vmem_limit_bytes=16 * 2**20),
+    )(gram)
+
+
+def diagonal_scale(gram):
+    row = lax.broadcasted_iota(jnp.int32, (RANK, RANK), 0)
+    column = lax.broadcasted_iota(jnp.int32, (RANK, RANK), 1)
+    return lax.rsqrt(jnp.sum(jnp.where(row == column, gram, 0.0), axis=0))
 
 
 def body(momentum, gradient, weight, right_basis):
@@ -91,8 +143,9 @@
     left = scatter_sum(product(buffer, right_basis), "dp", DP)
     left = gather(left, "dp", DP)
     sums = sum_over_mp(jnp.concatenate([inner_rows(buffer, left), inner_rows(left, left)], axis=0))
-    scale, inverse = scaled_inverse_factor(sums[share:])
-    raw = sums[:share] * scale[None, :]
+    gram = sums[share:]
+    raw = sums[:share] * diagonal_scale(gram)[None, :]
+    inverse = inverse_factor(gram, False)
     left = scatter_sum(product(buffer, raw), "dp", DP)
     right = outer_rows(raw, inverse)
     own_squares = jnp.sum(right * right, axis=0, keepdims=True)
@@ -103,9 +156,9 @@
 
     left = outer_rows(left, inverse) / (jnp.sqrt(squares) + norm_eps)[None, :]
     sums = sum_over_mp(jnp.concatenate([inner_rows(buffer, left), inner_rows(left, left)], axis=0))
-    scale, inverse = scaled_inverse_factor(sums[share:])
-    right = outer_rows(sums[:share] * scale[None, :], inverse)
-    left = outer_rows(left * scale[None, :], inverse)
+    inverse = inverse_factor(sums[share:], True)
+    right = outer_rows(sums[:share], inverse)
+    left = outer_rows(left, inverse)
     own_squares = jnp.sum(right * right, axis=0, keepdims=True)
     squares = jnp.sum(gather(own_squares, "dp", DP), axis=0)
     new_momentum = buffer - (1.0 - retain) * outer_rows(left, right)

time: 379 us -> 239 us (0.63); the launches traced: 372 us -> 238 us
  other arithmetic: 115 us -> 1.73 us
  blocking collectives: 90.8 us -> 116 us
  local copies, waits for them, and re-layouts: 28.3 us -> 3.7 us
  Pallas kernels: 0 us -> 18.1 us
  starting transfers between devices: 64.1 us -> 48.6 us
  matrix products: 29.2 us -> 17.7 us
  waiting for transfers between devices: 40.5 us -> 30.7 us
    another operation x18 -> x0, other arithmetic: 111 us -> none  [the longest x13 68.7 us: scaled_inverse_factor(): factor = jnp.linalg.cholesky(gram * scale[:, None] * scale[None, :])]
    all_to_all x2 -> x3, blocking collectives: 33.2 us -> 61.1 us  [scatter_sum(): lax.all_to_all(values, axis, 0, 0, axis_index_groups=groups, tiled=True)]
    pallas_call x0 -> x2, Pallas kernels: none -> 18.1 us  [inverse_factor(): pl.pallas_call(functools.partial(inverse_factor_kernel, unscale=unscale),...]
    all_to_all x2 -> x1, starting transfers between devices: 21.9 us -> 5.47 us  [scatter_sum(): lax.all_to_all(values, axis, 0, 0, axis_index_groups=groups, tiled=True)]
    another operation x19 -> x0, local copies, waits for them, and re-layouts: 11.8 us -> none  [the longest x15 11.7 us: scaled_inverse_factor(): lax.linalg.triangular_solve(factor, jnp.eye(RANK, dtype=jnp.float32), lef...]
    all_to_all x2 -> x1, waiting for transfers between devices: 13.1 us -> 3.04 us  [scatter_sum(): lax.all_to_all(values, axis, 0, 0, axis_index_groups=groups, tiled=True)]
    another operation x10 -> x0, matrix products: 8.87 us -> none  [the longest x6 4.52 us: scaled_inverse_factor(): lax.linalg.triangular_solve(factor, jnp.eye(RANK, dtype=jnp.float32), lef...]
    gather x2 -> x0, local copies, waits for them, and re-layouts: 4.95 us -> none  [scaled_inverse_factor(): scale = lax.rsqrt(jnp.diagonal(gram))]
  transfers between devices with their start and end apart: 8 -> 7, of which waited for: 7 -> 7; matrix products, arithmetic and copies ran while one was open for 20% -> 2% of each run, Pallas kernels for 0% -> 4%
where the time goes in v2:
time: 239 us; the launch traced here: 238 us
  blocking collectives  116 us (49%)
  starting transfers between devices  48.6 us (20%)
  waiting for transfers between devices  30.7 us (13%)
  Pallas kernels  18.1 us (8%)
  matrix products  17.7 us (7%)
  local copies, waits for them, and re-layouts  3.7 us (2%)
    all_to_all x3, blocking collectives, scatter_sum(): lax.all_to_all(values, axis, 0, 0, axis_index_groups=groups, tiled=True)  61.1 us
    all_to_all x3, blocking collectives, gather(): lax.all_to_all(copies.reshape(count * rows, columns), axis, 0, 0, axis_in...  55.4 us
    all_to_all x2, waiting for transfers between devices, gather(): lax.all_to_all(copies.reshape(count * rows, columns), axis, 0, 0, axis_in...  21.5 us
    pallas_call x2, Pallas kernels, inverse_factor(): pl.pallas_call(functools.partial(inverse_factor_kernel, unscale=unscale),...  18.1 us
    ppermute x2, starting transfers between devices, sum_over_mp(): own = own + lax.ppermute(other, 'mp', CORE_PAIRS)  17.1 us
    all_to_all x2, starting transfers between devices, gather(): lax.all_to_all(copies.reshape(count * rows, columns), axis, 0, 0, axis_in...  16.6 us
    ppermute x2, starting transfers between devices, sum_over_mp(): other = lax.ppermute(own, 'mp', CORE_PAIRS)  9.49 us
    dot_general x6, matrix products, outer_rows(): lax.dot_general(first, second, (((1,), (1,)), ((), ())), precision=highes...  9.18 us
  transfers between devices with their start and end apart: 7, of which 7 were waited for; matrix products, arithmetic and copies ran while one was open for 2% of the time, Pallas kernels for 4%

profile of v2, /device:TPU:1, one launch (start us, length us, event | category | flops | bytes accessed | tf_op | source)
XLA Modules:
  0.0 238.0 jit_solution(10655717536955946412)
XLA Ops:
  1.8 2.3 fusion.18
  4.2 28.8 %all_to_all.75 = f32[16,16,256]{2,1,0:T(8,128)S(1)} all-to-all(f32[16,16,256]{2,1,0:T(8,128)S(1)} %bitcast.36), channel_id=1, replica_groups=mesh['mp'=32,'dp'=16] {'dp'}, dimensions={0} | all-to-all | bytes 524288 | tf_op jit(solution)/shard_map/all_to_all | solution.py:55
  33.7 10.9 %all-to-all-start.1 = ((f32[16,16,256]{2,1,0:T(8,128)}), f32[16,16,256]{2,1,0:T(8,128)S(1)}, u32[]{:S(2)}, u32[]{:S(2)}) async-start(f32[16,16,256]{2,1,0:T(8,128)} %broadcast_in_dim.14), calls=%async_computation.1 | async-start | bytes 524288 | tf_op jit(solution)/shard_map/all_to_all | solution.py:62
  44.7 13.1 %all-to-all-done.1 = f32[16,16,256]{2,1,0:T(8,128)S(1)} async-done(((f32[16,16,256]{2,1,0:T(8,128)}), f32[16,16,256]{2,1,0:T(8,128)S(1)}, u32[]{:S(2)}, u32[]{:S(2)}) %all-to-all-start.1) | async-done | bytes 262176 | tf_op jit(solution)/shard_map/all_to_all | solution.py:62
  60.1 8.3 %collective-permute-start = (f32[1152,128]{1,0:T(8,128)S(1)}, f32[1152,128]{1,0:T(8,128)S(1)}, u32[]{:S(2)}, u32[]{:S(2)}) collective-permute-start(f32[1152,128]{1,0:T(8,128)S(1)} %broadcast_select_fusion.5), channel_id=1, source_target_pairs={{0,16},{16,0},{32,48},{48,32},{64,80},{80,64},{96,112},{112,96},{1... | collective-permute-start | bytes 1769480 | tf_op jit(solution)/shard_map/ppermute | solution.py:72
  70.0 18.0 %all_to_all.76 = f32[16,72,128]{2,1,0:T(8,128)S(1)} all-to-all(f32[16,72,128]{2,1,0:T(8,128)S(1)} %bitcast.33), channel_id=1, replica_groups={{0,32,64,96,128,160,192,224,256,288,320,352,384,416,448,480},{16,48,80,..., dimensions={0} | all-to-all | bytes 1179648 | tf_op jit(solution)/shard_map/all_to_all | solution.py:55
  88.1 13.8 %all_to_all.77 = f32[16,72,128]{2,1,0:T(8,128)S(1)} all-to-all(f32[16,72,128]{2,1,0:T(8,128)S(1)} %broadcast_in_dim.15), channel_id=1, replica_groups={{0,32,64,96,128,160,192,224,256,288,320,352,384,416,448,480},{16,48,80,..., dimensions={0} | all-to-all | bytes 1179648 | tf_op jit(solution)/shard_map/all_to_all | solution.py:62
  101.8 4.6 %collective-permute-start.1 = (f32[1152,128]{1,0:T(8,128)S(1)}, f32[1152,128]{1,0:T(8,128)S(1)}, u32[]{:S(2)}, u32[]{:S(2)}) collective-permute-start(f32[1152,128]{1,0:T(8,128)S(1)} %bitcast.32), channel_id=1, source_target_pairs={{0,16},{16,0},{32,48},{48,32},{64,80},{80,64},{96,112},{112,96},{1... | collective-permute-start | bytes 1769480 | tf_op jit(solution)/shard_map/ppermute | solution.py:75
  108.2 1.8 fusion.11
  110.0 5.5 %all-to-all-start.4 = ((f32[16,16,256]{2,1,0:T(8,128)}), f32[16,16,256]{2,1,0:T(8,128)}, u32[]{:S(2)}, u32[]{:S(2)}) async-start(f32[16,16,256]{2,1,0:T(8,128)} %bitcast.5), calls=%async_computation.4 | async-start | bytes 524288 | tf_op jit(solution)/shard_map/all_to_all | solution.py:55
  115.5 9.1 %shard_map.67 = f32[256,256]{1,0:T(8,128)S(1)} custom-call(f32[256,256]{1,0:T(8,128)S(1)} %get-tuple-element.4.gram_ref), custom_call_target="tpu_custom_call" | custom-call | flops 201326592 | bytes 524288 | tf_op jit(solution)/shard_map/pallas_call | solution.py:122
  124.6 2.0 fusion.3
  126.5 3.0 %all-to-all-done.4 = f32[16,16,256]{2,1,0:T(8,128)} async-done(((f32[16,16,256]{2,1,0:T(8,128)}), f32[16,16,256]{2,1,0:T(8,128)}, u32[]{:S(2)}, u32[]{:S(2)}) %all-to-all-start.4) | async-done | bytes 262176 | tf_op jit(solution)/shard_map/all_to_all | solution.py:55
  130.6 27.9 %all_to_all.78 = f32[16,24,256]{2,1,0:T(8,128)S(1)} all-to-all(f32[16,24,256]{2,1,0:T(8,128)S(1)} %broadcast_in_dim.18), channel_id=1, replica_groups=mesh['mp'=32,'dp'=16] {'dp'}, dimensions={0} | all-to-all | bytes 786432 | tf_op jit(solution)/shard_map/all_to_all | solution.py:62
  159.6 1.6 fusion.16
  161.3 8.8 %collective-permute-start.2 = (f32[1152,128]{1,0:T(8,128)S(1)}, f32[1152,128]{1,0:T(8,128)S(1)}, u32[]{:S(2)}, u32[]{:S(2)}) collective-permute-start(f32[1152,128]{1,0:T(8,128)S(1)} %broadcast_select_fusion.2), channel_id=1, source_target_pairs={{0,16},{16,0},{32,48},{48,32},{64,80},{80,64},{96,112},{112,96},{1... | collective-permute-start | bytes 1769480 | tf_op jit(solution)/shard_map/ppermute | solution.py:72
  171.8 14.3 %all_to_all.79 = f32[16,72,128]{2,1,0:T(8,128)S(1)} all-to-all(f32[16,72,128]{2,1,0:T(8,128)S(1)} %bitcast.34), channel_id=1, replica_groups={{0,32,64,96,128,160,192,224,256,288,320,352,384,416,448,480},{16,48,80,..., dimensions={0} | all-to-all | bytes 1179648 | tf_op jit(solution)/shard_map/all_to_all | solution.py:55
  186.2 13.8 %all_to_all.80 = f32[16,72,128]{2,1,0:T(8,128)S(1)} all-to-all(f32[16,72,128]{2,1,0:T(8,128)S(1)} %broadcast_in_dim.19), channel_id=1, replica_groups={{0,32,64,96,128,160,192,224,256,288,320,352,384,416,448,480},{16,48,80,..., dimensions={0} | all-to-all | bytes 1179648 | tf_op jit(solution)/shard_map/all_to_all | solution.py:62
  199.9 4.9 %collective-permute-start.3 = (f32[1152,128]{1,0:T(8,128)S(1)}, f32[1152,128]{1,0:T(8,128)S(1)}, u32[]{:S(2)}, u32[]{:S(2)}) collective-permute-start(f32[1152,128]{1,0:T(8,128)S(1)} %bitcast.31), channel_id=1, source_target_pairs={{0,16},{16,0},{32,48},{48,32},{64,80},{80,64},{96,112},{112,96},{1... | collective-permute-start | bytes 1769480 | tf_op jit(solution)/shard_map/ppermute | solution.py:75
  206.3 9.1 %shard_map.68 = f32[256,256]{1,0:T(8,128)S(1)} custom-call(f32[256,256]{1,0:T(8,128)S(1)} %pad_maximum_fusion.4.gram_ref), custom_call_target="tpu_custom_call" | custom-call | flops 201326592 | bytes 524288 | tf_op jit(solution)/shard_map/pallas_call | solution.py:122
  218.0 5.6 %all-to-all-start.8 = ((f32[16,1,256]{2,1,0:T(1,128)}), f32[16,1,256]{2,1,0:T(1,128)S(1)}, u32[]{:S(2)}, u32[]{:S(2)}) async-start(f32[16,1,256]{2,1,0:T(1,128)} %reshape.71), calls=%async_computation.8 | async-start | bytes 32768 | tf_op jit(solution)/shard_map/all_to_all | solution.py:62
  223.6 2.9 %fusion = f32[256,896]{1,0:T(8,128)} fusion(f32[256,256]{1,0:T(8,128)} %fusion.20, f32[896,256]{1,0:T(8,128)S(1)} %get-tuple-element.10, f32[256,896]{1,0:T(8,128)S(1)} %copy-done.1, bf16[256,896]{1,0:T(8,128)(2,1)S(1)} %copy-done.2), kind=kOutput, calls=%fused_computation.2 | convolution fusion | flops 705560576 | bytes 3473408 | tf_op jit(solution)/shard_map/dot_general | solution.py:44
  226.6 8.4 %all-to-all-done.8 = f32[16,1,256]{2,1,0:T(1,128)S(1)} async-done(((f32[16,1,256]{2,1,0:T(1,128)}), f32[16,1,256]{2,1,0:T(1,128)S(1)}, u32[]{:S(2)}, u32[]{:S(2)}) %all-to-all-start.8) | async-done | bytes 16416 | tf_op jit(solution)/shard_map/all_to_all | solution.py:62
  236.2 1.8 fusion.2
  (50 shorter events, 16.9 us)
Async XLA Ops:
  0.6 1.2 copy-start
  4.2 53.6 %copy-start.1 = (f32[256,896]{1,0:T(8,128)S(1)}, f32[256,896]{1,0:T(8,128)}, u32[]{:S(2)}) copy-start(f32[256,896]{1,0:T(8,128)} %param.4) | copy-start | bytes 2752516
  4.2 53.6 %copy-start.2 = (bf16[256,896]{1,0:T(8,128)(2,1)S(1)}, bf16[256,896]{1,0:T(8,128)(2,1)}, u32[]{:S(2)}) copy-start(bf16[256,896]{1,0:T(8,128)(2,1)} %param.5) | copy-start | bytes 1376260
  33.7 24.0 %all-to-all-start.1 = ((f32[16,16,256]{2,1,0:T(8,128)}), f32[16,16,256]{2,1,0:T(8,128)S(1)}, u32[]{:S(2)}, u32[]{:S(2)}) async-start(f32[16,16,256]{2,1,0:T(8,128)} %broadcast_in_dim.14), calls=%async_computation.1 | async-start | bytes 524288 | tf_op jit(solution)/shard_map/all_to_all | solution.py:62
  60.1 9.9 %collective-permute-start = (f32[1152,128]{1,0:T(8,128)S(1)}, f32[1152,128]{1,0:T(8,128)S(1)}, u32[]{:S(2)}, u32[]{:S(2)}) collective-permute-start(f32[1152,128]{1,0:T(8,128)S(1)} %broadcast_select_fusion.5), channel_id=1, source_target_pairs={{0,16},{16,0},{32,48},{48,32},{64,80},{80,64},{96,112},{112,96},{1... | collective-permute-start | bytes 1769480 | tf_op jit(solution)/shard_map/ppermute | solution.py:72
  101.8 6.3 %collective-permute-start.1 = (f32[1152,128]{1,0:T(8,128)S(1)}, f32[1152,128]{1,0:T(8,128)S(1)}, u32[]{:S(2)}, u32[]{:S(2)}) collective-permute-start(f32[1152,128]{1,0:T(8,128)S(1)} %bitcast.32), channel_id=1, source_target_pairs={{0,16},{16,0},{32,48},{48,32},{64,80},{80,64},{96,112},{112,96},{1... | collective-permute-start | bytes 1769480 | tf_op jit(solution)/shard_map/ppermute | solution.py:75
  108.2 1.8 copy-start.3
  110.0 19.5 %all-to-all-start.4 = ((f32[16,16,256]{2,1,0:T(8,128)}), f32[16,16,256]{2,1,0:T(8,128)}, u32[]{:S(2)}, u32[]{:S(2)}) async-start(f32[16,16,256]{2,1,0:T(8,128)} %bitcast.5), calls=%async_computation.4 | async-start | bytes 524288 | tf_op jit(solution)/shard_map/all_to_all | solution.py:55
  161.3 10.4 %collective-permute-start.2 = (f32[1152,128]{1,0:T(8,128)S(1)}, f32[1152,128]{1,0:T(8,128)S(1)}, u32[]{:S(2)}, u32[]{:S(2)}) collective-permute-start(f32[1152,128]{1,0:T(8,128)S(1)} %broadcast_select_fusion.2), channel_id=1, source_target_pairs={{0,16},{16,0},{32,48},{48,32},{64,80},{80,64},{96,112},{112,96},{1... | collective-permute-start | bytes 1769480 | tf_op jit(solution)/shard_map/ppermute | solution.py:72
  199.9 6.3 %collective-permute-start.3 = (f32[1152,128]{1,0:T(8,128)S(1)}, f32[1152,128]{1,0:T(8,128)S(1)}, u32[]{:S(2)}, u32[]{:S(2)}) collective-permute-start(f32[1152,128]{1,0:T(8,128)S(1)} %bitcast.31), channel_id=1, source_target_pairs={{0,16},{16,0},{32,48},{48,32},{64,80},{80,64},{96,112},{112,96},{1... | collective-permute-start | bytes 1769480 | tf_op jit(solution)/shard_map/ppermute | solution.py:75
  218.0 17.0 %all-to-all-start.8 = ((f32[16,1,256]{2,1,0:T(1,128)}), f32[16,1,256]{2,1,0:T(1,128)S(1)}, u32[]{:S(2)}, u32[]{:S(2)}) async-start(f32[16,1,256]{2,1,0:T(1,128)} %reshape.71), calls=%async_computation.8 | async-start | bytes 32768 | tf_op jit(solution)/shard_map/all_to_all | solution.py:62
  235.1 1.0 copy-start.5
  235.1 1.1 copy-start.6
  236.2 1.8 copy-start.4

commit v3 on v0

v3 whole, which is shorter than its diff:
```python
import math

import jax
import jax.numpy as jnp
from jax import lax
from jax.experimental import pallas as pl
from jax.experimental.pallas import tpu as pltpu
from jax.sharding import PartitionSpec as P

ROWS = 8192
COLS = 14336
RANK = 256
ITERS = 2

highest = lax.Precision.HIGHEST
retain = 0.95
step_size = 0.5
norm_eps = 1e-06
step = step_size * math.sqrt(ROWS * COLS / RANK)

MP = 32
DP = 16
HALF = RANK // 2
PANEL = 16
OWN_ROWS = ROWS // MP
OWN_COLS = COLS // DP
SAME_CORE = [[c + 2 * i for i in range(MP // 2)] for c in range(2)]
CORE_PAIRS = [(i, i ^ 1) for i in range(MP)]
NEXT_TO = (((1,), (1,)), ((), ()))


def product(first, second):
    return jnp.dot(first, second, precision=highest, preferred_element_type=jnp.float32)


def outer_rows(first, second):
    return lax.dot_general(
        first, second, NEXT_TO, precision=highest, preferred_element_type=jnp.float32
    )


def two_parts(values):
    high = values.astype(jnp.bfloat16)
    return high, (values - high.astype(jnp.float32)).astype(jnp.bfloat16)


def three_parts(values):
    high = values.astype(jnp.bfloat16)
    rest = values - high.astype(jnp.float32)
    middle = rest.astype(jnp.bfloat16)
    return high, middle, (rest - middle.astype(jnp.float32)).astype(jnp.bfloat16)


def product_of_parts(first, second):
    high, low = two_parts(first)
    other_high, other_low = two_parts(second)
    dot = lambda a, b: jnp.dot(a, b, preferred_element_type=jnp.float32)
    return dot(high, other_high) + (dot(high, other_low) + dot(low, other_high))


def on_diagonal():
    row = lax.broadcasted_iota(jnp.int32, (RANK, RANK), 0)
    return row == lax.broadcasted_iota(jnp.int32, (RANK, RANK), 1)


def as_row(column):
    return jnp.sum(jnp.where(on_diagonal(), column, 0.0), axis=0, keepdims=True)


def as_column(row):
    return jnp.sum(jnp.where(on_diagonal(), row, 0.0), axis=1, keepdims=True)


def scales_of(gram):
    diagonal = jnp.where(on_diagonal(), gram, 0.0)
    return (
        lax.rsqrt(jnp.sum(diagonal, axis=1, keepdims=True)),
        lax.rsqrt(jnp.sum(diagonal, axis=0, keepdims=True)),
    )


def write_inverse_factor(rest, out_ref, unscale):
    lane = lax.broadcasted_iota(jnp.int32, (PANEL, RANK), 1)
    place = lax.broadcasted_iota(jnp.int32, (PANEL, RANK), 0)
    short = place[:, :HALF]
    panel, rest = rest[:PANEL], rest[PANEL:]
    for start in range(0, RANK, PANEL):
        own = [
            jnp.broadcast_to(panel[:, start + t : start + t + 1], (PANEL, HALF))
            for t in range(PANEL)
        ]
        inside = (lane >= start) & (lane < start + PANEL)
        panel = jnp.where(inside, jnp.where(lane - start == place, 1.0, 0.0), panel)
        pivots = own[0]
        for t in range(PANEL):
            if t > 0:
                pivots = jnp.where(short == t, own[t], pivots)
            if t < PANEL - 1:
                below = jnp.where(short > t, own[t], 0.0)
                inverse = jnp.broadcast_to(1.0 / own[t][t : t + 1], (PANEL, HALF))
                for later in range(t + 1, PANEL):
                    own[later] = own[later] - (below * own[later][t : t + 1]) * inverse
                factor = below * inverse
                panel = panel - jnp.concatenate([factor, factor], axis=1) * panel[t : t + 1]
        root = lax.rsqrt(pivots)
        done = panel * jnp.concatenate([root, root], axis=1)
        result = jnp.where(lane < start + PANEL, done, 0.0)
        out_ref[start : start + PANEL, :] = result if unscale is None else result * unscale
        end = start + PANEL
        if end < RANK:
            a, b, c = three_parts(done)
            first = jnp.concatenate([a, a, b, b, a, c], axis=0)
            second = jnp.concatenate([a, b, a, b, c, a], axis=0)
            base = 0 if end < HALF else HALF
            taken = lax.dot_general(
                first[:, base:],
                second,
                (((0,), (0,)), ((), ())),
                preferred_element_type=jnp.float32,
            )
            kept = jnp.where(inside, 0.0, 1.0)[:1]
            at = end - base
            panel = rest[:PANEL] * kept - taken[at : at + PANEL]
            if end + PANEL < RANK:
                rest = rest[PANEL:] * kept - taken[at + PANEL :]


def first_kernel(momentum_ref, gradient_ref, basis_ref, buffer_ref, left_ref):
    buffer = momentum_ref[...] + gradient_ref[...].astype(jnp.float32)
    buffer_ref[...] = buffer
    left_ref[...] = product(buffer, basis_ref[...])


def sums_kernel(left_ref, buffer_ref, out_ref):
    left = left_ref[...]
    turned = left.T
    out_ref[:, :OWN_COLS] = product(turned, buffer_ref[...])
    out_ref[:, OWN_COLS:] = product(turned, left)


def next_left_kernel(sums_ref, buffer_ref, out_ref):
    scale, _ = scales_of(sums_ref[:, OWN_COLS:])
    out_ref[...] = outer_rows(buffer_ref[...], sums_ref[:, :OWN_COLS] * scale)


def middle_kernel(sums_ref, inverse_ref, squares_ref):
    gram = sums_ref[:, OWN_COLS:]
    scale, scale_row = scales_of(gram)
    write_inverse_factor(gram * scale * scale_row, inverse_ref, None)
    right = product(inverse_ref[...], sums_ref[:, :OWN_COLS] * scale)
    squares_ref[...] = as_row(jnp.sum(right * right, axis=1, keepdims=True))


def second_left_kernel(raw_ref, inverse_ref, squares_ref, buffer_ref, left_ref, out_ref):
    squares = jnp.sum(squares_ref[...], axis=0, keepdims=True)
    left = outer_rows(raw_ref[...], inverse_ref[...]) / (jnp.sqrt(squares) + norm_eps)
    left_ref[...] = left
    turned = left.T
    out_ref[:, :OWN_COLS] = product(turned, buffer_ref[...])
    out_ref[:, OWN_COLS:] = product(turned, left)


def last_right_kernel(sums_ref, inverse_ref, right_ref, squares_ref):
    gram = sums_ref[:, OWN_COLS:]
    scale, scale_row = scales_of(gram)
    write_inverse_factor(gram * scale * scale_row, inverse_ref, scale_row)
    right = product(inverse_ref[...], sums_ref[:, :OWN_COLS])
    right_ref[...] = right
    squares = as_row(jnp.sum(right * right, axis=1, keepdims=True))
    squares_ref[...] = jnp.broadcast_to(squares[None], (DP, 1, RANK))


def momentum_kernel(raw_ref, inverse_ref, right_ref, buffer_ref, left_ref, out_ref):
    left = outer_rows(raw_ref[...], inverse_ref[...])
    left_ref[...] = left
    out_ref[...] = buffer_ref[...] - (1.0 - retain) * product_of_parts(left, right_ref[...])


def weight_kernel(left_ref, right_ref, squares_ref, weight_ref, basis_ref, out_ref):
    squares = as_column(jnp.sum(squares_ref[...], axis=0))
    basis = right_ref[...] / (jnp.sqrt(squares) + norm_eps)
    basis_ref[...] = basis.T
    update = product_of_parts(left_ref[...], basis)
    out_ref[...] = (weight_ref[...].astype(jnp.float32) - step * update).astype(jnp.bfloat16)


def call(kernel, products, *shapes, dtypes=None, vmem=24):
    dtypes = dtypes or [jnp.float32] * len(shapes)
    out = tuple(jax.ShapeDtypeStruct(s, d) for s, d in zip(shapes, dtypes))
    return pl.pallas_call(
        kernel,
        out_shape=out if len(out) > 1 else out[0],
        cost_estimate=pl.CostEstimate(
            flops=int(products * 12 * RANK * RANK * OWN_COLS),
            bytes_accessed=4 * RANK * OWN_COLS,
            transcendentals=0,
        ),
        compiler_params=pltpu.CompilerParams(vmem_limit_bytes=vmem * 2**20),
    )


def scatter_sum(values, axis, count, groups=None):
    rows, columns = values.shape
    parts = lax.all_to_all(values, axis, 0, 0, axis_index_groups=groups, tiled=True)
    return jnp.sum(parts.reshape(count, rows // count, columns), axis=0)


def gather(values, axis, count, groups=None):
    copies = jnp.broadcast_to(values[None], (count,) + values.shape)
    return lax.all_to_all(copies, axis, 0, 0, axis_index_groups=groups, tiled=True)


def sum_over_mp(values, core):
    halves = values.reshape(2, HALF, values.shape[1])
    own = lax.dynamic_index_in_dim(halves, core, 0, keepdims=False)
    other = lax.dynamic_index_in_dim(halves, 1 - core, 0, keepdims=False)
    own = own + lax.ppermute(other, "mp", CORE_PAIRS)
    own = scatter_sum(own, "mp", MP // 2, SAME_CORE)
    own = gather(own, "mp", MP // 2, SAME_CORE).reshape(HALF, values.shape[1])
    other = lax.ppermute(own, "mp", CORE_PAIRS)
    return jnp.concatenate(
        [jnp.where(core == 0, own, other), jnp.where(core == 0, other, own)], axis=0
    )


def body(momentum, gradient, weight, right_basis):
    square = (RANK, RANK)
    wide = (RANK, OWN_COLS)
    both = (RANK, OWN_COLS + RANK)
    own_rows = OWN_ROWS // DP

    core, momentum = lax.optimization_barrier((lax.axis_index("mp") % 2, momentum))
    buffer, left = call(first_kernel, 1, (OWN_ROWS, OWN_COLS), (OWN_ROWS, RANK), vmem=60)(
        momentum, gradient, right_basis
    )
    left = gather(scatter_sum(left, "dp", DP), "dp", DP).reshape(OWN_ROWS, RANK)
    sums = sum_over_mp(call(sums_kernel, 1.3, both)(left, buffer), core)
    left = scatter_sum(call(next_left_kernel, 1, square)(sums, buffer), "dp", DP)
    inverse, own_squares = call(middle_kernel, 8, square, (1, RANK))(sums)
    sent = jnp.concatenate([left, own_squares], axis=0).reshape(own_rows + 1, 2, HALF)
    came = gather(sent, "dp", DP)
    raw = came[:, :own_rows].reshape(OWN_ROWS, RANK)
    squares = came[:, own_rows].reshape(DP, RANK)

    left, sums = call(second_left_kernel, 1.6, square, both)(raw, inverse, squares, buffer)
    sums = sum_over_mp(sums, core)
    inverse, right, own_squares = call(last_right_kernel, 8, square, wide, (DP, 1, RANK))(sums)
    squares = lax.all_to_all(own_squares, "dp", 0, 0, tiled=True)
    left, new_momentum = call(momentum_kernel, 1, square, (OWN_ROWS, OWN_COLS))(
        left, inverse, right, buffer
    )
    basis, new_weight = call(
        weight_kernel,
        1,
        (OWN_COLS, RANK),
        (OWN_ROWS, OWN_COLS),
        dtypes=[jnp.float32, jnp.bfloat16],
    )(left, right, squares, weight)
    return (new_weight, new_momentum, basis)


def solution(mesh):
    in_specs = (P("mp", "dp"), P("mp", "dp"), P("mp", "dp"), P("dp", None))
    out_specs = (P("mp", "dp"), P("mp", "dp"), P("dp", None))
    return jax.shard_map(body, mesh=mesh, in_specs=in_specs, out_specs=out_specs, check_vma=False)
```

time: 1040 us -> 228 us (0.22); the launches traced: 1020 us -> 227 us
  waiting for transfers between devices: 810 us -> 33.9 us
  other arithmetic: 111 us -> 0.56 us
  blocking collectives: 48.7 us -> 112 us
  starting transfers between devices: 0.46 us -> 47.7 us
  Pallas kernels: 0 us -> 30.7 us
  matrix products: 22.8 us -> 0 us
  between operations: 17.4 us -> 0.88 us
  local copies, waits for them, and re-layouts: 12.4 us -> 1.05 us
    psum x6 -> x0, waiting for transfers between devices: 810 us -> none  [the longest x2 279 us: body(): gram = lax.psum(inner_rows(left, left), 'mp')]
    all_to_all x0 -> x6, blocking collectives: none -> 112 us  [the longest x3 61.3 us: scatter_sum(): lax.all_to_all(values, axis, 0, 0, axis_index_groups=groups, tiled=True)]
    another operation x18 -> x0, other arithmetic: 108 us -> none  [the longest x13 68.6 us: orthonormal(): factor = jnp.linalg.cholesky(gram)]
    psum x2 -> x0, blocking collectives: 48.7 us -> none  [body(): squares = lax.psum(own_squares, 'dp')]
    pallas_call x0 -> x8, Pallas kernels: none -> 30.7 us  [the longest x1 9.34 us: body(): call(last_right_kernel, 8, square, wide, (DP, 1, RANK))(sums)]
    all_to_all x0 -> x3, waiting for transfers between devices: none -> 27.5 us  [the longest x1 13.1 us: gather(): lax.all_to_all(copies, axis, 0, 0, axis_index_groups=groups, tiled=True)]
    ppermute x0 -> x4, starting transfers between devices: none -> 25.6 us  [the longest x2 16.3 us: sum_over_mp(): own = own + lax.ppermute(other, 'mp', CORE_PAIRS)]
    all_to_all x0 -> x3, starting transfers between devices: none -> 22.2 us  [the longest x1 10.9 us: gather(): lax.all_to_all(copies, axis, 0, 0, axis_index_groups=groups, tiled=True)]
  transfers between devices with their start and end apart: 6 -> 7, of which waited for: 6 -> 7; matrix products, arithmetic and copies ran while one was open for 0% -> 0% of each run, Pallas kernels for 0% -> 5%
where the time goes in v3:
time: 228 us; the launch traced here: 227 us
  blocking collectives  112 us (49%)
  starting transfers between devices  47.7 us (21%)
  waiting for transfers between devices  33.9 us (15%)
  Pallas kernels  30.7 us (13%)
    all_to_all x3, blocking collectives, scatter_sum(): lax.all_to_all(values, axis, 0, 0, axis_index_groups=groups, tiled=True)  61.3 us
    all_to_all x3, blocking collectives, gather(): lax.all_to_all(copies, axis, 0, 0, axis_index_groups=groups, tiled=True)  51.1 us
    ppermute x2, starting transfers between devices, sum_over_mp(): own = own + lax.ppermute(other, 'mp', CORE_PAIRS)  16.3 us
    all_to_all x1, waiting for transfers between devices, gather(): lax.all_to_all(copies, axis, 0, 0, axis_index_groups=groups, tiled=True)  13.1 us
    all_to_all x1, starting transfers between devices, gather(): lax.all_to_all(copies, axis, 0, 0, axis_index_groups=groups, tiled=True)  10.9 us
    pallas_call x1, Pallas kernels, body(): call(last_right_kernel, 8, square, wide, (DP, 1, RANK))(sums)  9.34 us
    ppermute x2, starting transfers between devices, sum_over_mp(): other = lax.ppermute(own, 'mp', CORE_PAIRS)  9.27 us
    all_to_all x1, waiting for transfers between devices, body(): squares = lax.all_to_all(own_squares, 'dp', 0, 0, tiled=True)  9.15 us
  transfers between devices with their start and end apart: 7, of which 7 were waited for; matrix products, arithmetic and copies ran while one was open for 0% of the time, Pallas kernels for 5%

profile of v3, /device:TPU:1, one launch (start us, length us, event | category | flops | bytes accessed | tf_op | source)
XLA Modules:
  0.0 227.2 jit_solution(11560404742465151392)
XLA Ops:
  0.6 3.4 %shard_map.67 = (f32[256,896]{1,0:T(8,128)}, f32[256,256]{1,0:T(8,128)}) custom-call(f32[256,896]{1,0:T(8,128)} %momentum_ref, bf16[256,896]{1,0:T(8,128)(2,1)} %gradient_ref.1, f32[896,256]{1,0:T(8,128)} %basis_ref.1), custom_call_target="tpu_custom_call" | custom-call | flops 704643072 | bytes 917504 | tf_op jit(solution)/shard_map/pallas_call | solution.py:233
  4.1 29.0 %all_to_all.61 = f32[16,16,256]{2,1,0:T(8,128)S(1)} all-to-all(f32[16,16,256]{2,1,0:T(8,128)} %bitcast.47), channel_id=1, replica_groups=mesh['mp'=32,'dp'=16] {'dp'}, dimensions={0} | all-to-all | bytes 524288 | tf_op jit(solution)/shard_map/all_to_all | solution.py:204
  33.8 10.9 %all-to-all-start.1 = ((f32[16,16,256]{2,1,0:T(8,128)}), f32[16,16,256]{2,1,0:T(8,128)S(1)}, u32[]{:S(2)}, u32[]{:S(2)}) async-start(f32[16,16,256]{2,1,0:T(8,128)} %broadcast_in_dim.10), calls=%async_computation.1 | async-start | bytes 524288 | tf_op jit(solution)/shard_map/all_to_all | solution.py:210
  44.8 13.1 %all-to-all-done.1 = f32[16,16,256]{2,1,0:T(8,128)S(1)} async-done(((f32[16,16,256]{2,1,0:T(8,128)}), f32[16,16,256]{2,1,0:T(8,128)S(1)}, u32[]{:S(2)}, u32[]{:S(2)}) %all-to-all-start.1) | async-done | bytes 262176 | tf_op jit(solution)/shard_map/all_to_all | solution.py:210
  59.1 8.3 %collective-permute-start = (f32[128,1152]{1,0:T(8,128)S(1)}, f32[128,1152]{1,0:T(8,128)S(1)}, u32[]{:S(2)}, u32[]{:S(2)}) collective-permute-start(f32[128,1152]{1,0:T(8,128)S(1)} %dynamic-slice_bitcast_fusion.1), channel_id=1, source_target_pairs={{0,16},{16,0},{32,48},{48,32},{64,80},{80,64},{96,112},{112,96},{1... | collective-permute-start | bytes 1769480 | tf_op jit(solution)/shard_map/ppermute | solution.py:217
  69.1 18.0 %all_to_all.62 = f32[16,8,1152]{2,1,0:T(8,128)S(1)} all-to-all(f32[16,8,1152]{2,1,0:T(8,128)S(1)} %fusion.1), channel_id=1, replica_groups={{0,32,64,96,128,160,192,224,256,288,320,352,384,416,448,480},{16,48,80,..., dimensions={0} | all-to-all | bytes 1179648 | tf_op jit(solution)/shard_map/all_to_all | solution.py:204
  87.1 13.8 %all_to_all.63 = f32[16,8,1152]{2,1,0:T(8,128)S(1)} all-to-all(f32[16,8,1152]{2,1,0:T(8,128)S(1)} %broadcast_in_dim.11), channel_id=1, replica_groups={{0,32,64,96,128,160,192,224,256,288,320,352,384,416,448,480},{16,48,80,..., dimensions={0} | all-to-all | bytes 1179648 | tf_op jit(solution)/shard_map/all_to_all | solution.py:210
  100.9 4.6 %collective-permute-start.1 = (f32[128,1152]{1,0:T(8,128)S(1)}, f32[128,1152]{1,0:T(8,128)S(1)}, u32[]{:S(2)}, u32[]{:S(2)}) collective-permute-start(f32[128,1152]{1,0:T(8,128)S(1)} %bitcast.44), channel_id=1, source_target_pairs={{0,16},{16,0},{32,48},{48,32},{64,80},{80,64},{96,112},{112,96},{1... | collective-permute-start | bytes 1769480 | tf_op jit(solution)/shard_map/ppermute | solution.py:220
  107.3 1.9 shard_map.69
  109.2 5.4 %all-to-all-start.4 = ((f32[16,16,256]{2,1,0:T(8,128)}), f32[16,16,256]{2,1,0:T(8,128)S(1)}, u32[]{:S(2)}, u32[]{:S(2)}) async-start(f32[16,16,256]{2,1,0:T(8,128)} %bitcast.7), calls=%async_computation.4 | async-start | bytes 524288 | tf_op jit(solution)/shard_map/all_to_all | solution.py:204
  114.6 8.7 %shard_map.70 = (f32[256,256]{1,0:T(8,128)S(1)}, f32[1,256]{1,0:T(1,128)S(1)}) custom-call(f32[256,1152]{1,0:T(8,128)S(1)} %pad_maximum_fusion.sums_ref), custom_call_target="tpu_custom_call" | custom-call | flops 5637144576 | bytes 917504 | tf_op jit(solution)/shard_map/pallas_call | solution.py:239
  123.4 5.3 %all-to-all-done.4 = f32[16,16,256]{2,1,0:T(8,128)S(1)} async-done(((f32[16,16,256]{2,1,0:T(8,128)}), f32[16,16,256]{2,1,0:T(8,128)S(1)}, u32[]{:S(2)}, u32[]{:S(2)}) %all-to-all-start.4) | async-done | bytes 262176 | tf_op jit(solution)/shard_map/all_to_all | solution.py:204
  128.8 23.6 %all_to_all.64 = f32[16,17,2,128]{3,2,1,0:T(2,128)S(1)} all-to-all(f32[16,17,2,128]{3,2,1,0:T(2,128)S(1)} %broadcast_in_dim.13), channel_id=1, replica_groups=mesh['mp'=32,'dp'=16] {'dp'}, dimensions={0} | all-to-all | bytes 557056 | tf_op jit(solution)/shard_map/all_to_all | solution.py:210
  152.5 2.0 shard_map.71
  154.6 8.0 %collective-permute-start.2 = (f32[128,1152]{1,0:T(8,128)S(1)}, f32[128,1152]{1,0:T(8,128)S(1)}, u32[]{:S(2)}, u32[]{:S(2)}) collective-permute-start(f32[128,1152]{1,0:T(8,128)S(1)} %dynamic-slice_bitcast_fusion), channel_id=1, source_target_pairs={{0,16},{16,0},{32,48},{48,32},{64,80},{80,64},{96,112},{112,96},{1... | collective-permute-start | bytes 1769480 | tf_op jit(solution)/shard_map/ppermute | solution.py:217
  162.6 1.6 collective-permute-done.2
  164.3 14.3 %all_to_all.65 = f32[16,8,1152]{2,1,0:T(8,128)S(1)} all-to-all(f32[16,8,1152]{2,1,0:T(8,128)S(1)} %fusion), channel_id=1, replica_groups={{0,32,64,96,128,160,192,224,256,288,320,352,384,416,448,480},{16,48,80,..., dimensions={0} | all-to-all | bytes 1179648 | tf_op jit(solution)/shard_map/all_to_all | solution.py:204
  178.6 13.8 %all_to_all.66 = f32[16,8,1152]{2,1,0:T(8,128)S(1)} all-to-all(f32[16,8,1152]{2,1,0:T(8,128)S(1)} %broadcast_in_dim.14), channel_id=1, replica_groups={{0,32,64,96,128,160,192,224,256,288,320,352,384,416,448,480},{16,48,80,..., dimensions={0} | all-to-all | bytes 1179648 | tf_op jit(solution)/shard_map/all_to_all | solution.py:210
  192.4 4.6 %collective-permute-start.3 = (f32[128,1152]{1,0:T(8,128)S(1)}, f32[128,1152]{1,0:T(8,128)S(1)}, u32[]{:S(2)}, u32[]{:S(2)}) collective-permute-start(f32[128,1152]{1,0:T(8,128)S(1)} %bitcast.45), channel_id=1, source_target_pairs={{0,16},{16,0},{32,48},{48,32},{64,80},{80,64},{96,112},{112,96},{1... | collective-permute-start | bytes 1769480 | tf_op jit(solution)/shard_map/ppermute | solution.py:220
  198.8 9.3 %shard_map.72 = (f32[256,256]{1,0:T(8,128)S(1)}, f32[256,896]{1,0:T(8,128)S(1)}, f32[16,1,256]{2,1,0:T(1,128)}) custom-call(f32[256,1152]{1,0:T(8,128)S(1)} %pad_maximum_fusion.1.sums_ref), custom_call_target="tpu_custom_call" | custom-call | flops 5637144576 | bytes 917504 | tf_op jit(solution)/shard_map/pallas_call | solution.py:247
  208.2 5.8 %all-to-all-start.8 = ((f32[16,1,256]{2,1,0:T(1,128)}), f32[16,1,256]{2,1,0:T(1,128)S(1)}, u32[]{:S(2)}, u32[]{:S(2)}) async-start(f32[16,1,256]{2,1,0:T(1,128)} %get-tuple-element.29), calls=%async_computation.8 | async-start | bytes 32768 | tf_op jit(solution)/shard_map/all_to_all | solution.py:248
  214.0 2.2 shard_map.73
  216.2 9.1 %all-to-all-done.8.squares_ref = f32[16,1,256]{2,1,0:T(1,128)S(1)} async-done(((f32[16,1,256]{2,1,0:T(1,128)}), f32[16,1,256]{2,1,0:T(1,128)S(1)}, u32[]{:S(2)}, u32[]{:S(2)}) %all-to-all-start.8) | async-done | bytes 16416 | tf_op jit(solution)/shard_map/all_to_all | solution.py:248
  225.4 1.8 shard_map.74
  (30 shorter events, 7.6 us)
Async XLA Ops:
  4.1 53.8 %copy-start.1 = (f32[256,896]{1,0:T(8,128)S(1)}, f32[256,896]{1,0:T(8,128)}, u32[]{:S(2)}) copy-start(f32[256,896]{1,0:T(8,128)} %get-tuple-element.21.buffer_ref) | copy-start | bytes 2752516
  33.8 24.0 %all-to-all-start.1 = ((f32[16,16,256]{2,1,0:T(8,128)}), f32[16,16,256]{2,1,0:T(8,128)S(1)}, u32[]{:S(2)}, u32[]{:S(2)}) async-start(f32[16,16,256]{2,1,0:T(8,128)} %broadcast_in_dim.10), calls=%async_computation.1 | async-start | bytes 524288 | tf_op jit(solution)/shard_map/all_to_all | solution.py:210
  59.1 9.9 %collective-permute-start = (f32[128,1152]{1,0:T(8,128)S(1)}, f32[128,1152]{1,0:T(8,128)S(1)}, u32[]{:S(2)}, u32[]{:S(2)}) collective-permute-start(f32[128,1152]{1,0:T(8,128)S(1)} %dynamic-slice_bitcast_fusion.1), channel_id=1, source_target_pairs={{0,16},{16,0},{32,48},{48,32},{64,80},{80,64},{96,112},{112,96},{1... | collective-permute-start | bytes 1769480 | tf_op jit(solution)/shard_map/ppermute | solution.py:217
  100.9 6.3 %collective-permute-start.1 = (f32[128,1152]{1,0:T(8,128)S(1)}, f32[128,1152]{1,0:T(8,128)S(1)}, u32[]{:S(2)}, u32[]{:S(2)}) collective-permute-start(f32[128,1152]{1,0:T(8,128)S(1)} %bitcast.44), channel_id=1, source_target_pairs={{0,16},{16,0},{32,48},{48,32},{64,80},{80,64},{96,112},{112,96},{1... | collective-permute-start | bytes 1769480 | tf_op jit(solution)/shard_map/ppermute | solution.py:220
  109.2 19.4 %all-to-all-start.4 = ((f32[16,16,256]{2,1,0:T(8,128)}), f32[16,16,256]{2,1,0:T(8,128)S(1)}, u32[]{:S(2)}, u32[]{:S(2)}) async-start(f32[16,16,256]{2,1,0:T(8,128)} %bitcast.7), calls=%async_computation.4 | async-start | bytes 524288 | tf_op jit(solution)/shard_map/all_to_all | solution.py:204
  154.6 9.6 %collective-permute-start.2 = (f32[128,1152]{1,0:T(8,128)S(1)}, f32[128,1152]{1,0:T(8,128)S(1)}, u32[]{:S(2)}, u32[]{:S(2)}) collective-permute-start(f32[128,1152]{1,0:T(8,128)S(1)} %dynamic-slice_bitcast_fusion), channel_id=1, source_target_pairs={{0,16},{16,0},{32,48},{48,32},{64,80},{80,64},{96,112},{112,96},{1... | collective-permute-start | bytes 1769480 | tf_op jit(solution)/shard_map/ppermute | solution.py:217
  192.4 6.3 %collective-permute-start.3 = (f32[128,1152]{1,0:T(8,128)S(1)}, f32[128,1152]{1,0:T(8,128)S(1)}, u32[]{:S(2)}, u32[]{:S(2)}) collective-permute-start(f32[128,1152]{1,0:T(8,128)S(1)} %bitcast.45), channel_id=1, source_target_pairs={{0,16},{16,0},{32,48},{48,32},{64,80},{80,64},{96,112},{112,96},{1... | collective-permute-start | bytes 1769480 | tf_op jit(solution)/shard_map/ppermute | solution.py:220
  208.2 17.2 %all-to-all-start.8 = ((f32[16,1,256]{2,1,0:T(1,128)}), f32[16,1,256]{2,1,0:T(1,128)S(1)}, u32[]{:S(2)}, u32[]{:S(2)}) async-start(f32[16,1,256]{2,1,0:T(1,128)} %get-tuple-element.29), calls=%async_computation.8 | async-start | bytes 32768 | tf_op jit(solution)/shard_map/all_to_all | solution.py:248
  214.0 11.4 %copy-start = (bf16[256,896]{1,0:T(8,128)(2,1)S(1)}, bf16[256,896]{1,0:T(8,128)(2,1)}, u32[]{:S(2)}) copy-start(bf16[256,896]{1,0:T(8,128)(2,1)} %weight_ref.1) | copy-start | bytes 1376260

commit v4 on v3

--- a/solution.py
+++ b/solution.py
@@ -21,7 +21,7 @@
 MP = 32
 DP = 16
 HALF = RANK // 2
-PANEL = 16
+PANEL = 32
 OWN_ROWS = ROWS // MP
 OWN_COLS = COLS // DP
 SAME_CORE = [[c + 2 * i for i in range(MP // 2)] for c in range(2)]
@@ -82,28 +82,44 @@
 def write_inverse_factor(rest, out_ref, unscale):
     lane = lax.broadcasted_iota(jnp.int32, (PANEL, RANK), 1)
     place = lax.broadcasted_iota(jnp.int32, (PANEL, RANK), 0)
-    short = place[:, :HALF]
+    short = lax.broadcasted_iota(jnp.int32, (8, HALF), 0)
+    groups = PANEL // 8
     panel, rest = rest[:PANEL], rest[PANEL:]
     for start in range(0, RANK, PANEL):
         own = [
-            jnp.broadcast_to(panel[:, start + t : start + t + 1], (PANEL, HALF))
+            {
+                g: jnp.broadcast_to(
+                    panel[8 * g : 8 * g + 8, start + t : start + t + 1], (8, HALF)
+                )
+                for g in range(t // 8, groups)
+            }
             for t in range(PANEL)
         ]
         inside = (lane >= start) & (lane < start + PANEL)
         panel = jnp.where(inside, jnp.where(lane - start == place, 1.0, 0.0), panel)
-        pivots = own[0]
+        rows = [panel[8 * g : 8 * g + 8] for g in range(groups)]
+        pivots = [None] * groups
         for t in range(PANEL):
-            if t > 0:
-                pivots = jnp.where(short == t, own[t], pivots)
-            if t < PANEL - 1:
-                below = jnp.where(short > t, own[t], 0.0)
-                inverse = jnp.broadcast_to(1.0 / own[t][t : t + 1], (PANEL, HALF))
-                for later in range(t + 1, PANEL):
-                    own[later] = own[later] - (below * own[later][t : t + 1]) * inverse
-                factor = below * inverse
-                panel = panel - jnp.concatenate([factor, factor], axis=1) * panel[t : t + 1]
-        root = lax.rsqrt(pivots)
-        done = panel * jnp.concatenate([root, root], axis=1)
+            at, row = divmod(t, 8)
+            column = own[t]
+            pivots[at] = jnp.where(short == row, column[at], pivots[at]) if row else column[at]
+            if t == PANEL - 1:
+                break
+            inverse = jnp.broadcast_to(1.0 / column[at][row : row + 1], (8, HALF))
+            factor = {g: column[g] * inverse for g in range(at, groups)}
+            factor[at] = jnp.where(short > row, factor[at], 0.0)
+            for later in range(t + 1, PANEL):
+                its_group, its_row = divmod(later, 8)
+                pivot_row = jnp.broadcast_to(column[its_group][its_row : its_row + 1], (8, HALF))
+                for g in range(its_group, groups):
+                    own[later][g] = own[later][g] - factor[g] * pivot_row
+            pivot_row = rows[at][row : row + 1]
+            for g in range(at, groups):
+                rows[g] = rows[g] - jnp.concatenate([factor[g]] * 2, axis=1) * pivot_row
+        for g in range(groups):
+            root = lax.rsqrt(pivots[g])
+            rows[g] = rows[g] * jnp.concatenate([root, root], axis=1)
+        done = jnp.concatenate(rows, axis=0)
         result = jnp.where(lane < start + PANEL, done, 0.0)
         out_ref[start : start + PANEL, :] = result if unscale is None else result * unscale
         end = start + PANEL
@@ -125,22 +141,25 @@
                 rest = rest[PANEL:] * kept - taken[at + PANEL :]
 
 
-def first_kernel(momentum_ref, gradient_ref, basis_ref, buffer_ref, left_ref):
-    buffer = momentum_ref[...] + gradient_ref[...].astype(jnp.float32)
-    buffer_ref[...] = buffer
-    left_ref[...] = product(buffer, basis_ref[...])
-
-
-def sums_kernel(left_ref, buffer_ref, out_ref):
+def buffer_of(momentum_ref, gradient_ref):
+    return momentum_ref[...] + gradient_ref[...].astype(jnp.float32)
+
+
+def first_kernel(momentum_ref, gradient_ref, basis_ref, left_ref):
+    left_ref[...] = product(buffer_of(momentum_ref, gradient_ref), basis_ref[...])
+
+
+def sums_kernel(left_ref, momentum_ref, gradient_ref, out_ref):
     left = left_ref[...]
     turned = left.T
-    out_ref[:, :OWN_COLS] = product(turned, buffer_ref[...])
+    out_ref[:, :OWN_COLS] = product(turned, buffer_of(momentum_ref, gradient_ref))
     out_ref[:, OWN_COLS:] = product(turned, left)
 
 
-def next_left_kernel(sums_ref, buffer_ref, out_ref):
+def next_left_kernel(sums_ref, momentum_ref, gradient_ref, out_ref):
     scale, _ = scales_of(sums_ref[:, OWN_COLS:])
-    out_ref[...] = outer_rows(buffer_ref[...], sums_ref[:, :OWN_COLS] * scale)
+    buffer = buffer_of(momentum_ref, gradient_ref)
+    out_ref[...] = outer_rows(buffer, sums_ref[:, :OWN_COLS] * scale)
 
 
 def middle_kernel(sums_ref, inverse_ref, squares_ref):
@@ -151,12 +170,14 @@
     squares_ref[...] = as_row(jnp.sum(right * right, axis=1, keepdims=True))
 
 
-def second_left_kernel(raw_ref, inverse_ref, squares_ref, buffer_ref, left_ref, out_ref):
+def second_left_kernel(
+    raw_ref, inverse_ref, squares_ref, momentum_ref, gradient_ref, left_ref, out_ref
+):
     squares = jnp.sum(squares_ref[...], axis=0, keepdims=True)
     left = outer_rows(raw_ref[...], inverse_ref[...]) / (jnp.sqrt(squares) + norm_eps)
     left_ref[...] = left
     turned = left.T
-    out_ref[:, :OWN_COLS] = product(turned, buffer_ref[...])
+    out_ref[:, :OWN_COLS] = product(turned, buffer_of(momentum_ref, gradient_ref))
     out_ref[:, OWN_COLS:] = product(turned, left)
 
 
@@ -170,22 +191,34 @@
     squares_ref[...] = jnp.broadcast_to(squares[None], (DP, 1, RANK))
 
 
-def momentum_kernel(raw_ref, inverse_ref, right_ref, buffer_ref, left_ref, out_ref):
+def momentum_kernel(
+    raw_ref, inverse_ref, right_ref, momentum_ref, gradient_ref, left_ref, out_ref
+):
     left = outer_rows(raw_ref[...], inverse_ref[...])
     left_ref[...] = left
-    out_ref[...] = buffer_ref[...] - (1.0 - retain) * product_of_parts(left, right_ref[...])
-
-
-def weight_kernel(left_ref, right_ref, squares_ref, weight_ref, basis_ref, out_ref):
+    buffer = buffer_of(momentum_ref, gradient_ref)
+    out_ref[...] = buffer - (1.0 - retain) * product_of_parts(left, right_ref[...])
+
+
+def weight_kernel(
+    left_ref, right_ref, squares_ref, weight_ref, basis_out, weight_out, own_b, own_w, done
+):
     squares = as_column(jnp.sum(squares_ref[...], axis=0))
     basis = right_ref[...] / (jnp.sqrt(squares) + norm_eps)
-    basis_ref[...] = basis.T
+    own_b[...] = basis.T
+    first = pltpu.make_async_copy(own_b, basis_out, done.at[0])
+    first.start()
     update = product_of_parts(left_ref[...], basis)
-    out_ref[...] = (weight_ref[...].astype(jnp.float32) - step * update).astype(jnp.bfloat16)
-
-
-def call(kernel, products, *shapes, dtypes=None, vmem=24):
-    dtypes = dtypes or [jnp.float32] * len(shapes)
+    own_w[...] = (weight_ref[...].astype(jnp.float32) - step * update).astype(jnp.bfloat16)
+    second = pltpu.make_async_copy(own_w, weight_out, done.at[1])
+    second.start()
+    first.wait()
+    second.wait()
+
+
+def call(kernel, products, *shapes, **options):
+    vmem = options.pop("vmem", 24)
+    dtypes = options.pop("dtypes", [jnp.float32] * len(shapes))
     out = tuple(jax.ShapeDtypeStruct(s, d) for s, d in zip(shapes, dtypes))
     return pl.pallas_call(
         kernel,
@@ -196,6 +229,7 @@
             transcendentals=0,
         ),
         compiler_params=pltpu.CompilerParams(vmem_limit_bytes=vmem * 2**20),
+        **options,
     )
 
 
@@ -210,16 +244,17 @@
     return lax.all_to_all(copies, axis, 0, 0, axis_index_groups=groups, tiled=True)
 
 
-def sum_over_mp(values, core):
-    halves = values.reshape(2, HALF, values.shape[1])
-    own = lax.dynamic_index_in_dim(halves, core, 0, keepdims=False)
-    other = lax.dynamic_index_in_dim(halves, 1 - core, 0, keepdims=False)
+def sum_over_mp(values, first_core, own_start, other_start):
+    width = values.shape[1]
+    zero = own_start * 0
+    own = lax.dynamic_slice(values, (own_start, zero), (HALF, width))
+    other = lax.dynamic_slice(values, (other_start, zero), (HALF, width))
     own = own + lax.ppermute(other, "mp", CORE_PAIRS)
     own = scatter_sum(own, "mp", MP // 2, SAME_CORE)
-    own = gather(own, "mp", MP // 2, SAME_CORE).reshape(HALF, values.shape[1])
+    own = gather(own, "mp", MP // 2, SAME_CORE).reshape(HALF, width)
     other = lax.ppermute(own, "mp", CORE_PAIRS)
     return jnp.concatenate(
-        [jnp.where(core == 0, own, other), jnp.where(core == 0, other, own)], axis=0
+        [jnp.where(first_core, own, other), jnp.where(first_core, other, own)], axis=0
     )
 
 
@@ -227,34 +262,47 @@
     square = (RANK, RANK)
     wide = (RANK, OWN_COLS)
     both = (RANK, OWN_COLS + RANK)
+    block = (OWN_ROWS, OWN_COLS)
     own_rows = OWN_ROWS // DP
-
-    core, momentum = lax.optimization_barrier((lax.axis_index("mp") % 2, momentum))
-    buffer, left = call(first_kernel, 1, (OWN_ROWS, OWN_COLS), (OWN_ROWS, RANK), vmem=60)(
-        momentum, gradient, right_basis
-    )
+    anywhere = pl.BlockSpec(memory_space=pl.ANY)
+
+    core = (lax.axis_index("mp") % 2).astype(jnp.uint32)
+    *halves, right_basis = lax.optimization_barrier(
+        (core == 0, core * HALF, HALF - core * HALF, right_basis)
+    )
+
+    left = call(first_kernel, 1, (OWN_ROWS, RANK), vmem=60)(momentum, gradient, right_basis)
     left = gather(scatter_sum(left, "dp", DP), "dp", DP).reshape(OWN_ROWS, RANK)
-    sums = sum_over_mp(call(sums_kernel, 1.3, both)(left, buffer), core)
-    left = scatter_sum(call(next_left_kernel, 1, square)(sums, buffer), "dp", DP)
+    sums = sum_over_mp(call(sums_kernel, 1.3, both)(left, momentum, gradient), *halves)
+    left = call(next_left_kernel, 1, square)(sums, momentum, gradient)
+    left = scatter_sum(left, "dp", DP)
     inverse, own_squares = call(middle_kernel, 8, square, (1, RANK))(sums)
     sent = jnp.concatenate([left, own_squares], axis=0).reshape(own_rows + 1, 2, HALF)
     came = gather(sent, "dp", DP)
     raw = came[:, :own_rows].reshape(OWN_ROWS, RANK)
     squares = came[:, own_rows].reshape(DP, RANK)
 
-    left, sums = call(second_left_kernel, 1.6, square, both)(raw, inverse, squares, buffer)
-    sums = sum_over_mp(sums, core)
+    left, sums = call(second_left_kernel, 1.6, square, both)(
+        raw, inverse, squares, momentum, gradient
+    )
+    sums = sum_over_mp(sums, *halves)
     inverse, right, own_squares = call(last_right_kernel, 8, square, wide, (DP, 1, RANK))(sums)
     squares = lax.all_to_all(own_squares, "dp", 0, 0, tiled=True)
-    left, new_momentum = call(momentum_kernel, 1, square, (OWN_ROWS, OWN_COLS))(
-        left, inverse, right, buffer
+    left, new_momentum = call(momentum_kernel, 1, square, block)(
+        left, inverse, right, momentum, gradient
     )
     basis, new_weight = call(
         weight_kernel,
         1,
         (OWN_COLS, RANK),
-        (OWN_ROWS, OWN_COLS),
+        block,
         dtypes=[jnp.float32, jnp.bfloat16],
+        out_specs=(anywhere, anywhere),
+        scratch_shapes=[
+            pltpu.VMEM((OWN_COLS, RANK), jnp.float32),
+            pltpu.VMEM(block, jnp.bfloat16),
+            pltpu.SemaphoreType.DMA((2,)),
+        ],
     )(left, right, squares, weight)
     return (new_weight, new_momentum, basis)
 

time: 228 us -> 227 us (level)
  blocking collectives: 112 us -> 136 us
  waiting for transfers between devices: 33.9 us -> 21.1 us
  starting transfers between devices: 47.7 us -> 36.8 us
    all_to_all x3 -> x4, blocking collectives: 51.1 us -> 74.9 us  [gather(): lax.all_to_all(copies, axis, 0, 0, axis_index_groups=groups, tiled=True)]
    all_to_all x1 -> x0, waiting for transfers between devices: 13.1 us -> none  [gather(): lax.all_to_all(copies, axis, 0, 0, axis_index_groups=groups, tiled=True)]
    all_to_all x1 -> x0, starting transfers between devices: 10.9 us -> none  [gather(): lax.all_to_all(copies, axis, 0, 0, axis_index_groups=groups, tiled=True)]
  transfers between devices with their start and end apart: 7 -> 6, of which waited for: 7 -> 6; matrix products, arithmetic and copies ran while one was open for 0% -> 0% of each run, Pallas kernels for 5% -> 5%
where the time goes in v4:
time: 227 us; the launch traced here: 226 us
  blocking collectives  136 us (60%)
  starting transfers between devices  36.8 us (16%)
  Pallas kernels  30.3 us (13%)
  waiting for transfers between devices  21.1 us (9%)
    all_to_all x4, blocking collectives, gather(): lax.all_to_all(copies, axis, 0, 0, axis_index_groups=groups, tiled=True)  74.9 us
    all_to_all x3, blocking collectives, scatter_sum(): lax.all_to_all(values, axis, 0, 0, axis_index_groups=groups, tiled=True)  61.3 us
    ppermute x2, starting transfers between devices, sum_over_mp(): own = own + lax.ppermute(other, 'mp', CORE_PAIRS)  16.3 us
    ppermute x2, starting transfers between devices, sum_over_mp(): other = lax.ppermute(own, 'mp', CORE_PAIRS)  9.27 us
    all_to_all x1, waiting for transfers between devices, body(): squares = lax.all_to_all(own_squares, 'dp', 0, 0, tiled=True)  9.15 us
    pallas_call x1, Pallas kernels, body(): call(last_right_kernel, 8, square, wide, (DP, 1, RANK))(sums)  9.06 us
    pallas_call x1, Pallas kernels, body(): inverse, own_squares = call(middle_kernel, 8, square, (1, RANK))(sums)  8.49 us
    all_to_all x1, starting transfers between devices, body(): squares = lax.all_to_all(own_squares, 'dp', 0, 0, tiled=True)  5.81 us
  transfers between devices with their start and end apart: 6, of which 6 were waited for; matrix products, arithmetic and copies ran while one was open for 0% of the time, Pallas kernels for 5%

profile of v4, /device:TPU:1, one launch (start us, length us, event | category | flops | bytes accessed | tf_op | source)
XLA Modules:
  0.0 226.3 jit_solution(4074198096744038639)
XLA Ops:
  0.6 3.4 %shard_map.67 = f32[256,256]{1,0:T(8,128)} custom-call(f32[256,896]{1,0:T(8,128)} %momentum_ref.9, bf16[256,896]{1,0:T(8,128)(2,1)} %gradient_ref.9, f32[896,256]{1,0:T(8,128)} %basis_ref), custom_call_target="tpu_custom_call" | custom-call | flops 704643072 | bytes 917504 | tf_op jit(solution)/shard_map/pallas_call | solution.py:274
  4.1 29.0 %all_to_all.61 = f32[16,16,256]{2,1,0:T(8,128)S(1)} all-to-all(f32[16,16,256]{2,1,0:T(8,128)} %bitcast.29), channel_id=1, replica_groups=mesh['mp'=32,'dp'=16] {'dp'}, dimensions={0} | all-to-all | bytes 524288 | tf_op jit(solution)/shard_map/all_to_all | solution.py:238
  33.1 23.8 %all_to_all.62 = f32[16,16,256]{2,1,0:T(8,128)S(1)} all-to-all(f32[16,16,256]{2,1,0:T(8,128)S(1)} %broadcast_in_dim.10), channel_id=1, replica_groups=mesh['mp'=32,'dp'=16] {'dp'}, dimensions={0} | all-to-all | bytes 524288 | tf_op jit(solution)/shard_map/all_to_all | solution.py:244
  58.3 8.3 %collective-permute-start = (f32[128,1152]{1,0:T(8,128)S(1)}, f32[128,1152]{1,0:T(8,128)S(1)}, u32[]{:S(2)}, u32[]{:S(2)}) collective-permute-start(f32[128,1152]{1,0:T(8,128)S(1)} %constant_dynamic-slice_fusion.1), channel_id=1, source_target_pairs={{0,16},{16,0},{32,48},{48,32},{64,80},{80,64},{96,112},{112,96},{1... | collective-permute-start | bytes 1769480 | tf_op jit(solution)/shard_map/ppermute | solution.py:252
  66.5 1.6 collective-permute-done
  68.2 18.0 %all_to_all.63 = f32[16,8,1152]{2,1,0:T(8,128)S(1)} all-to-all(f32[16,8,1152]{2,1,0:T(8,128)S(1)} %add_bitcast_fusion.1), channel_id=1, replica_groups={{0,32,64,96,128,160,192,224,256,288,320,352,384,416,448,480},{16,48,80,..., dimensions={0} | all-to-all | bytes 1179648 | tf_op jit(solution)/shard_map/all_to_all | solution.py:238
  86.3 13.8 %all_to_all.64 = f32[16,8,1152]{2,1,0:T(8,128)S(1)} all-to-all(f32[16,8,1152]{2,1,0:T(8,128)S(1)} %broadcast_in_dim.11), channel_id=1, replica_groups={{0,32,64,96,128,160,192,224,256,288,320,352,384,416,448,480},{16,48,80,..., dimensions={0} | all-to-all | bytes 1179648 | tf_op jit(solution)/shard_map/all_to_all | solution.py:244
  100.0 4.6 %collective-permute-start.1 = (f32[128,1152]{1,0:T(8,128)S(1)}, f32[128,1152]{1,0:T(8,128)S(1)}, u32[]{:S(2)}, u32[]{:S(2)}) collective-permute-start(f32[128,1152]{1,0:T(8,128)S(1)} %bitcast.27), channel_id=1, source_target_pairs={{0,16},{16,0},{32,48},{48,32},{64,80},{80,64},{96,112},{112,96},{1... | collective-permute-start | bytes 1769480 | tf_op jit(solution)/shard_map/ppermute | solution.py:255
  104.7 1.6 collective-permute-done.1
  106.5 1.9 shard_map.69
  108.4 5.4 %all-to-all-start.4 = ((f32[16,16,256]{2,1,0:T(8,128)}), f32[16,16,256]{2,1,0:T(8,128)S(1)}, u32[]{:S(2)}, u32[]{:S(2)}) async-start(f32[16,16,256]{2,1,0:T(8,128)} %bitcast.4), calls=%async_computation.4 | async-start | bytes 524288 | tf_op jit(solution)/shard_map/all_to_all | solution.py:238
  113.8 8.5 %shard_map.70 = (f32[256,256]{1,0:T(8,128)S(1)}, f32[1,256]{1,0:T(1,128)S(1)}) custom-call(f32[256,1152]{1,0:T(8,128)S(1)} %pad_maximum_fusion.sums_ref), custom_call_target="tpu_custom_call" | custom-call | flops 5637144576 | bytes 917504 | tf_op jit(solution)/shard_map/pallas_call | solution.py:279
  122.3 5.5 %all-to-all-done.4 = f32[16,16,256]{2,1,0:T(8,128)S(1)} async-done(((f32[16,16,256]{2,1,0:T(8,128)}), f32[16,16,256]{2,1,0:T(8,128)S(1)}, u32[]{:S(2)}, u32[]{:S(2)}) %all-to-all-start.4) | async-done | bytes 262176 | tf_op jit(solution)/shard_map/all_to_all | solution.py:238
  128.0 23.6 %all_to_all.65 = f32[16,17,2,128]{3,2,1,0:T(2,128)S(1)} all-to-all(f32[16,17,2,128]{3,2,1,0:T(2,128)S(1)} %broadcast_in_dim.13), channel_id=1, replica_groups=mesh['mp'=32,'dp'=16] {'dp'}, dimensions={0} | all-to-all | bytes 557056 | tf_op jit(solution)/shard_map/all_to_all | solution.py:244
  151.7 2.1 shard_map.71
  153.8 8.0 %collective-permute-start.2 = (f32[128,1152]{1,0:T(8,128)S(1)}, f32[128,1152]{1,0:T(8,128)S(1)}, u32[]{:S(2)}, u32[]{:S(2)}) collective-permute-start(f32[128,1152]{1,0:T(8,128)S(1)} %constant_dynamic-slice_fusion), channel_id=1, source_target_pairs={{0,16},{16,0},{32,48},{48,32},{64,80},{80,64},{96,112},{112,96},{1... | collective-permute-start | bytes 1769480 | tf_op jit(solution)/shard_map/ppermute | solution.py:252
  163.5 14.3 %all_to_all.66 = f32[16,8,1152]{2,1,0:T(8,128)S(1)} all-to-all(f32[16,8,1152]{2,1,0:T(8,128)S(1)} %add_bitcast_fusion), channel_id=1, replica_groups={{0,32,64,96,128,160,192,224,256,288,320,352,384,416,448,480},{16,48,80,..., dimensions={0} | all-to-all | bytes 1179648 | tf_op jit(solution)/shard_map/all_to_all | solution.py:238
  177.8 13.8 %all_to_all.67 = f32[16,8,1152]{2,1,0:T(8,128)S(1)} all-to-all(f32[16,8,1152]{2,1,0:T(8,128)S(1)} %broadcast_in_dim.14), channel_id=1, replica_groups={{0,32,64,96,128,160,192,224,256,288,320,352,384,416,448,480},{16,48,80,..., dimensions={0} | all-to-all | bytes 1179648 | tf_op jit(solution)/shard_map/all_to_all | solution.py:244
  191.6 4.6 %collective-permute-start.3 = (f32[128,1152]{1,0:T(8,128)S(1)}, f32[128,1152]{1,0:T(8,128)S(1)}, u32[]{:S(2)}, u32[]{:S(2)}) collective-permute-start(f32[128,1152]{1,0:T(8,128)S(1)} %bitcast.26), channel_id=1, source_target_pairs={{0,16},{16,0},{32,48},{48,32},{64,80},{80,64},{96,112},{112,96},{1... | collective-permute-start | bytes 1769480 | tf_op jit(solution)/shard_map/ppermute | solution.py:255
  198.0 9.1 %shard_map.72 = (f32[256,256]{1,0:T(8,128)S(1)}, f32[256,896]{1,0:T(8,128)S(1)}, f32[16,1,256]{2,1,0:T(1,128)}) custom-call(f32[256,1152]{1,0:T(8,128)S(1)} %pad_maximum_fusion.1.sums_ref), custom_call_target="tpu_custom_call" | custom-call | flops 5637144576 | bytes 917504 | tf_op jit(solution)/shard_map/pallas_call | solution.py:289
  207.1 5.8 %all-to-all-start.8 = ((f32[16,1,256]{2,1,0:T(1,128)}), f32[16,1,256]{2,1,0:T(1,128)S(1)}, u32[]{:S(2)}, u32[]{:S(2)}) async-start(f32[16,1,256]{2,1,0:T(1,128)} %get-tuple-element.29), calls=%async_computation.8 | async-start | bytes 32768 | tf_op jit(solution)/shard_map/all_to_all | solution.py:290
  212.9 2.2 shard_map.73
  215.1 9.2 %all-to-all-done.8.squares_ref = f32[16,1,256]{2,1,0:T(1,128)S(1)} async-done(((f32[16,1,256]{2,1,0:T(1,128)}), f32[16,1,256]{2,1,0:T(1,128)S(1)}, u32[]{:S(2)}, u32[]{:S(2)}) %all-to-all-start.8) | async-done | bytes 16416 | tf_op jit(solution)/shard_map/all_to_all | solution.py:290
  224.3 1.8 shard_map.74
  (31 shorter events, 5.4 us)
Async XLA Ops:
  4.1 52.9 %copy-start = (f32[256,896]{1,0:T(8,128)S(1)}, f32[256,896]{1,0:T(8,128)}, u32[]{:S(2)}) copy-start(f32[256,896]{1,0:T(8,128)} %momentum_ref.9) | copy-start | bytes 2752516
  4.1 52.9 %copy-start.1 = (bf16[256,896]{1,0:T(8,128)(2,1)S(1)}, bf16[256,896]{1,0:T(8,128)(2,1)}, u32[]{:S(2)}) copy-start(bf16[256,896]{1,0:T(8,128)(2,1)} %gradient_ref.9) | copy-start | bytes 1376260
  58.3 9.9 %collective-permute-start = (f32[128,1152]{1,0:T(8,128)S(1)}, f32[128,1152]{1,0:T(8,128)S(1)}, u32[]{:S(2)}, u32[]{:S(2)}) collective-permute-start(f32[128,1152]{1,0:T(8,128)S(1)} %constant_dynamic-slice_fusion.1), channel_id=1, source_target_pairs={{0,16},{16,0},{32,48},{48,32},{64,80},{80,64},{96,112},{112,96},{1... | collective-permute-start | bytes 1769480 | tf_op jit(solution)/shard_map/ppermute | solution.py:252
  100.0 6.3 %collective-permute-start.1 = (f32[128,1152]{1,0:T(8,128)S(1)}, f32[128,1152]{1,0:T(8,128)S(1)}, u32[]{:S(2)}, u32[]{:S(2)}) collective-permute-start(f32[128,1152]{1,0:T(8,128)S(1)} %bitcast.27), channel_id=1, source_target_pairs={{0,16},{16,0},{32,48},{48,32},{64,80},{80,64},{96,112},{112,96},{1... | collective-permute-start | bytes 1769480 | tf_op jit(solution)/shard_map/ppermute | solution.py:255
  108.4 19.4 %all-to-all-start.4 = ((f32[16,16,256]{2,1,0:T(8,128)}), f32[16,16,256]{2,1,0:T(8,128)S(1)}, u32[]{:S(2)}, u32[]{:S(2)}) async-start(f32[16,16,256]{2,1,0:T(8,128)} %bitcast.4), calls=%async_computation.4 | async-start | bytes 524288 | tf_op jit(solution)/shard_map/all_to_all | solution.py:238
  153.8 9.6 %collective-permute-start.2 = (f32[128,1152]{1,0:T(8,128)S(1)}, f32[128,1152]{1,0:T(8,128)S(1)}, u32[]{:S(2)}, u32[]{:S(2)}) collective-permute-start(f32[128,1152]{1,0:T(8,128)S(1)} %constant_dynamic-slice_fusion), channel_id=1, source_target_pairs={{0,16},{16,0},{32,48},{48,32},{64,80},{80,64},{96,112},{112,96},{1... | collective-permute-start | bytes 1769480 | tf_op jit(solution)/shard_map/ppermute | solution.py:252
  191.6 6.3 %collective-permute-start.3 = (f32[128,1152]{1,0:T(8,128)S(1)}, f32[128,1152]{1,0:T(8,128)S(1)}, u32[]{:S(2)}, u32[]{:S(2)}) collective-permute-start(f32[128,1152]{1,0:T(8,128)S(1)} %bitcast.26), channel_id=1, source_target_pairs={{0,16},{16,0},{32,48},{48,32},{64,80},{80,64},{96,112},{112,96},{1... | collective-permute-start | bytes 1769480 | tf_op jit(solution)/shard_map/ppermute | solution.py:255
  207.1 17.2 %all-to-all-start.8 = ((f32[16,1,256]{2,1,0:T(1,128)}), f32[16,1,256]{2,1,0:T(1,128)S(1)}, u32[]{:S(2)}, u32[]{:S(2)}) async-start(f32[16,1,256]{2,1,0:T(1,128)} %get-tuple-element.29), calls=%async_computation.8 | async-start | bytes 32768 | tf_op jit(solution)/shard_map/all_to_all | solution.py:290
  212.9 11.4 %copy-start.2 = (bf16[256,896]{1,0:T(8,128)(2,1)S(1)}, bf16[256,896]{1,0:T(8,128)(2,1)}, u32[]{:S(2)}) copy-start(bf16[256,896]{1,0:T(8,128)(2,1)} %weight_ref.1) | copy-start | bytes 1376260

commit v5 on v4

--- a/solution.py
+++ b/solution.py
@@ -21,7 +21,7 @@
 MP = 32
 DP = 16
 HALF = RANK // 2
-PANEL = 32
+PANEL = 16
 OWN_ROWS = ROWS // MP
 OWN_COLS = COLS // DP
 SAME_CORE = [[c + 2 * i for i in range(MP // 2)] for c in range(2)]
@@ -77,6 +77,14 @@
         lax.rsqrt(jnp.sum(diagonal, axis=1, keepdims=True)),
         lax.rsqrt(jnp.sum(diagonal, axis=0, keepdims=True)),
     )
+
+
+def spread(row):
+    return jnp.broadcast_to(row, (8, HALF))
+
+
+def doubled(values):
+    return jnp.concatenate([values, values], axis=1)
 
 
 def write_inverse_factor(rest, out_ref, unscale):
@@ -99,26 +107,35 @@
         panel = jnp.where(inside, jnp.where(lane - start == place, 1.0, 0.0), panel)
         rows = [panel[8 * g : 8 * g + 8] for g in range(groups)]
         pivots = [None] * groups
-        for t in range(PANEL):
+        for t in range(0, PANEL, 2):
             at, row = divmod(t, 8)
-            column = own[t]
-            pivots[at] = jnp.where(short == row, column[at], pivots[at]) if row else column[at]
-            if t == PANEL - 1:
-                break
-            inverse = jnp.broadcast_to(1.0 / column[at][row : row + 1], (8, HALF))
-            factor = {g: column[g] * inverse for g in range(at, groups)}
-            factor[at] = jnp.where(short > row, factor[at], 0.0)
-            for later in range(t + 1, PANEL):
+            one, two = own[t], own[t + 1]
+            p = spread(one[at][row : row + 1])
+            r = spread(one[at][row + 1 : row + 2])
+            minor = p * spread(two[at][row + 1 : row + 2]) - r * r
+            over_p = 1.0 / p
+            over_q = p * (1.0 / minor)
+            ratio = r * over_p
+            pair = jnp.where(short == row, p, minor * over_p)
+            pivots[at] = jnp.where(short >= row, pair, pivots[at]) if row else pair
+            two = {g: two[g] - one[g] * ratio for g in range(at, groups)}
+            by_one = {g: one[g] * over_p for g in range(at, groups)}
+            by_two = {g: two[g] * over_q for g in range(at, groups)}
+            by_one[at] = jnp.where(short > row, by_one[at], 0.0)
+            by_two[at] = jnp.where(short > row + 1, by_two[at], 0.0)
+            for later in range(t + 2, PANEL):
                 its_group, its_row = divmod(later, 8)
-                pivot_row = jnp.broadcast_to(column[its_group][its_row : its_row + 1], (8, HALF))
+                from_one = spread(one[its_group][its_row : its_row + 1])
+                from_two = spread(two[its_group][its_row : its_row + 1])
                 for g in range(its_group, groups):
-                    own[later][g] = own[later][g] - factor[g] * pivot_row
-            pivot_row = rows[at][row : row + 1]
+                    own[later][g] = own[later][g] - by_one[g] * from_one - by_two[g] * from_two
+            first = rows[at][row : row + 1]
+            second = rows[at][row + 1 : row + 2] - doubled(ratio[:1]) * first
             for g in range(at, groups):
-                rows[g] = rows[g] - jnp.concatenate([factor[g]] * 2, axis=1) * pivot_row
+                rows[g] = rows[g] - doubled(by_one[g]) * first - doubled(by_two[g]) * second
         for g in range(groups):
             root = lax.rsqrt(pivots[g])
-            rows[g] = rows[g] * jnp.concatenate([root, root], axis=1)
+            rows[g] = rows[g] * doubled(root)
         done = jnp.concatenate(rows, axis=0)
         result = jnp.where(lane < start + PANEL, done, 0.0)
         out_ref[start : start + PANEL, :] = result if unscale is None else result * unscale
@@ -141,25 +158,30 @@
                 rest = rest[PANEL:] * kept - taken[at + PANEL :]
 
 
-def buffer_of(momentum_ref, gradient_ref):
-    return momentum_ref[...] + gradient_ref[...].astype(jnp.float32)
-
-
-def first_kernel(momentum_ref, gradient_ref, basis_ref, left_ref):
-    left_ref[...] = product(buffer_of(momentum_ref, gradient_ref), basis_ref[...])
-
-
-def sums_kernel(left_ref, momentum_ref, gradient_ref, out_ref):
+def first_kernel(momentum_ref, gradient_ref, basis_ref, buffer_ref, left_ref):
+    buffer = momentum_ref[...] + gradient_ref[...].astype(jnp.float32)
+    buffer_ref[...] = buffer
+    left_ref[...] = product(buffer, basis_ref[...])
+
+
+def sums_kernel(left_ref, buffer_ref, out_ref):
     left = left_ref[...]
     turned = left.T
-    out_ref[:, :OWN_COLS] = product(turned, buffer_of(momentum_ref, gradient_ref))
+    out_ref[:, :OWN_COLS] = product(turned, buffer_ref[...])
     out_ref[:, OWN_COLS:] = product(turned, left)
 
 
-def next_left_kernel(sums_ref, momentum_ref, gradient_ref, out_ref):
-    scale, _ = scales_of(sums_ref[:, OWN_COLS:])
-    buffer = buffer_of(momentum_ref, gradient_ref)
-    out_ref[...] = outer_rows(buffer, sums_ref[:, :OWN_COLS] * scale)
+def next_left_kernel(core_ref, half_ref, buffer_ref, other_ref, out_ref):
+    core = core_ref[0]
+    row = lax.broadcasted_iota(jnp.int32, (HALF, RANK), 0)
+    column = lax.broadcasted_iota(jnp.int32, (HALF, RANK), 1)
+    diagonal = jnp.where(column == row + core * HALF, half_ref[:, OWN_COLS:], 0.0)
+    scale = lax.rsqrt(jnp.sum(diagonal, axis=1, keepdims=True))
+    right = half_ref[:, :OWN_COLS] * scale
+    mine = pl.ds(pl.multiple_of(core * OWN_ROWS, OWN_ROWS), OWN_ROWS)
+    its = pl.ds(pl.multiple_of((1 - core) * OWN_ROWS, OWN_ROWS), OWN_ROWS)
+    out_ref[mine, :] = outer_rows(buffer_ref[...], right)
+    out_ref[its, :] = outer_rows(other_ref[...], right)
 
 
 def middle_kernel(sums_ref, inverse_ref, squares_ref):
@@ -171,13 +193,20 @@
 
 
 def second_left_kernel(
-    raw_ref, inverse_ref, squares_ref, momentum_ref, gradient_ref, left_ref, out_ref
+    core_ref, raw_ref, raw_other_ref, inverse_ref, squares_ref, buffer_ref, other_ref, left_ref, out_ref
 ):
+    first_core = core_ref[0] == 0
+    pick = lambda a, b: jnp.where(first_core, a, b)
+    mine, its = raw_ref[...], raw_other_ref[...]
+    raw = jnp.concatenate([pick(mine, its), pick(its, mine)], axis=1)
     squares = jnp.sum(squares_ref[...], axis=0, keepdims=True)
-    left = outer_rows(raw_ref[...], inverse_ref[...]) / (jnp.sqrt(squares) + norm_eps)
-    left_ref[...] = left
-    turned = left.T
-    out_ref[:, :OWN_COLS] = product(turned, buffer_of(momentum_ref, gradient_ref))
+    left = outer_rows(raw, inverse_ref[...]) / (jnp.sqrt(squares) + norm_eps)
+    left_ref[...] = pick(left[:OWN_ROWS], left[OWN_ROWS:])
+    turned = pick(left[:, :HALF], left[:, HALF:]).T
+    early, late = turned[:, :OWN_ROWS], turned[:, OWN_ROWS:]
+    out_ref[:, :OWN_COLS] = product(pick(early, late), buffer_ref[...]) + product(
+        pick(late, early), other_ref[...]
+    )
     out_ref[:, OWN_COLS:] = product(turned, left)
 
 
@@ -191,13 +220,10 @@
     squares_ref[...] = jnp.broadcast_to(squares[None], (DP, 1, RANK))
 
 
-def momentum_kernel(
-    raw_ref, inverse_ref, right_ref, momentum_ref, gradient_ref, left_ref, out_ref
-):
+def momentum_kernel(raw_ref, inverse_ref, right_ref, buffer_ref, left_ref, out_ref):
     left = outer_rows(raw_ref[...], inverse_ref[...])
     left_ref[...] = left
-    buffer = buffer_of(momentum_ref, gradient_ref)
-    out_ref[...] = buffer - (1.0 - retain) * product_of_parts(left, right_ref[...])
+    out_ref[...] = buffer_ref[...] - (1.0 - retain) * product_of_parts(left, right_ref[...])
 
 
 def weight_kernel(
@@ -244,53 +270,72 @@
     return lax.all_to_all(copies, axis, 0, 0, axis_index_groups=groups, tiled=True)
 
 
-def sum_over_mp(values, first_core, own_start, other_start):
-    width = values.shape[1]
-    zero = own_start * 0
-    own = lax.dynamic_slice(values, (own_start, zero), (HALF, width))
-    other = lax.dynamic_slice(values, (other_start, zero), (HALF, width))
-    own = own + lax.ppermute(other, "mp", CORE_PAIRS)
-    own = scatter_sum(own, "mp", MP // 2, SAME_CORE)
-    own = gather(own, "mp", MP // 2, SAME_CORE).reshape(HALF, width)
-    other = lax.ppermute(own, "mp", CORE_PAIRS)
+def sum_over_chips(values):
+    own = scatter_sum(values, "mp", MP // 2, SAME_CORE)
+    return gather(own, "mp", MP // 2, SAME_CORE).reshape(values.shape)
+
+
+def with_other_core(values):
+    return lax.ppermute(values, "mp", CORE_PAIRS)
+
+
+def joined(half, first_core):
+    other = with_other_core(half)
     return jnp.concatenate(
-        [jnp.where(first_core, own, other), jnp.where(first_core, other, own)], axis=0
+        [jnp.where(first_core, half, other), jnp.where(first_core, other, half)], axis=0
     )
 
 
 def body(momentum, gradient, weight, right_basis):
     square = (RANK, RANK)
     wide = (RANK, OWN_COLS)
-    both = (RANK, OWN_COLS + RANK)
+    width = OWN_COLS + RANK
     block = (OWN_ROWS, OWN_COLS)
-    own_rows = OWN_ROWS // DP
     anywhere = pl.BlockSpec(memory_space=pl.ANY)
+    scalar = pl.BlockSpec(memory_space=pltpu.SMEM)
+    vector = pl.BlockSpec(memory_space=pltpu.VMEM)
 
     core = (lax.axis_index("mp") % 2).astype(jnp.uint32)
-    *halves, right_basis = lax.optimization_barrier(
-        (core == 0, core * HALF, HALF - core * HALF, right_basis)
-    )
-
-    left = call(first_kernel, 1, (OWN_ROWS, RANK), vmem=60)(momentum, gradient, right_basis)
+    first_core, own_start, other_start, zero, core, right_basis = lax.optimization_barrier(
+        (
+            core == 0,
+            core * HALF,
+            HALF - core * HALF,
+            core * 0,
+            core.astype(jnp.int32).reshape(1),
+            right_basis,
+        )
+    )
+
+    buffer, left = call(first_kernel, 1, block, (OWN_ROWS, RANK), vmem=60)(
+        momentum, gradient, right_basis
+    )
+    buffer_other = with_other_core(buffer)
     left = gather(scatter_sum(left, "dp", DP), "dp", DP).reshape(OWN_ROWS, RANK)
-    sums = sum_over_mp(call(sums_kernel, 1.3, both)(left, momentum, gradient), *halves)
-    left = call(next_left_kernel, 1, square)(sums, momentum, gradient)
-    left = scatter_sum(left, "dp", DP)
-    inverse, own_squares = call(middle_kernel, 8, square, (1, RANK))(sums)
-    sent = jnp.concatenate([left, own_squares], axis=0).reshape(own_rows + 1, 2, HALF)
-    came = gather(sent, "dp", DP)
-    raw = came[:, :own_rows].reshape(OWN_ROWS, RANK)
-    squares = came[:, own_rows].reshape(DP, RANK)
-
-    left, sums = call(second_left_kernel, 1.6, square, both)(
-        raw, inverse, squares, momentum, gradient
-    )
-    sums = sum_over_mp(sums, *halves)
+    sums = call(sums_kernel, 1.3, (RANK, width))(left, buffer)
+    half = lax.dynamic_slice(sums, (own_start, zero), (HALF, width))
+    other = lax.dynamic_slice(sums, (other_start, zero), (HALF, width))
+    half = scatter_sum(half + with_other_core(other), "mp", MP // 2, SAME_CORE)
+    half, buffer_other = lax.optimization_barrier((half, buffer_other))
+    half = gather(half, "mp", MP // 2, SAME_CORE).reshape(HALF, width)
+    raw = call(
+        next_left_kernel, 1, (2 * OWN_ROWS, HALF), in_specs=[scalar, vector, vector, vector]
+    )(core, half, buffer, buffer_other)
+    raw = scatter_sum(raw, "dp", DP)
+    inverse, own_squares = call(middle_kernel, 8, square, (1, RANK))(joined(half, first_core))
+    shared = 2 * OWN_ROWS // DP
+    sent = [raw.reshape(shared // 2, 2, HALF), own_squares.reshape(1, 2, HALF)]
+    came = gather(jnp.concatenate(sent, axis=0), "dp", DP)
+    raw = came[:, : shared // 2].reshape(2 * OWN_ROWS, HALF)
+    squares = came[:, shared // 2].reshape(DP, RANK)
+
+    left, half = call(
+        second_left_kernel, 1.6, square, (HALF, width), in_specs=[scalar] + [vector] * 6
+    )(core, raw, with_other_core(raw), inverse, squares, buffer, buffer_other)
+    sums = joined(sum_over_chips(half), first_core)
     inverse, right, own_squares = call(last_right_kernel, 8, square, wide, (DP, 1, RANK))(sums)
     squares = lax.all_to_all(own_squares, "dp", 0, 0, tiled=True)
-    left, new_momentum = call(momentum_kernel, 1, square, block)(
-        left, inverse, right, momentum, gradient
-    )
+    left, new_momentum = call(momentum_kernel, 1, square, block)(left, inverse, right, buffer)
     basis, new_weight = call(
         weight_kernel,
         1,

time: 227 us -> 225 us (level)
  waiting for transfers between devices: 21.1 us -> 18.3 us
    ppermute x4 -> x5, waiting for transfers between devices: 6.43 us -> 2.55 us  [with_other_core(): return lax.ppermute(values, 'mp', CORE_PAIRS)]
    ppermute x4 -> x5, starting transfers between devices: 25.6 us -> 27.2 us  [with_other_core(): return lax.ppermute(values, 'mp', CORE_PAIRS)]
  transfers between devices with their start and end apart: 6 -> 7, of which waited for: 6 -> 4; matrix products, arithmetic and copies ran while one was open for 0% -> 0% of each run, Pallas kernels for 5% -> 5%
where the time goes in v5:
time: 225 us; the launch traced here: 224 us
  blocking collectives  136 us (60%)
  starting transfers between devices  38.4 us (17%)
  Pallas kernels  29.7 us (13%)
  waiting for transfers between devices  18.3 us (8%)
    all_to_all x4, blocking collectives, gather(): lax.all_to_all(copies, axis, 0, 0, axis_index_groups=groups, tiled=True)  75.1 us
    all_to_all x3, blocking collectives, scatter_sum(): lax.all_to_all(values, axis, 0, 0, axis_index_groups=groups, tiled=True)  61.1 us
    ppermute x5, starting transfers between devices, with_other_core(): return lax.ppermute(values, 'mp', CORE_PAIRS)  27.2 us
    all_to_all x1, waiting for transfers between devices, body(): squares = lax.all_to_all(own_squares, 'dp', 0, 0, tiled=True)  9.15 us
    pallas_call x1, Pallas kernels, body(): call(last_right_kernel, 8, square, wide, (DP, 1, RANK))(sums)  8.23 us
    pallas_call x1, Pallas kernels, body(): call(middle_kernel, 8, square, (1, RANK))(joined(half, first_core))  7.6 us
    all_to_all x1, waiting for transfers between devices, scatter_sum(): lax.all_to_all(values, axis, 0, 0, axis_index_groups=groups, tiled=True)  6.65 us
    all_to_all x1, starting transfers between devices, body(): squares = lax.all_to_all(own_squares, 'dp', 0, 0, tiled=True)  5.81 us
  transfers between devices with their start and end apart: 7, of which 4 were waited for; matrix products, arithmetic and copies ran while one was open for 0% of the time, Pallas kernels for 5%

profile of v5, /device:TPU:1, one launch (start us, length us, event | category | flops | bytes accessed | tf_op | source)
XLA Modules:
  0.0 224.5 jit_solution(11380832202625166789)
XLA Ops:
  0.6 3.4 %shard_map.67 = (f32[256,896]{1,0:T(8,128)}, f32[256,256]{1,0:T(8,128)}) custom-call(f32[256,896]{1,0:T(8,128)} %momentum_ref.1, bf16[256,896]{1,0:T(8,128)(2,1)} %gradient_ref.1, f32[896,256]{1,0:T(8,128)} %basis_ref), custom_call_target="tpu_custom_call" | custom-call | flops 704643072 | bytes 917504 | tf_op jit(solution)/shard_map/pallas_call | solution.py:310
  4.1 29.0 %all_to_all.61 = f32[16,16,256]{2,1,0:T(8,128)S(1)} all-to-all(f32[16,16,256]{2,1,0:T(8,128)} %bitcast.30), channel_id=1, replica_groups=mesh['mp'=32,'dp'=16] {'dp'}, dimensions={0} | all-to-all | bytes 524288 | tf_op jit(solution)/shard_map/all_to_all | solution.py:264
  33.1 23.8 %all_to_all.62 = f32[16,16,256]{2,1,0:T(8,128)S(1)} all-to-all(f32[16,16,256]{2,1,0:T(8,128)S(1)} %broadcast_in_dim.8), channel_id=1, replica_groups=mesh['mp'=32,'dp'=16] {'dp'}, dimensions={0} | all-to-all | bytes 524288 | tf_op jit(solution)/shard_map/all_to_all | solution.py:270
  58.3 8.3 %collective-permute-start = (f32[128,1152]{1,0:T(8,128)S(1)}, f32[128,1152]{1,0:T(8,128)S(1)}, u32[]{:S(2)}, u32[]{:S(2)}) collective-permute-start(f32[128,1152]{1,0:T(8,128)S(1)} %constant_dynamic-slice_fusion), channel_id=1, source_target_pairs={{0,16},{16,0},{32,48},{48,32},{64,80},{80,64},{96,112},{112,96},{1... | collective-permute-start | bytes 1769480 | tf_op jit(solution)/shard_map/ppermute | solution.py:279
  66.5 1.9 collective-permute-start.1
  68.6 17.8 %all_to_all.63 = f32[16,8,1152]{2,1,0:T(8,128)S(1)} all-to-all(f32[16,8,1152]{2,1,0:T(8,128)S(1)} %add_bitcast_fusion), channel_id=1, replica_groups={{0,32,64,96,128,160,192,224,256,288,320,352,384,416,448,480},{16,48,80,..., dimensions={0} | all-to-all | bytes 1179648 | tf_op jit(solution)/shard_map/all_to_all | solution.py:264
  86.5 13.8 %all_to_all.64 = f32[16,8,1152]{2,1,0:T(8,128)S(1)} all-to-all(f32[16,8,1152]{2,1,0:T(8,128)S(1)} %broadcast_in_dim.9), channel_id=1, replica_groups={{0,32,64,96,128,160,192,224,256,288,320,352,384,416,448,480},{16,48,80,..., dimensions={0} | all-to-all | bytes 1179648 | tf_op jit(solution)/shard_map/all_to_all | solution.py:270
  100.3 4.6 %collective-permute-start.2 = (f32[128,1152]{1,0:T(8,128)S(1)}, f32[128,1152]{1,0:T(8,128)S(1)}, u32[]{:S(2)}, u32[]{:S(2)}) collective-permute-start(f32[128,1152]{1,0:T(8,128)S(1)} %bitcast.21), channel_id=1, source_target_pairs={{0,16},{16,0},{32,48},{48,32},{64,80},{80,64},{96,112},{112,96},{1... | collective-permute-start | bytes 1769480 | tf_op jit(solution)/shard_map/ppermute | solution.py:279
  104.9 2.4 %shard_map.69 = f32[512,128]{1,0:T(8,128)} custom-call(s32[1]{0:T(128)} %bitcast.core_ref, f32[128,1152]{1,0:T(8,128)S(1)} %bitcast.22, f32[256,896]{1,0:T(8,128)S(1)} %copy-done, f32[256,896]{1,0:T(8,128)S(1)} %collective-permute-done.1.other_ref), custom_call_target="tpu_custom_call" | custom-call | flops 704643072 | bytes 917504 | tf_op jit(solution)/shard_map/pallas_call | solution.py:321
  107.3 5.4 %all-to-all-start.4 = ((f32[16,32,128]{2,1,0:T(8,128)}), f32[16,32,128]{2,1,0:T(8,128)S(1)}, u32[]{:S(2)}, u32[]{:S(2)}) async-start(f32[16,32,128]{2,1,0:T(8,128)} %bitcast.5), calls=%async_computation.4 | async-start | bytes 524288 | tf_op jit(solution)/shard_map/all_to_all | solution.py:264
  112.9 7.6 %shard_map.70 = (f32[256,256]{1,0:T(8,128)S(1)}, f32[1,256]{1,0:T(1,128)S(1)}) custom-call(f32[256,1152]{1,0:T(8,128)S(1)} %pad_maximum_fusion.sums_ref), custom_call_target="tpu_custom_call" | custom-call | flops 5637144576 | bytes 917504 | tf_op jit(solution)/shard_map/pallas_call | solution.py:325
  120.5 6.7 %all-to-all-done.4 = f32[16,32,128]{2,1,0:T(8,128)S(1)} async-done(((f32[16,32,128]{2,1,0:T(8,128)}), f32[16,32,128]{2,1,0:T(8,128)S(1)}, u32[]{:S(2)}, u32[]{:S(2)}) %all-to-all-start.4) | async-done | bytes 262176 | tf_op jit(solution)/shard_map/all_to_all | solution.py:264
  127.3 23.8 %all_to_all.65 = f32[16,17,2,128]{3,2,1,0:T(2,128)S(1)} all-to-all(f32[16,17,2,128]{3,2,1,0:T(2,128)S(1)} %broadcast_in_dim.10), channel_id=1, replica_groups=mesh['mp'=32,'dp'=16] {'dp'}, dimensions={0} | all-to-all | bytes 557056 | tf_op jit(solution)/shard_map/all_to_all | solution.py:270
  151.1 7.7 %collective-permute-start.3 = (f32[512,128]{1,0:T(8,128)S(1)}, f32[512,128]{1,0:T(8,128)S(1)}, u32[]{:S(2)}, u32[]{:S(2)}) collective-permute-start(f32[512,128]{1,0:T(8,128)S(1)} %bitcast.24), channel_id=1, source_target_pairs={{0,16},{16,0},{32,48},{48,32},{64,80},{80,64},{96,112},{112,96},{1... | collective-permute-start | bytes 786440 | tf_op jit(solution)/shard_map/ppermute | solution.py:279
  159.8 2.7 %shard_map.71 = (f32[256,256]{1,0:T(8,128)S(1)}, f32[128,1152]{1,0:T(8,128)S(1)}) custom-call(s32[1]{0:T(128)} %bitcast.core_ref, f32[512,128]{1,0:T(8,128)S(1)} %bitcast.25, f32[512,128]{1,0:T(8,128)S(1)} %collective-permute-done.3.raw_other_ref, f32[256,256]{1,0:T(8,128)S(1)} %get-tuple-element.33.inverse_ref, f32[16,256]{1,0:T(8,128)S(1)} %bitcast.27, ...), custom_call_target="tpu_custom_call" | custom-call | flops 1127428864 | bytes 917504 | tf_op jit(solution)/shard_map/pallas_call | solution.py:332
  162.5 14.3 %all_to_all.66 = f32[16,8,1152]{2,1,0:T(8,128)S(1)} all-to-all(f32[16,8,1152]{2,1,0:T(8,128)S(1)} %bitcast.23), channel_id=1, replica_groups={{0,32,64,96,128,160,192,224,256,288,320,352,384,416,448,480},{16,48,80,..., dimensions={0} | all-to-all | bytes 1179648 | tf_op jit(solution)/shard_map/all_to_all | solution.py:264
  176.9 13.7 %all_to_all.67 = f32[16,8,1152]{2,1,0:T(8,128)S(1)} all-to-all(f32[16,8,1152]{2,1,0:T(8,128)S(1)} %broadcast_in_dim.11), channel_id=1, replica_groups={{0,32,64,96,128,160,192,224,256,288,320,352,384,416,448,480},{16,48,80,..., dimensions={0} | all-to-all | bytes 1179648 | tf_op jit(solution)/shard_map/all_to_all | solution.py:270
  190.6 4.6 %collective-permute-start.4 = (f32[128,1152]{1,0:T(8,128)S(1)}, f32[128,1152]{1,0:T(8,128)S(1)}, u32[]{:S(2)}, u32[]{:S(2)}) collective-permute-start(f32[128,1152]{1,0:T(8,128)S(1)} %bitcast.29), channel_id=1, source_target_pairs={{0,16},{16,0},{32,48},{48,32},{64,80},{80,64},{96,112},{112,96},{1... | collective-permute-start | bytes 1769480 | tf_op jit(solution)/shard_map/ppermute | solution.py:279
  195.3 1.6 collective-permute-done.4
  197.1 8.2 %shard_map.72 = (f32[256,256]{1,0:T(8,128)S(1)}, f32[256,896]{1,0:T(8,128)S(1)}, f32[16,1,256]{2,1,0:T(1,128)}) custom-call(f32[256,1152]{1,0:T(8,128)S(1)} %pad_maximum_fusion.1.sums_ref), custom_call_target="tpu_custom_call" | custom-call | flops 5637144576 | bytes 917504 | tf_op jit(solution)/shard_map/pallas_call | solution.py:336
  205.3 5.8 %all-to-all-start.8 = ((f32[16,1,256]{2,1,0:T(1,128)}), f32[16,1,256]{2,1,0:T(1,128)S(1)}, u32[]{:S(2)}, u32[]{:S(2)}) async-start(f32[16,1,256]{2,1,0:T(1,128)} %get-tuple-element.39), calls=%async_computation.8 | async-start | bytes 32768 | tf_op jit(solution)/shard_map/all_to_all | solution.py:337
  211.1 2.2 shard_map.73
  213.3 9.1 %all-to-all-done.8.squares_ref = f32[16,1,256]{2,1,0:T(1,128)S(1)} async-done(((f32[16,1,256]{2,1,0:T(1,128)}), f32[16,1,256]{2,1,0:T(1,128)S(1)}, u32[]{:S(2)}, u32[]{:S(2)}) %all-to-all-start.8) | async-done | bytes 16416 | tf_op jit(solution)/shard_map/all_to_all | solution.py:337
  222.5 1.8 shard_map.74
  (27 shorter events, 3.0 us)
Async XLA Ops:
  4.1 52.9 %copy-start = (f32[256,896]{1,0:T(8,128)S(1)}, f32[256,896]{1,0:T(8,128)}, u32[]{:S(2)}) copy-start(f32[256,896]{1,0:T(8,128)} %get-tuple-element.26.buffer_ref) | copy-start | bytes 2752516
  58.3 10.2 %collective-permute-start = (f32[128,1152]{1,0:T(8,128)S(1)}, f32[128,1152]{1,0:T(8,128)S(1)}, u32[]{:S(2)}, u32[]{:S(2)}) collective-permute-start(f32[128,1152]{1,0:T(8,128)S(1)} %constant_dynamic-slice_fusion), channel_id=1, source_target_pairs={{0,16},{16,0},{32,48},{48,32},{64,80},{80,64},{96,112},{112,96},{1... | collective-permute-start | bytes 1769480 | tf_op jit(solution)/shard_map/ppermute | solution.py:279
  66.5 19.9 %collective-permute-start.1 = (f32[256,896]{1,0:T(8,128)S(1)}, f32[256,896]{1,0:T(8,128)S(1)}, u32[]{:S(2)}, u32[]{:S(2)}) collective-permute-start(f32[256,896]{1,0:T(8,128)S(1)} %copy-done), channel_id=1, source_target_pairs={{0,16},{16,0},{32,48},{48,32},{64,80},{80,64},{96,112},{112,96},{1... | collective-permute-start | bytes 2752520 | tf_op jit(solution)/shard_map/ppermute | solution.py:279
  100.3 12.5 %collective-permute-start.2 = (f32[128,1152]{1,0:T(8,128)S(1)}, f32[128,1152]{1,0:T(8,128)S(1)}, u32[]{:S(2)}, u32[]{:S(2)}) collective-permute-start(f32[128,1152]{1,0:T(8,128)S(1)} %bitcast.21), channel_id=1, source_target_pairs={{0,16},{16,0},{32,48},{48,32},{64,80},{80,64},{96,112},{112,96},{1... | collective-permute-start | bytes 1769480 | tf_op jit(solution)/shard_map/ppermute | solution.py:279
  107.3 19.9 %all-to-all-start.4 = ((f32[16,32,128]{2,1,0:T(8,128)}), f32[16,32,128]{2,1,0:T(8,128)S(1)}, u32[]{:S(2)}, u32[]{:S(2)}) async-start(f32[16,32,128]{2,1,0:T(8,128)} %bitcast.5), calls=%async_computation.4 | async-start | bytes 524288 | tf_op jit(solution)/shard_map/all_to_all | solution.py:264
  151.1 8.7 %collective-permute-start.3 = (f32[512,128]{1,0:T(8,128)S(1)}, f32[512,128]{1,0:T(8,128)S(1)}, u32[]{:S(2)}, u32[]{:S(2)}) collective-permute-start(f32[512,128]{1,0:T(8,128)S(1)} %bitcast.24), channel_id=1, source_target_pairs={{0,16},{16,0},{32,48},{48,32},{64,80},{80,64},{96,112},{112,96},{1... | collective-permute-start | bytes 786440 | tf_op jit(solution)/shard_map/ppermute | solution.py:279
  190.6 6.3 %collective-permute-start.4 = (f32[128,1152]{1,0:T(8,128)S(1)}, f32[128,1152]{1,0:T(8,128)S(1)}, u32[]{:S(2)}, u32[]{:S(2)}) collective-permute-start(f32[128,1152]{1,0:T(8,128)S(1)} %bitcast.29), channel_id=1, source_target_pairs={{0,16},{16,0},{32,48},{48,32},{64,80},{80,64},{96,112},{112,96},{1... | collective-permute-start | bytes 1769480 | tf_op jit(solution)/shard_map/ppermute | solution.py:279
  205.3 17.2 %all-to-all-start.8 = ((f32[16,1,256]{2,1,0:T(1,128)}), f32[16,1,256]{2,1,0:T(1,128)S(1)}, u32[]{:S(2)}, u32[]{:S(2)}) async-start(f32[16,1,256]{2,1,0:T(1,128)} %get-tuple-element.39), calls=%async_computation.8 | async-start | bytes 32768 | tf_op jit(solution)/shard_map/all_to_all | solution.py:337
  211.1 11.4 %copy-start.1 = (bf16[256,896]{1,0:T(8,128)(2,1)S(1)}, bf16[256,896]{1,0:T(8,128)(2,1)}, u32[]{:S(2)}) copy-start(bf16[256,896]{1,0:T(8,128)(2,1)} %weight_ref.1) | copy-start | bytes 1376260

commit v6 on v5

--- a/solution.py
+++ b/solution.py
@@ -56,6 +56,17 @@
     other_high, other_low = two_parts(second)
     dot = lambda a, b: jnp.dot(a, b, preferred_element_type=jnp.float32)
     return dot(high, other_high) + (dot(high, other_low) + dot(low, other_high))
+
+
+def outer_rows_paired(first, second):
+    rows = second.shape[0]
+    a, b, c = three_parts(first)
+    high, middle, low = three_parts(second)
+    dot = lambda x, y: lax.dot_general(x, y, NEXT_TO, preferred_element_type=jnp.float32)
+    pair = jnp.concatenate([high, middle], axis=0)
+    by_a, by_b = dot(a, pair), dot(b, pair)
+    small = by_b[:, rows:] + dot(a, low) + dot(c, high)
+    return by_a[:, :rows] + (by_a[:, rows:] + by_b[:, :rows] + small)
 
 
 def on_diagonal():
@@ -180,14 +191,32 @@
     right = half_ref[:, :OWN_COLS] * scale
     mine = pl.ds(pl.multiple_of(core * OWN_ROWS, OWN_ROWS), OWN_ROWS)
     its = pl.ds(pl.multiple_of((1 - core) * OWN_ROWS, OWN_ROWS), OWN_ROWS)
-    out_ref[mine, :] = outer_rows(buffer_ref[...], right)
-    out_ref[its, :] = outer_rows(other_ref[...], right)
-
-
-def middle_kernel(sums_ref, inverse_ref, squares_ref):
+    out_ref[mine, :] = outer_rows_paired(buffer_ref[...], right)
+    out_ref[its, :] = outer_rows_paired(other_ref[...], right)
+
+
+def write_first_factor(sums_ref, inverse_ref):
     gram = sums_ref[:, OWN_COLS:]
     scale, scale_row = scales_of(gram)
     write_inverse_factor(gram * scale * scale_row, inverse_ref, None)
+
+
+def early_factor_kernel(core_ref, sums_ref, inverse_ref):
+    @pl.when(core_ref[0] == 1)
+    def _():
+        write_first_factor(sums_ref, inverse_ref)
+
+
+def middle_kernel(core_ref, sums_ref, early_ref, inverse_ref, squares_ref):
+    @pl.when(core_ref[0] == 0)
+    def _():
+        write_first_factor(sums_ref, inverse_ref)
+
+    @pl.when(core_ref[0] == 1)
+    def _():
+        inverse_ref[...] = early_ref[...]
+
+    scale, _ = scales_of(sums_ref[:, OWN_COLS:])
     right = product(inverse_ref[...], sums_ref[:, :OWN_COLS] * scale)
     squares_ref[...] = as_row(jnp.sum(right * right, axis=1, keepdims=True))
 
@@ -321,8 +350,13 @@
     raw = call(
         next_left_kernel, 1, (2 * OWN_ROWS, HALF), in_specs=[scalar, vector, vector, vector]
     )(core, half, buffer, buffer_other)
+    sums = joined(half, first_core)
+    early = call(early_factor_kernel, 1, square, in_specs=[scalar, vector])(core, sums)
+    raw, early = lax.optimization_barrier((raw, early))
     raw = scatter_sum(raw, "dp", DP)
-    inverse, own_squares = call(middle_kernel, 8, square, (1, RANK))(joined(half, first_core))
+    inverse, own_squares = call(
+        middle_kernel, 8, square, (1, RANK), in_specs=[scalar, vector, vector]
+    )(core, sums, early)
     shared = 2 * OWN_ROWS // DP
     sent = [raw.reshape(shared // 2, 2, HALF), own_squares.reshape(1, 2, HALF)]
     came = gather(jnp.concatenate(sent, axis=0), "dp", DP)

time: 225 us -> 222 us (0.987)
  waiting for transfers between devices: 18.3 us -> 25.5 us
  starting transfers between devices: 38.4 us -> 31.8 us
  blocking collectives: 136 us -> 132 us
    all_to_all x1, waiting for transfers between devices: 6.65 us -> 13.4 us  [scatter_sum(): lax.all_to_all(values, axis, 0, 0, axis_index_groups=groups, tiled=True)]
    ppermute x5, starting transfers between devices: 27.2 us -> 21.3 us  [with_other_core(): return lax.ppermute(values, 'mp', CORE_PAIRS)]
    all_to_all x4, blocking collectives: 75.1 us -> 70.3 us  [gather(): lax.all_to_all(copies, axis, 0, 0, axis_index_groups=groups, tiled=True)]
    pallas_call x1 -> x2, Pallas kernels: 7.6 us -> 8.05 us  [the longest x1 6.58 us: body(): call(early_factor_kernel, 1, square, in_specs=[scalar, vector])(core, sums)]
  transfers between devices with their start and end apart: 7 -> 7, of which waited for: 4 -> 4; matrix products, arithmetic and copies ran while one was open for 0% -> 0% of each run, Pallas kernels for 5% -> 3%
where the time goes in v6:
time: 222 us
  blocking collectives  132 us (59%)
  starting transfers between devices  31.8 us (14%)
  Pallas kernels  29.8 us (13%)
  waiting for transfers between devices  25.5 us (11%)
    all_to_all x4, blocking collectives, gather(): lax.all_to_all(copies, axis, 0, 0, axis_index_groups=groups, tiled=True)  70.3 us
    all_to_all x3, blocking collectives, scatter_sum(): lax.all_to_all(values, axis, 0, 0, axis_index_groups=groups, tiled=True)  61.3 us
    ppermute x5, starting transfers between devices, with_other_core(): return lax.ppermute(values, 'mp', CORE_PAIRS)  21.3 us
    all_to_all x1, waiting for transfers between devices, scatter_sum(): lax.all_to_all(values, axis, 0, 0, axis_index_groups=groups, tiled=True)  13.4 us
    all_to_all x1, waiting for transfers between devices, body(): squares = lax.all_to_all(own_squares, 'dp', 0, 0, tiled=True)  9.15 us
    pallas_call x1, Pallas kernels, body(): call(last_right_kernel, 8, square, wide, (DP, 1, RANK))(sums)  8.23 us
    pallas_call x1, Pallas kernels, body(): call(early_factor_kernel, 1, square, in_specs=[scalar, vector])(core, sums)  6.58 us
    all_to_all x1, starting transfers between devices, scatter_sum(): lax.all_to_all(values, axis, 0, 0, axis_index_groups=groups, tiled=True)  5.47 us
  transfers between devices with their start and end apart: 7, of which 4 were waited for; matrix products, arithmetic and copies ran while one was open for 0% of the time, Pallas kernels for 3%

profile of v6, /device:TPU:1, one launch (start us, length us, event | category | flops | bytes accessed | tf_op | source)
XLA Modules:
  0.0 221.5 jit_solution(2796541364795290930)
XLA Ops:
  0.6 3.4 %shard_map.67 = (f32[256,896]{1,0:T(8,128)}, f32[256,256]{1,0:T(8,128)}) custom-call(f32[256,896]{1,0:T(8,128)} %momentum_ref.1, bf16[256,896]{1,0:T(8,128)(2,1)} %gradient_ref.1, f32[896,256]{1,0:T(8,128)} %basis_ref), custom_call_target="tpu_custom_call" | custom-call | flops 704643072 | bytes 917504 | tf_op jit(solution)/shard_map/pallas_call | solution.py:339
  4.1 29.0 %all_to_all.61 = f32[16,16,256]{2,1,0:T(8,128)S(1)} all-to-all(f32[16,16,256]{2,1,0:T(8,128)} %bitcast.30), channel_id=1, replica_groups=mesh['mp'=32,'dp'=16] {'dp'}, dimensions={0} | all-to-all | bytes 524288 | tf_op jit(solution)/shard_map/all_to_all | solution.py:293
  33.1 23.8 %all_to_all.62 = f32[16,16,256]{2,1,0:T(8,128)S(1)} all-to-all(f32[16,16,256]{2,1,0:T(8,128)S(1)} %broadcast_in_dim.8), channel_id=1, replica_groups=mesh['mp'=32,'dp'=16] {'dp'}, dimensions={0} | all-to-all | bytes 524288 | tf_op jit(solution)/shard_map/all_to_all | solution.py:299
  58.3 8.3 %collective-permute-start = (f32[128,1152]{1,0:T(8,128)S(1)}, f32[128,1152]{1,0:T(8,128)S(1)}, u32[]{:S(2)}, u32[]{:S(2)}) collective-permute-start(f32[128,1152]{1,0:T(8,128)S(1)} %constant_dynamic-slice_fusion), channel_id=1, source_target_pairs={{0,16},{16,0},{32,48},{48,32},{64,80},{80,64},{96,112},{112,96},{1... | collective-permute-start | bytes 1769480 | tf_op jit(solution)/shard_map/ppermute | solution.py:308
  66.5 1.9 collective-permute-start.1
  68.6 17.8 %all_to_all.63 = f32[16,8,1152]{2,1,0:T(8,128)S(1)} all-to-all(f32[16,8,1152]{2,1,0:T(8,128)S(1)} %add_bitcast_fusion), channel_id=1, replica_groups={{0,32,64,96,128,160,192,224,256,288,320,352,384,416,448,480},{16,48,80,..., dimensions={0} | all-to-all | bytes 1179648 | tf_op jit(solution)/shard_map/all_to_all | solution.py:293
  86.5 13.8 %all_to_all.64 = f32[16,8,1152]{2,1,0:T(8,128)S(1)} all-to-all(f32[16,8,1152]{2,1,0:T(8,128)S(1)} %broadcast_in_dim.9), channel_id=1, replica_groups={{0,32,64,96,128,160,192,224,256,288,320,352,384,416,448,480},{16,48,80,..., dimensions={0} | all-to-all | bytes 1179648 | tf_op jit(solution)/shard_map/all_to_all | solution.py:299
  100.3 4.6 %collective-permute-start.2 = (f32[128,1152]{1,0:T(8,128)S(1)}, f32[128,1152]{1,0:T(8,128)S(1)}, u32[]{:S(2)}, u32[]{:S(2)}) collective-permute-start(f32[128,1152]{1,0:T(8,128)S(1)} %bitcast.21), channel_id=1, source_target_pairs={{0,16},{16,0},{32,48},{48,32},{64,80},{80,64},{96,112},{112,96},{1... | collective-permute-start | bytes 1769480 | tf_op jit(solution)/shard_map/ppermute | solution.py:308
  104.9 2.1 shard_map.69
  107.1 6.6 %shard_map.70.early_ref = f32[256,256]{1,0:T(8,128)S(1)} custom-call(s32[1]{0:T(128)} %bitcast.core_ref, f32[256,1152]{1,0:T(8,128)S(1)} %pad_maximum_fusion.sums_ref), custom_call_target="tpu_custom_call" | custom-call | flops 704643072 | bytes 917504 | tf_op jit(solution)/shard_map/pallas_call | solution.py:354
  113.7 5.5 %all-to-all-start.4 = ((f32[16,32,128]{2,1,0:T(8,128)}), f32[16,32,128]{2,1,0:T(8,128)}, u32[]{:S(2)}, u32[]{:S(2)}) async-start(f32[16,32,128]{2,1,0:T(8,128)} %bitcast.5), calls=%async_computation.4 | async-start | bytes 524288 | tf_op jit(solution)/shard_map/all_to_all | solution.py:293
  120.7 13.4 %all-to-all-done.4 = f32[16,32,128]{2,1,0:T(8,128)} async-done(((f32[16,32,128]{2,1,0:T(8,128)}), f32[16,32,128]{2,1,0:T(8,128)}, u32[]{:S(2)}, u32[]{:S(2)}) %all-to-all-start.4) | async-done | bytes 262176 | tf_op jit(solution)/shard_map/all_to_all | solution.py:293
  135.2 18.8 %all_to_all.65 = f32[16,17,2,128]{3,2,1,0:T(2,128)S(1)} all-to-all(f32[16,17,2,128]{3,2,1,0:T(2,128)S(1)} %broadcast_in_dim.10), channel_id=1, replica_groups=mesh['mp'=32,'dp'=16] {'dp'}, dimensions={0} | all-to-all | bytes 557056 | tf_op jit(solution)/shard_map/all_to_all | solution.py:299
  154.1 1.9 collective-permute-start.3
  156.0 1.5 collective-permute-done.3.raw_other_ref
  157.5 2.7 %shard_map.72 = (f32[256,256]{1,0:T(8,128)S(1)}, f32[128,1152]{1,0:T(8,128)S(1)}) custom-call(s32[1]{0:T(128)} %bitcast.core_ref, f32[512,128]{1,0:T(8,128)S(1)} %bitcast.25, f32[512,128]{1,0:T(8,128)S(1)} %collective-permute-done.3.raw_other_ref, f32[256,256]{1,0:T(8,128)S(1)} %get-tuple-element.37.inverse_ref, f32[16,256]{1,0:T(8,128)S(1)} %bitcast.27, ...), custom_call_target="tpu_custom_call" | custom-call | flops 1127428864 | bytes 917504 | tf_op jit(solution)/shard_map/pallas_call | solution.py:366
  160.2 14.5 %all_to_all.66 = f32[16,8,1152]{2,1,0:T(8,128)S(1)} all-to-all(f32[16,8,1152]{2,1,0:T(8,128)S(1)} %bitcast.23), channel_id=1, replica_groups={{0,32,64,96,128,160,192,224,256,288,320,352,384,416,448,480},{16,48,80,..., dimensions={0} | all-to-all | bytes 1179648 | tf_op jit(solution)/shard_map/all_to_all | solution.py:293
  174.8 13.9 %all_to_all.67 = f32[16,8,1152]{2,1,0:T(8,128)S(1)} all-to-all(f32[16,8,1152]{2,1,0:T(8,128)S(1)} %broadcast_in_dim.11), channel_id=1, replica_groups={{0,32,64,96,128,160,192,224,256,288,320,352,384,416,448,480},{16,48,80,..., dimensions={0} | all-to-all | bytes 1179648 | tf_op jit(solution)/shard_map/all_to_all | solution.py:299
  188.7 4.5 %collective-permute-start.4 = (f32[128,1152]{1,0:T(8,128)S(1)}, f32[128,1152]{1,0:T(8,128)S(1)}, u32[]{:S(2)}, u32[]{:S(2)}) collective-permute-start(f32[128,1152]{1,0:T(8,128)S(1)} %bitcast.29), channel_id=1, source_target_pairs={{0,16},{16,0},{32,48},{48,32},{64,80},{80,64},{96,112},{112,96},{1... | collective-permute-start | bytes 1769480 | tf_op jit(solution)/shard_map/ppermute | solution.py:308
  194.8 8.2 %shard_map.73 = (f32[256,256]{1,0:T(8,128)S(1)}, f32[256,896]{1,0:T(8,128)S(1)}, f32[16,1,256]{2,1,0:T(1,128)}) custom-call(f32[256,1152]{1,0:T(8,128)S(1)} %pad_maximum_fusion.1.sums_ref), custom_call_target="tpu_custom_call" | custom-call | flops 5637144576 | bytes 917504 | tf_op jit(solution)/shard_map/pallas_call | solution.py:370
  203.0 5.1 %all-to-all-start.8 = ((f32[16,1,256]{2,1,0:T(1,128)}), f32[16,1,256]{2,1,0:T(1,128)S(1)}, u32[]{:S(2)}, u32[]{:S(2)}) async-start(f32[16,1,256]{2,1,0:T(1,128)} %get-tuple-element.43), calls=%async_computation.8 | async-start | bytes 32768 | tf_op jit(solution)/shard_map/all_to_all | solution.py:371
  208.1 2.2 %shard_map.74 = (f32[256,256]{1,0:T(8,128)S(1)}, f32[256,896]{1,0:T(8,128)}) custom-call(f32[256,256]{1,0:T(8,128)S(1)} %get-tuple-element.38.raw_ref, f32[256,256]{1,0:T(8,128)S(1)} %get-tuple-element.40.inverse_ref, f32[256,896]{1,0:T(8,128)S(1)} %get-tuple-element.41.right_ref, f32[256,896]{1,0:T(8,128)S(1)} %copy-done), custom_call_target="tpu_custom_call" | custom-call | flops 704643072 | bytes 917504 | tf_op jit(solution)/shard_map/pallas_call | solution.py:372
  210.3 9.1 %all-to-all-done.8.squares_ref = f32[16,1,256]{2,1,0:T(1,128)S(1)} async-done(((f32[16,1,256]{2,1,0:T(1,128)}), f32[16,1,256]{2,1,0:T(1,128)S(1)}, u32[]{:S(2)}, u32[]{:S(2)}) %all-to-all-start.8) | async-done | bytes 16416 | tf_op jit(solution)/shard_map/all_to_all | solution.py:371
  219.5 1.8 shard_map.75
  (28 shorter events, 5.8 us)
Async XLA Ops:
  4.1 52.9 %copy-start = (f32[256,896]{1,0:T(8,128)S(1)}, f32[256,896]{1,0:T(8,128)}, u32[]{:S(2)}) copy-start(f32[256,896]{1,0:T(8,128)} %get-tuple-element.28.buffer_ref) | copy-start | bytes 2752516
  58.3 10.2 %collective-permute-start = (f32[128,1152]{1,0:T(8,128)S(1)}, f32[128,1152]{1,0:T(8,128)S(1)}, u32[]{:S(2)}, u32[]{:S(2)}) collective-permute-start(f32[128,1152]{1,0:T(8,128)S(1)} %constant_dynamic-slice_fusion), channel_id=1, source_target_pairs={{0,16},{16,0},{32,48},{48,32},{64,80},{80,64},{96,112},{112,96},{1... | collective-permute-start | bytes 1769480 | tf_op jit(solution)/shard_map/ppermute | solution.py:308
  66.5 19.9 %collective-permute-start.1 = (f32[256,896]{1,0:T(8,128)S(1)}, f32[256,896]{1,0:T(8,128)S(1)}, u32[]{:S(2)}, u32[]{:S(2)}) collective-permute-start(f32[256,896]{1,0:T(8,128)S(1)} %copy-done), channel_id=1, source_target_pairs={{0,16},{16,0},{32,48},{48,32},{64,80},{80,64},{96,112},{112,96},{1... | collective-permute-start | bytes 2752520 | tf_op jit(solution)/shard_map/ppermute | solution.py:308
  100.3 6.7 %collective-permute-start.2 = (f32[128,1152]{1,0:T(8,128)S(1)}, f32[128,1152]{1,0:T(8,128)S(1)}, u32[]{:S(2)}, u32[]{:S(2)}) collective-permute-start(f32[128,1152]{1,0:T(8,128)S(1)} %bitcast.21), channel_id=1, source_target_pairs={{0,16},{16,0},{32,48},{48,32},{64,80},{80,64},{96,112},{112,96},{1... | collective-permute-start | bytes 1769480 | tf_op jit(solution)/shard_map/ppermute | solution.py:308
  113.7 20.4 %all-to-all-start.4 = ((f32[16,32,128]{2,1,0:T(8,128)}), f32[16,32,128]{2,1,0:T(8,128)}, u32[]{:S(2)}, u32[]{:S(2)}) async-start(f32[16,32,128]{2,1,0:T(8,128)} %bitcast.5), calls=%async_computation.4 | async-start | bytes 524288 | tf_op jit(solution)/shard_map/all_to_all | solution.py:293
  154.1 3.4 %collective-permute-start.3 = (f32[512,128]{1,0:T(8,128)S(1)}, f32[512,128]{1,0:T(8,128)S(1)}, u32[]{:S(2)}, u32[]{:S(2)}) collective-permute-start(f32[512,128]{1,0:T(8,128)S(1)} %bitcast.24), channel_id=1, source_target_pairs={{0,16},{16,0},{32,48},{48,32},{64,80},{80,64},{96,112},{112,96},{1... | collective-permute-start | bytes 786440 | tf_op jit(solution)/shard_map/ppermute | solution.py:308
  188.7 5.9 %collective-permute-start.4 = (f32[128,1152]{1,0:T(8,128)S(1)}, f32[128,1152]{1,0:T(8,128)S(1)}, u32[]{:S(2)}, u32[]{:S(2)}) collective-permute-start(f32[128,1152]{1,0:T(8,128)S(1)} %bitcast.29), channel_id=1, source_target_pairs={{0,16},{16,0},{32,48},{48,32},{64,80},{80,64},{96,112},{112,96},{1... | collective-permute-start | bytes 1769480 | tf_op jit(solution)/shard_map/ppermute | solution.py:308
  203.0 16.5 %all-to-all-start.8 = ((f32[16,1,256]{2,1,0:T(1,128)}), f32[16,1,256]{2,1,0:T(1,128)S(1)}, u32[]{:S(2)}, u32[]{:S(2)}) async-start(f32[16,1,256]{2,1,0:T(1,128)} %get-tuple-element.43), calls=%async_computation.8 | async-start | bytes 32768 | tf_op jit(solution)/shard_map/all_to_all | solution.py:371
  208.1 11.4 %copy-start.1 = (bf16[256,896]{1,0:T(8,128)(2,1)S(1)}, bf16[256,896]{1,0:T(8,128)(2,1)}, u32[]{:S(2)}) copy-start(bf16[256,896]{1,0:T(8,128)(2,1)} %weight_ref.1) | copy-start | bytes 1376260

commit v7 on v6

--- a/solution.py
+++ b/solution.py
@@ -22,6 +22,7 @@
 DP = 16
 HALF = RANK // 2
 PANEL = 16
+PARTS = COLS // DP // HALF
 OWN_ROWS = ROWS // MP
 OWN_COLS = COLS // DP
 SAME_CORE = [[c + 2 * i for i in range(MP // 2)] for c in range(2)]
@@ -195,29 +196,39 @@
     out_ref[its, :] = outer_rows_paired(other_ref[...], right)
 
 
-def write_first_factor(sums_ref, inverse_ref):
-    gram = sums_ref[:, OWN_COLS:]
+def both_halves(core_ref, half_ref, other_ref):
+    first_core = core_ref[0] == 0
+    half, other = half_ref[...], other_ref[...]
+    return jnp.concatenate(
+        [jnp.where(first_core, half, other), jnp.where(first_core, other, half)], axis=0
+    )
+
+
+def write_first_factor(sums, inverse_ref):
+    gram = sums[:, OWN_COLS:]
     scale, scale_row = scales_of(gram)
     write_inverse_factor(gram * scale * scale_row, inverse_ref, None)
 
 
-def early_factor_kernel(core_ref, sums_ref, inverse_ref):
+def early_factor_kernel(core_ref, half_ref, other_ref, inverse_ref):
     @pl.when(core_ref[0] == 1)
     def _():
-        write_first_factor(sums_ref, inverse_ref)
-
-
-def middle_kernel(core_ref, sums_ref, early_ref, inverse_ref, squares_ref):
+        write_first_factor(both_halves(core_ref, half_ref, other_ref), inverse_ref)
+
+
+def middle_kernel(core_ref, half_ref, other_ref, early_ref, inverse_ref, squares_ref):
+    sums = both_halves(core_ref, half_ref, other_ref)
+
     @pl.when(core_ref[0] == 0)
     def _():
-        write_first_factor(sums_ref, inverse_ref)
+        write_first_factor(sums, inverse_ref)
 
     @pl.when(core_ref[0] == 1)
     def _():
         inverse_ref[...] = early_ref[...]
 
-    scale, _ = scales_of(sums_ref[:, OWN_COLS:])
-    right = product(inverse_ref[...], sums_ref[:, :OWN_COLS] * scale)
+    scale, _ = scales_of(sums[:, OWN_COLS:])
+    right = product(inverse_ref[...], sums[:, :OWN_COLS] * scale)
     squares_ref[...] = as_row(jnp.sum(right * right, axis=1, keepdims=True))
 
 
@@ -239,11 +250,12 @@
     out_ref[:, OWN_COLS:] = product(turned, left)
 
 
-def last_right_kernel(sums_ref, inverse_ref, right_ref, squares_ref):
-    gram = sums_ref[:, OWN_COLS:]
+def last_right_kernel(core_ref, half_ref, other_ref, inverse_ref, right_ref, squares_ref):
+    sums = both_halves(core_ref, half_ref, other_ref)
+    gram = sums[:, OWN_COLS:]
     scale, scale_row = scales_of(gram)
     write_inverse_factor(gram * scale * scale_row, inverse_ref, scale_row)
-    right = product(inverse_ref[...], sums_ref[:, :OWN_COLS])
+    right = product(inverse_ref[...], sums[:, :OWN_COLS])
     right_ref[...] = right
     squares = as_row(jnp.sum(right * right, axis=1, keepdims=True))
     squares_ref[...] = jnp.broadcast_to(squares[None], (DP, 1, RANK))
@@ -260,15 +272,18 @@
 ):
     squares = as_column(jnp.sum(squares_ref[...], axis=0))
     basis = right_ref[...] / (jnp.sqrt(squares) + norm_eps)
-    own_b[...] = basis.T
-    first = pltpu.make_async_copy(own_b, basis_out, done.at[0])
-    first.start()
+    copies = []
+    for j in range(PARTS):
+        at = pl.ds(j * HALF, HALF)
+        own_b[at, :] = basis[:, j * HALF : (j + 1) * HALF].T
+        copies.append(pltpu.make_async_copy(own_b.at[at, :], basis_out.at[at, :], done.at[j]))
+        copies[-1].start()
     update = product_of_parts(left_ref[...], basis)
     own_w[...] = (weight_ref[...].astype(jnp.float32) - step * update).astype(jnp.bfloat16)
-    second = pltpu.make_async_copy(own_w, weight_out, done.at[1])
-    second.start()
-    first.wait()
-    second.wait()
+    copies.append(pltpu.make_async_copy(own_w, weight_out, done.at[PARTS]))
+    copies[-1].start()
+    for copy in copies:
+        copy.wait()
 
 
 def call(kernel, products, *shapes, **options):
@@ -308,13 +323,6 @@
     return lax.ppermute(values, "mp", CORE_PAIRS)
 
 
-def joined(half, first_core):
-    other = with_other_core(half)
-    return jnp.concatenate(
-        [jnp.where(first_core, half, other), jnp.where(first_core, other, half)], axis=0
-    )
-
-
 def body(momentum, gradient, weight, right_basis):
     square = (RANK, RANK)
     wide = (RANK, OWN_COLS)
@@ -325,9 +333,8 @@
     vector = pl.BlockSpec(memory_space=pltpu.VMEM)
 
     core = (lax.axis_index("mp") % 2).astype(jnp.uint32)
-    first_core, own_start, other_start, zero, core, right_basis = lax.optimization_barrier(
+    own_start, other_start, zero, core, right_basis = lax.optimization_barrier(
         (
-            core == 0,
             core * HALF,
             HALF - core * HALF,
             core * 0,
@@ -350,13 +357,13 @@
     raw = call(
         next_left_kernel, 1, (2 * OWN_ROWS, HALF), in_specs=[scalar, vector, vector, vector]
     )(core, half, buffer, buffer_other)
-    sums = joined(half, first_core)
-    early = call(early_factor_kernel, 1, square, in_specs=[scalar, vector])(core, sums)
+    halves = (core, half, with_other_core(half))
+    early = call(early_factor_kernel, 1, square, in_specs=[scalar, vector, vector])(*halves)
     raw, early = lax.optimization_barrier((raw, early))
     raw = scatter_sum(raw, "dp", DP)
     inverse, own_squares = call(
-        middle_kernel, 8, square, (1, RANK), in_specs=[scalar, vector, vector]
-    )(core, sums, early)
+        middle_kernel, 8, square, (1, RANK), in_specs=[scalar] + [vector] * 3
+    )(*halves, early)
     shared = 2 * OWN_ROWS // DP
     sent = [raw.reshape(shared // 2, 2, HALF), own_squares.reshape(1, 2, HALF)]
     came = gather(jnp.concatenate(sent, axis=0), "dp", DP)
@@ -366,8 +373,15 @@
     left, half = call(
         second_left_kernel, 1.6, square, (HALF, width), in_specs=[scalar] + [vector] * 6
     )(core, raw, with_other_core(raw), inverse, squares, buffer, buffer_other)
-    sums = joined(sum_over_chips(half), first_core)
-    inverse, right, own_squares = call(last_right_kernel, 8, square, wide, (DP, 1, RANK))(sums)
+    half = sum_over_chips(half)
+    inverse, right, own_squares = call(
+        last_right_kernel,
+        8,
+        square,
+        wide,
+        (DP, 1, RANK),
+        in_specs=[scalar, vector, vector],
+    )(core, half, with_other_core(half))
     squares = lax.all_to_all(own_squares, "dp", 0, 0, tiled=True)
     left, new_momentum = call(momentum_kernel, 1, square, block)(left, inverse, right, buffer)
     basis, new_weight = call(
@@ -380,7 +394,7 @@
         scratch_shapes=[
             pltpu.VMEM((OWN_COLS, RANK), jnp.float32),
             pltpu.VMEM(block, jnp.bfloat16),
-            pltpu.SemaphoreType.DMA((2,)),
+            pltpu.SemaphoreType.DMA((PARTS + 1,)),
         ],
     )(left, right, squares, weight)
     return (new_weight, new_momentum, basis)

time: 222 us -> 222 us (level)
  no operation moved by 1% of the time
where the time goes in v7:
time: 222 us; the launch traced here: 221 us
  blocking collectives  132 us (59%)
  starting transfers between devices  31.7 us (14%)
  Pallas kernels  29.8 us (13%)
  waiting for transfers between devices  25.2 us (11%)
    all_to_all x4, blocking collectives, gather(): lax.all_to_all(copies, axis, 0, 0, axis_index_groups=groups, tiled=True)  70.7 us
    all_to_all x3, blocking collectives, scatter_sum(): lax.all_to_all(values, axis, 0, 0, axis_index_groups=groups, tiled=True)  61.3 us
    ppermute x5, starting transfers between devices, with_other_core(): return lax.ppermute(values, 'mp', CORE_PAIRS)  21.3 us
    all_to_all x1, waiting for transfers between devices, scatter_sum(): lax.all_to_all(values, axis, 0, 0, axis_index_groups=groups, tiled=True)  13.2 us
    all_to_all x1, waiting for transfers between devices, body(): squares = lax.all_to_all(own_squares, 'dp', 0, 0, tiled=True)  9.15 us
    pallas_call x1, Pallas kernels, body(): call(last_right_kernel, 8, square, wide, (DP, 1, RANK), in_specs=[scalar,...  8.26 us
    pallas_call x1, Pallas kernels, body(): call(early_factor_kernel, 1, square, in_specs=[scalar, vector, vector])  6.57 us
    all_to_all x1, starting transfers between devices, scatter_sum(): lax.all_to_all(values, axis, 0, 0, axis_index_groups=groups, tiled=True)  5.47 us
  transfers between devices with their start and end apart: 7, of which 4 were waited for; matrix products, arithmetic and copies ran while one was open for 0% of the time, Pallas kernels for 3%

profile of v7, /device:TPU:1, one launch (start us, length us, event | category | flops | bytes accessed | tf_op | source)
XLA Modules:
  0.0 221.1 jit_solution(10274958079720937575)
XLA Ops:
  0.6 3.4 %shard_map.67 = (f32[256,896]{1,0:T(8,128)}, f32[256,256]{1,0:T(8,128)}) custom-call(f32[256,896]{1,0:T(8,128)} %momentum_ref.1, bf16[256,896]{1,0:T(8,128)(2,1)} %gradient_ref.1, f32[896,256]{1,0:T(8,128)} %basis_ref), custom_call_target="tpu_custom_call" | custom-call | flops 704643072 | bytes 917504 | tf_op jit(solution)/shard_map/pallas_call | solution.py:346
  4.1 29.0 %all_to_all.61 = f32[16,16,256]{2,1,0:T(8,128)S(1)} all-to-all(f32[16,16,256]{2,1,0:T(8,128)} %bitcast.29), channel_id=1, replica_groups=mesh['mp'=32,'dp'=16] {'dp'}, dimensions={0} | all-to-all | bytes 524288 | tf_op jit(solution)/shard_map/all_to_all | solution.py:308
  33.1 23.8 %all_to_all.62 = f32[16,16,256]{2,1,0:T(8,128)S(1)} all-to-all(f32[16,16,256]{2,1,0:T(8,128)S(1)} %broadcast_in_dim.8), channel_id=1, replica_groups=mesh['mp'=32,'dp'=16] {'dp'}, dimensions={0} | all-to-all | bytes 524288 | tf_op jit(solution)/shard_map/all_to_all | solution.py:314
  58.3 8.3 %collective-permute-start = (f32[128,1152]{1,0:T(8,128)S(1)}, f32[128,1152]{1,0:T(8,128)S(1)}, u32[]{:S(2)}, u32[]{:S(2)}) collective-permute-start(f32[128,1152]{1,0:T(8,128)S(1)} %constant_dynamic-slice_fusion), channel_id=1, source_target_pairs={{0,16},{16,0},{32,48},{48,32},{64,80},{80,64},{96,112},{112,96},{1... | collective-permute-start | bytes 1769480 | tf_op jit(solution)/shard_map/ppermute | solution.py:323
  66.5 1.9 collective-permute-start.1
  68.5 17.9 %all_to_all.63 = f32[16,8,1152]{2,1,0:T(8,128)S(1)} all-to-all(f32[16,8,1152]{2,1,0:T(8,128)S(1)} %add_bitcast_fusion), channel_id=1, replica_groups={{0,32,64,96,128,160,192,224,256,288,320,352,384,416,448,480},{16,48,80,..., dimensions={0} | all-to-all | bytes 1179648 | tf_op jit(solution)/shard_map/all_to_all | solution.py:308
  86.5 13.8 %all_to_all.64 = f32[16,8,1152]{2,1,0:T(8,128)S(1)} all-to-all(f32[16,8,1152]{2,1,0:T(8,128)S(1)} %broadcast_in_dim.9), channel_id=1, replica_groups={{0,32,64,96,128,160,192,224,256,288,320,352,384,416,448,480},{16,48,80,..., dimensions={0} | all-to-all | bytes 1179648 | tf_op jit(solution)/shard_map/all_to_all | solution.py:314
  100.3 4.6 %collective-permute-start.2 = (f32[128,1152]{1,0:T(8,128)S(1)}, f32[128,1152]{1,0:T(8,128)S(1)}, u32[]{:S(2)}, u32[]{:S(2)}) collective-permute-start(f32[128,1152]{1,0:T(8,128)S(1)} %bitcast.17), channel_id=1, source_target_pairs={{0,16},{16,0},{32,48},{48,32},{64,80},{80,64},{96,112},{112,96},{1... | collective-permute-start | bytes 1769480 | tf_op jit(solution)/shard_map/ppermute | solution.py:323
  104.9 2.1 shard_map.69
  107.0 6.6 %shard_map.70.early_ref = f32[256,256]{1,0:T(8,128)S(1)} custom-call(s32[1]{0:T(128)} %bitcast.core_ref, f32[128,1152]{1,0:T(8,128)S(1)} %bitcast.19, f32[128,1152]{1,0:T(8,128)S(1)} %collective-permute-done.2.other_ref), custom_call_target="tpu_custom_call" | custom-call | flops 704643072 | bytes 917504 | tf_op jit(solution)/shard_map/pallas_call | solution.py:361
  113.5 5.5 %all-to-all-start.4 = ((f32[16,32,128]{2,1,0:T(8,128)}), f32[16,32,128]{2,1,0:T(8,128)}, u32[]{:S(2)}, u32[]{:S(2)}) async-start(f32[16,32,128]{2,1,0:T(8,128)} %bitcast.5), calls=%async_computation.4 | async-start | bytes 524288 | tf_op jit(solution)/shard_map/all_to_all | solution.py:308
  119.0 1.6 shard_map.71
  120.6 13.2 %all-to-all-done.4 = f32[16,32,128]{2,1,0:T(8,128)} async-done(((f32[16,32,128]{2,1,0:T(8,128)}), f32[16,32,128]{2,1,0:T(8,128)}, u32[]{:S(2)}, u32[]{:S(2)}) %all-to-all-start.4) | async-done | bytes 262176 | tf_op jit(solution)/shard_map/all_to_all | solution.py:308
  134.9 19.2 %all_to_all.65 = f32[16,17,2,128]{3,2,1,0:T(2,128)S(1)} all-to-all(f32[16,17,2,128]{3,2,1,0:T(2,128)S(1)} %broadcast_in_dim.10), channel_id=1, replica_groups=mesh['mp'=32,'dp'=16] {'dp'}, dimensions={0} | all-to-all | bytes 557056 | tf_op jit(solution)/shard_map/all_to_all | solution.py:314
  154.1 1.9 collective-permute-start.3
  157.5 2.7 %shard_map.72 = (f32[256,256]{1,0:T(8,128)S(1)}, f32[128,1152]{1,0:T(8,128)S(1)}) custom-call(s32[1]{0:T(128)} %bitcast.core_ref, f32[512,128]{1,0:T(8,128)S(1)} %bitcast.25, f32[512,128]{1,0:T(8,128)S(1)} %collective-permute-done.3.raw_other_ref, f32[256,256]{1,0:T(8,128)S(1)} %get-tuple-element.35.inverse_ref, f32[16,256]{1,0:T(8,128)S(1)} %bitcast.27, ...), custom_call_target="tpu_custom_call" | custom-call | flops 1127428864 | bytes 917504 | tf_op jit(solution)/shard_map/pallas_call | solution.py:373
  160.3 14.5 %all_to_all.66 = f32[16,8,1152]{2,1,0:T(8,128)S(1)} all-to-all(f32[16,8,1152]{2,1,0:T(8,128)S(1)} %bitcast.23), channel_id=1, replica_groups={{0,32,64,96,128,160,192,224,256,288,320,352,384,416,448,480},{16,48,80,..., dimensions={0} | all-to-all | bytes 1179648 | tf_op jit(solution)/shard_map/all_to_all | solution.py:308
  174.8 13.9 %all_to_all.67 = f32[16,8,1152]{2,1,0:T(8,128)S(1)} all-to-all(f32[16,8,1152]{2,1,0:T(8,128)S(1)} %broadcast_in_dim.11), channel_id=1, replica_groups={{0,32,64,96,128,160,192,224,256,288,320,352,384,416,448,480},{16,48,80,..., dimensions={0} | all-to-all | bytes 1179648 | tf_op jit(solution)/shard_map/all_to_all | solution.py:314
  188.7 4.5 %collective-permute-start.4 = (f32[128,1152]{1,0:T(8,128)S(1)}, f32[128,1152]{1,0:T(8,128)S(1)}, u32[]{:S(2)}, u32[]{:S(2)}) collective-permute-start(f32[128,1152]{1,0:T(8,128)S(1)} %bitcast.21), channel_id=1, source_target_pairs={{0,16},{16,0},{32,48},{48,32},{64,80},{80,64},{96,112},{112,96},{1... | collective-permute-start | bytes 1769480 | tf_op jit(solution)/shard_map/ppermute | solution.py:323
  194.7 8.3 %shard_map.73 = (f32[256,256]{1,0:T(8,128)S(1)}, f32[256,896]{1,0:T(8,128)S(1)}, f32[16,1,256]{2,1,0:T(1,128)}) custom-call(s32[1]{0:T(128)} %bitcast.core_ref, f32[128,1152]{1,0:T(8,128)S(1)} %bitcast.22, f32[128,1152]{1,0:T(8,128)S(1)} %collective-permute-done.4.other_ref), custom_call_target="tpu_custom_call" | custom-call | flops 5637144576 | bytes 917504 | tf_op jit(solution)/shard_map/pallas_call | solution.py:377
  202.9 5.0 %all-to-all-start.8 = ((f32[16,1,256]{2,1,0:T(1,128)}), f32[16,1,256]{2,1,0:T(1,128)S(1)}, u32[]{:S(2)}, u32[]{:S(2)}) async-start(f32[16,1,256]{2,1,0:T(1,128)} %get-tuple-element.41), calls=%async_computation.8 | async-start | bytes 32768 | tf_op jit(solution)/shard_map/all_to_all | solution.py:385
  207.9 2.2 %shard_map.74 = (f32[256,256]{1,0:T(8,128)S(1)}, f32[256,896]{1,0:T(8,128)}) custom-call(f32[256,256]{1,0:T(8,128)S(1)} %get-tuple-element.36.raw_ref, f32[256,256]{1,0:T(8,128)S(1)} %get-tuple-element.38.inverse_ref, f32[256,896]{1,0:T(8,128)S(1)} %get-tuple-element.39.right_ref, f32[256,896]{1,0:T(8,128)S(1)} %copy-done), custom_call_target="tpu_custom_call" | custom-call | flops 704643072 | bytes 917504 | tf_op jit(solution)/shard_map/pallas_call | solution.py:386
  210.1 9.1 %all-to-all-done.8.squares_ref = f32[16,1,256]{2,1,0:T(1,128)S(1)} async-done(((f32[16,1,256]{2,1,0:T(1,128)}), f32[16,1,256]{2,1,0:T(1,128)S(1)}, u32[]{:S(2)}, u32[]{:S(2)}) %all-to-all-start.8) | async-done | bytes 16416 | tf_op jit(solution)/shard_map/all_to_all | solution.py:385
  219.3 1.6 shard_map.75
  (24 shorter events, 5.5 us)
Async XLA Ops:
  4.1 52.9 %copy-start = (f32[256,896]{1,0:T(8,128)S(1)}, f32[256,896]{1,0:T(8,128)}, u32[]{:S(2)}) copy-start(f32[256,896]{1,0:T(8,128)} %get-tuple-element.27.buffer_ref) | copy-start | bytes 2752516
  58.3 10.2 %collective-permute-start = (f32[128,1152]{1,0:T(8,128)S(1)}, f32[128,1152]{1,0:T(8,128)S(1)}, u32[]{:S(2)}, u32[]{:S(2)}) collective-permute-start(f32[128,1152]{1,0:T(8,128)S(1)} %constant_dynamic-slice_fusion), channel_id=1, source_target_pairs={{0,16},{16,0},{32,48},{48,32},{64,80},{80,64},{96,112},{112,96},{1... | collective-permute-start | bytes 1769480 | tf_op jit(solution)/shard_map/ppermute | solution.py:323
  66.5 19.9 %collective-permute-start.1 = (f32[256,896]{1,0:T(8,128)S(1)}, f32[256,896]{1,0:T(8,128)S(1)}, u32[]{:S(2)}, u32[]{:S(2)}) collective-permute-start(f32[256,896]{1,0:T(8,128)S(1)} %copy-done), channel_id=1, source_target_pairs={{0,16},{16,0},{32,48},{48,32},{64,80},{80,64},{96,112},{112,96},{1... | collective-permute-start | bytes 2752520 | tf_op jit(solution)/shard_map/ppermute | solution.py:323
  100.3 6.7 %collective-permute-start.2 = (f32[128,1152]{1,0:T(8,128)S(1)}, f32[128,1152]{1,0:T(8,128)S(1)}, u32[]{:S(2)}, u32[]{:S(2)}) collective-permute-start(f32[128,1152]{1,0:T(8,128)S(1)} %bitcast.17), channel_id=1, source_target_pairs={{0,16},{16,0},{32,48},{48,32},{64,80},{80,64},{96,112},{112,96},{1... | collective-permute-start | bytes 1769480 | tf_op jit(solution)/shard_map/ppermute | solution.py:323
  113.5 20.3 %all-to-all-start.4 = ((f32[16,32,128]{2,1,0:T(8,128)}), f32[16,32,128]{2,1,0:T(8,128)}, u32[]{:S(2)}, u32[]{:S(2)}) async-start(f32[16,32,128]{2,1,0:T(8,128)} %bitcast.5), calls=%async_computation.4 | async-start | bytes 524288 | tf_op jit(solution)/shard_map/all_to_all | solution.py:308
  154.1 3.4 %collective-permute-start.3 = (f32[512,128]{1,0:T(8,128)S(1)}, f32[512,128]{1,0:T(8,128)S(1)}, u32[]{:S(2)}, u32[]{:S(2)}) collective-permute-start(f32[512,128]{1,0:T(8,128)S(1)} %bitcast.24), channel_id=1, source_target_pairs={{0,16},{16,0},{32,48},{48,32},{64,80},{80,64},{96,112},{112,96},{1... | collective-permute-start | bytes 786440 | tf_op jit(solution)/shard_map/ppermute | solution.py:323
  188.7 5.9 %collective-permute-start.4 = (f32[128,1152]{1,0:T(8,128)S(1)}, f32[128,1152]{1,0:T(8,128)S(1)}, u32[]{:S(2)}, u32[]{:S(2)}) collective-permute-start(f32[128,1152]{1,0:T(8,128)S(1)} %bitcast.21), channel_id=1, source_target_pairs={{0,16},{16,0},{32,48},{48,32},{64,80},{80,64},{96,112},{112,96},{1... | collective-permute-start | bytes 1769480 | tf_op jit(solution)/shard_map/ppermute | solution.py:323
  202.9 16.4 %all-to-all-start.8 = ((f32[16,1,256]{2,1,0:T(1,128)}), f32[16,1,256]{2,1,0:T(1,128)S(1)}, u32[]{:S(2)}, u32[]{:S(2)}) async-start(f32[16,1,256]{2,1,0:T(1,128)} %get-tuple-element.41), calls=%async_computation.8 | async-start | bytes 32768 | tf_op jit(solution)/shard_map/all_to_all | solution.py:385
  207.9 11.4 %copy-start.1 = (bf16[256,896]{1,0:T(8,128)(2,1)S(1)}, bf16[256,896]{1,0:T(8,128)(2,1)}, u32[]{:S(2)}) copy-start(bf16[256,896]{1,0:T(8,128)(2,1)} %weight_ref.1) | copy-start | bytes 1376260

commit v8 on v7

--- a/solution.py
+++ b/solution.py
@@ -176,11 +176,15 @@
     left_ref[...] = product(buffer, basis_ref[...])
 
 
-def sums_kernel(left_ref, buffer_ref, out_ref):
+def sums_kernel(core_ref, left_ref, buffer_ref, own_ref, other_ref):
+    first_core = core_ref[0] == 0
     left = left_ref[...]
     turned = left.T
-    out_ref[:, :OWN_COLS] = product(turned, buffer_ref[...])
-    out_ref[:, OWN_COLS:] = product(turned, left)
+    for at, right in ((0, buffer_ref[...]), (OWN_COLS, left)):
+        columns = slice(at, at + right.shape[1])
+        sums = product(turned, right)
+        own_ref[:, columns] = jnp.where(first_core, sums[:HALF], sums[HALF:])
+        other_ref[:, columns] = jnp.where(first_core, sums[HALF:], sums[:HALF])
 
 
 def next_left_kernel(core_ref, half_ref, buffer_ref, other_ref, out_ref):
@@ -240,7 +244,8 @@
     mine, its = raw_ref[...], raw_other_ref[...]
     raw = jnp.concatenate([pick(mine, its), pick(its, mine)], axis=1)
     squares = jnp.sum(squares_ref[...], axis=0, keepdims=True)
-    left = outer_rows(raw, inverse_ref[...]) / (jnp.sqrt(squares) + norm_eps)
+    norms = as_column(jnp.sqrt(squares) + norm_eps)
+    left = outer_rows(raw, inverse_ref[...] / norms)
     left_ref[...] = pick(left[:OWN_ROWS], left[OWN_ROWS:])
     turned = pick(left[:, :HALF], left[:, HALF:]).T
     early, late = turned[:, :OWN_ROWS], turned[:, OWN_ROWS:]
@@ -332,25 +337,17 @@
     scalar = pl.BlockSpec(memory_space=pltpu.SMEM)
     vector = pl.BlockSpec(memory_space=pltpu.VMEM)
 
-    core = (lax.axis_index("mp") % 2).astype(jnp.uint32)
-    own_start, other_start, zero, core, right_basis = lax.optimization_barrier(
-        (
-            core * HALF,
-            HALF - core * HALF,
-            core * 0,
-            core.astype(jnp.int32).reshape(1),
-            right_basis,
-        )
-    )
+    core = (lax.axis_index("mp") % 2).reshape(1)
+    core, right_basis = lax.optimization_barrier((core, right_basis))
 
     buffer, left = call(first_kernel, 1, block, (OWN_ROWS, RANK), vmem=60)(
         momentum, gradient, right_basis
     )
     buffer_other = with_other_core(buffer)
     left = gather(scatter_sum(left, "dp", DP), "dp", DP).reshape(OWN_ROWS, RANK)
-    sums = call(sums_kernel, 1.3, (RANK, width))(left, buffer)
-    half = lax.dynamic_slice(sums, (own_start, zero), (HALF, width))
-    other = lax.dynamic_slice(sums, (other_start, zero), (HALF, width))
+    half, other = call(
+        sums_kernel, 1.3, (HALF, width), (HALF, width), in_specs=[scalar, vector, vector]
+    )(core, left, buffer)
     half = scatter_sum(half + with_other_core(other), "mp", MP // 2, SAME_CORE)
     half, buffer_other = lax.optimization_barrier((half, buffer_other))
     half = gather(half, "mp", MP // 2, SAME_CORE).reshape(HALF, width)

time: 222 us -> 222 us (level)
  no operation moved by 1% of the time
where the time goes in v8:
time: 222 us; the launch traced here: 221 us
  blocking collectives  132 us (59%)
  starting transfers between devices  31.7 us (14%)
  Pallas kernels  29.9 us (13%)
  waiting for transfers between devices  25.2 us (11%)
    all_to_all x4, blocking collectives, gather(): lax.all_to_all(copies, axis, 0, 0, axis_index_groups=groups, tiled=True)  70.7 us
    all_to_all x3, blocking collectives, scatter_sum(): lax.all_to_all(values, axis, 0, 0, axis_index_groups=groups, tiled=True)  61.3 us
    ppermute x5, starting transfers between devices, with_other_core(): return lax.ppermute(values, 'mp', CORE_PAIRS)  21.3 us
    all_to_all x1, waiting for transfers between devices, scatter_sum(): lax.all_to_all(values, axis, 0, 0, axis_index_groups=groups, tiled=True)  13.2 us
    all_to_all x1, waiting for transfers between devices, body(): squares = lax.all_to_all(own_squares, 'dp', 0, 0, tiled=True)  9.15 us
    pallas_call x1, Pallas kernels, body(): call(last_right_kernel, 8, square, wide, (DP, 1, RANK), in_specs=[scalar,...  8.26 us
    pallas_call x1, Pallas kernels, body(): call(early_factor_kernel, 1, square, in_specs=[scalar, vector, vector])  6.58 us
    all_to_all x1, starting transfers between devices, scatter_sum(): lax.all_to_all(values, axis, 0, 0, axis_index_groups=groups, tiled=True)  5.47 us
  transfers between devices with their start and end apart: 7, of which 4 were waited for; matrix products, arithmetic and copies ran while one was open for 0% of the time, Pallas kernels for 3%

profile of v8, /device:TPU:1, one launch (start us, length us, event | category | flops | bytes accessed | tf_op | source)
XLA Modules:
  0.0 221.2 jit_solution(7814504200253560884)
XLA Ops:
  0.6 3.4 %shard_map.67 = (f32[256,896]{1,0:T(8,128)}, f32[256,256]{1,0:T(8,128)}) custom-call(f32[256,896]{1,0:T(8,128)} %momentum_ref.1, bf16[256,896]{1,0:T(8,128)(2,1)} %gradient_ref.1, f32[896,256]{1,0:T(8,128)} %basis_ref), custom_call_target="tpu_custom_call" | custom-call | flops 704643072 | bytes 917504 | tf_op jit(solution)/shard_map/pallas_call | solution.py:343
  4.1 29.0 %all_to_all.61 = f32[16,16,256]{2,1,0:T(8,128)S(1)} all-to-all(f32[16,16,256]{2,1,0:T(8,128)} %bitcast.29), channel_id=1, replica_groups=mesh['mp'=32,'dp'=16] {'dp'}, dimensions={0} | all-to-all | bytes 524288 | tf_op jit(solution)/shard_map/all_to_all | solution.py:313
  33.1 23.8 %all_to_all.62 = f32[16,16,256]{2,1,0:T(8,128)S(1)} all-to-all(f32[16,16,256]{2,1,0:T(8,128)S(1)} %broadcast_in_dim.8), channel_id=1, replica_groups=mesh['mp'=32,'dp'=16] {'dp'}, dimensions={0} | all-to-all | bytes 524288 | tf_op jit(solution)/shard_map/all_to_all | solution.py:319
  58.2 8.3 %collective-permute-start = (f32[128,1152]{1,0:T(8,128)S(1)}, f32[128,1152]{1,0:T(8,128)S(1)}, u32[]{:S(2)}, u32[]{:S(2)}) collective-permute-start(f32[128,1152]{1,0:T(8,128)S(1)} %get-tuple-element.29), channel_id=1, source_target_pairs={{0,16},{16,0},{32,48},{48,32},{64,80},{80,64},{96,112},{112,96},{1... | collective-permute-start | bytes 1769480 | tf_op jit(solution)/shard_map/ppermute | solution.py:328
  66.5 1.9 collective-permute-start.1
  68.5 17.8 %all_to_all.63 = f32[16,8,1152]{2,1,0:T(8,128)S(1)} all-to-all(f32[16,8,1152]{2,1,0:T(8,128)S(1)} %add_bitcast_fusion), channel_id=1, replica_groups={{0,32,64,96,128,160,192,224,256,288,320,352,384,416,448,480},{16,48,80,..., dimensions={0} | all-to-all | bytes 1179648 | tf_op jit(solution)/shard_map/all_to_all | solution.py:313
  86.4 13.8 %all_to_all.64 = f32[16,8,1152]{2,1,0:T(8,128)S(1)} all-to-all(f32[16,8,1152]{2,1,0:T(8,128)S(1)} %broadcast_in_dim.9), channel_id=1, replica_groups={{0,32,64,96,128,160,192,224,256,288,320,352,384,416,448,480},{16,48,80,..., dimensions={0} | all-to-all | bytes 1179648 | tf_op jit(solution)/shard_map/all_to_all | solution.py:319
  100.2 4.6 %collective-permute-start.2 = (f32[128,1152]{1,0:T(8,128)S(1)}, f32[128,1152]{1,0:T(8,128)S(1)}, u32[]{:S(2)}, u32[]{:S(2)}) collective-permute-start(f32[128,1152]{1,0:T(8,128)S(1)} %bitcast.17), channel_id=1, source_target_pairs={{0,16},{16,0},{32,48},{48,32},{64,80},{80,64},{96,112},{112,96},{1... | collective-permute-start | bytes 1769480 | tf_op jit(solution)/shard_map/ppermute | solution.py:328
  104.8 2.1 shard_map.69
  106.9 6.6 %shard_map.70.early_ref = f32[256,256]{1,0:T(8,128)S(1)} custom-call(s32[1]{0:T(128)} %bitcast.core_ref, f32[128,1152]{1,0:T(8,128)S(1)} %bitcast.19, f32[128,1152]{1,0:T(8,128)S(1)} %collective-permute-done.2.other_ref), custom_call_target="tpu_custom_call" | custom-call | flops 704643072 | bytes 917504 | tf_op jit(solution)/shard_map/pallas_call | solution.py:358
  113.5 5.5 %all-to-all-start.4 = ((f32[16,32,128]{2,1,0:T(8,128)}), f32[16,32,128]{2,1,0:T(8,128)}, u32[]{:S(2)}, u32[]{:S(2)}) async-start(f32[16,32,128]{2,1,0:T(8,128)} %bitcast.5), calls=%async_computation.4 | async-start | bytes 524288 | tf_op jit(solution)/shard_map/all_to_all | solution.py:313
  118.9 1.6 shard_map.71
  120.5 13.2 %all-to-all-done.4 = f32[16,32,128]{2,1,0:T(8,128)} async-done(((f32[16,32,128]{2,1,0:T(8,128)}), f32[16,32,128]{2,1,0:T(8,128)}, u32[]{:S(2)}, u32[]{:S(2)}) %all-to-all-start.4) | async-done | bytes 262176 | tf_op jit(solution)/shard_map/all_to_all | solution.py:313
  134.8 19.2 %all_to_all.65 = f32[16,17,2,128]{3,2,1,0:T(2,128)S(1)} all-to-all(f32[16,17,2,128]{3,2,1,0:T(2,128)S(1)} %broadcast_in_dim.10), channel_id=1, replica_groups=mesh['mp'=32,'dp'=16] {'dp'}, dimensions={0} | all-to-all | bytes 557056 | tf_op jit(solution)/shard_map/all_to_all | solution.py:319
  154.0 1.9 collective-permute-start.3
  157.5 2.9 %shard_map.72 = (f32[256,256]{1,0:T(8,128)S(1)}, f32[128,1152]{1,0:T(8,128)S(1)}) custom-call(s32[1]{0:T(128)} %bitcast.core_ref, f32[512,128]{1,0:T(8,128)S(1)} %bitcast.25, f32[512,128]{1,0:T(8,128)S(1)} %collective-permute-done.3.raw_other_ref, f32[256,256]{1,0:T(8,128)S(1)} %get-tuple-element.35.inverse_ref, f32[16,256]{1,0:T(8,128)S(1)} %bitcast.27, ...), custom_call_target="tpu_custom_call" | custom-call | flops 1127428864 | bytes 917504 | tf_op jit(solution)/shard_map/pallas_call | solution.py:370
  160.4 14.5 %all_to_all.66 = f32[16,8,1152]{2,1,0:T(8,128)S(1)} all-to-all(f32[16,8,1152]{2,1,0:T(8,128)S(1)} %bitcast.23), channel_id=1, replica_groups={{0,32,64,96,128,160,192,224,256,288,320,352,384,416,448,480},{16,48,80,..., dimensions={0} | all-to-all | bytes 1179648 | tf_op jit(solution)/shard_map/all_to_all | solution.py:313
  174.9 13.9 %all_to_all.67 = f32[16,8,1152]{2,1,0:T(8,128)S(1)} all-to-all(f32[16,8,1152]{2,1,0:T(8,128)S(1)} %broadcast_in_dim.11), channel_id=1, replica_groups={{0,32,64,96,128,160,192,224,256,288,320,352,384,416,448,480},{16,48,80,..., dimensions={0} | all-to-all | bytes 1179648 | tf_op jit(solution)/shard_map/all_to_all | solution.py:319
  188.8 4.5 %collective-permute-start.4 = (f32[128,1152]{1,0:T(8,128)S(1)}, f32[128,1152]{1,0:T(8,128)S(1)}, u32[]{:S(2)}, u32[]{:S(2)}) collective-permute-start(f32[128,1152]{1,0:T(8,128)S(1)} %bitcast.21), channel_id=1, source_target_pairs={{0,16},{16,0},{32,48},{48,32},{64,80},{80,64},{96,112},{112,96},{1... | collective-permute-start | bytes 1769480 | tf_op jit(solution)/shard_map/ppermute | solution.py:328
  194.7 8.3 %shard_map.73 = (f32[256,256]{1,0:T(8,128)S(1)}, f32[256,896]{1,0:T(8,128)S(1)}, f32[16,1,256]{2,1,0:T(1,128)}) custom-call(s32[1]{0:T(128)} %bitcast.core_ref, f32[128,1152]{1,0:T(8,128)S(1)} %bitcast.22, f32[128,1152]{1,0:T(8,128)S(1)} %collective-permute-done.4.other_ref), custom_call_target="tpu_custom_call" | custom-call | flops 5637144576 | bytes 917504 | tf_op jit(solution)/shard_map/pallas_call | solution.py:374
  203.0 5.0 %all-to-all-start.8 = ((f32[16,1,256]{2,1,0:T(1,128)}), f32[16,1,256]{2,1,0:T(1,128)S(1)}, u32[]{:S(2)}, u32[]{:S(2)}) async-start(f32[16,1,256]{2,1,0:T(1,128)} %get-tuple-element.41), calls=%async_computation.8 | async-start | bytes 32768 | tf_op jit(solution)/shard_map/all_to_all | solution.py:382
  208.0 2.2 %shard_map.74 = (f32[256,256]{1,0:T(8,128)S(1)}, f32[256,896]{1,0:T(8,128)}) custom-call(f32[256,256]{1,0:T(8,128)S(1)} %get-tuple-element.36.raw_ref, f32[256,256]{1,0:T(8,128)S(1)} %get-tuple-element.38.inverse_ref, f32[256,896]{1,0:T(8,128)S(1)} %get-tuple-element.39.right_ref, f32[256,896]{1,0:T(8,128)S(1)} %copy-done), custom_call_target="tpu_custom_call" | custom-call | flops 704643072 | bytes 917504 | tf_op jit(solution)/shard_map/pallas_call | solution.py:383
  210.2 9.1 %all-to-all-done.8.squares_ref = f32[16,1,256]{2,1,0:T(1,128)S(1)} async-done(((f32[16,1,256]{2,1,0:T(1,128)}), f32[16,1,256]{2,1,0:T(1,128)S(1)}, u32[]{:S(2)}, u32[]{:S(2)}) %all-to-all-start.8) | async-done | bytes 16416 | tf_op jit(solution)/shard_map/all_to_all | solution.py:382
  219.4 1.6 shard_map.75
  (23 shorter events, 5.5 us)
Async XLA Ops:
  4.1 52.9 %copy-start = (f32[256,896]{1,0:T(8,128)S(1)}, f32[256,896]{1,0:T(8,128)}, u32[]{:S(2)}) copy-start(f32[256,896]{1,0:T(8,128)} %get-tuple-element.27.buffer_ref) | copy-start | bytes 2752516
  58.2 10.2 %collective-permute-start = (f32[128,1152]{1,0:T(8,128)S(1)}, f32[128,1152]{1,0:T(8,128)S(1)}, u32[]{:S(2)}, u32[]{:S(2)}) collective-permute-start(f32[128,1152]{1,0:T(8,128)S(1)} %get-tuple-element.29), channel_id=1, source_target_pairs={{0,16},{16,0},{32,48},{48,32},{64,80},{80,64},{96,112},{112,96},{1... | collective-permute-start | bytes 1769480 | tf_op jit(solution)/shard_map/ppermute | solution.py:328
  66.5 19.9 %collective-permute-start.1 = (f32[256,896]{1,0:T(8,128)S(1)}, f32[256,896]{1,0:T(8,128)S(1)}, u32[]{:S(2)}, u32[]{:S(2)}) collective-permute-start(f32[256,896]{1,0:T(8,128)S(1)} %copy-done), channel_id=1, source_target_pairs={{0,16},{16,0},{32,48},{48,32},{64,80},{80,64},{96,112},{112,96},{1... | collective-permute-start | bytes 2752520 | tf_op jit(solution)/shard_map/ppermute | solution.py:328
  100.2 6.7 %collective-permute-start.2 = (f32[128,1152]{1,0:T(8,128)S(1)}, f32[128,1152]{1,0:T(8,128)S(1)}, u32[]{:S(2)}, u32[]{:S(2)}) collective-permute-start(f32[128,1152]{1,0:T(8,128)S(1)} %bitcast.17), channel_id=1, source_target_pairs={{0,16},{16,0},{32,48},{48,32},{64,80},{80,64},{96,112},{112,96},{1... | collective-permute-start | bytes 1769480 | tf_op jit(solution)/shard_map/ppermute | solution.py:328
  113.5 20.3 %all-to-all-start.4 = ((f32[16,32,128]{2,1,0:T(8,128)}), f32[16,32,128]{2,1,0:T(8,128)}, u32[]{:S(2)}, u32[]{:S(2)}) async-start(f32[16,32,128]{2,1,0:T(8,128)} %bitcast.5), calls=%async_computation.4 | async-start | bytes 524288 | tf_op jit(solution)/shard_map/all_to_all | solution.py:313
  154.0 3.4 %collective-permute-start.3 = (f32[512,128]{1,0:T(8,128)S(1)}, f32[512,128]{1,0:T(8,128)S(1)}, u32[]{:S(2)}, u32[]{:S(2)}) collective-permute-start(f32[512,128]{1,0:T(8,128)S(1)} %bitcast.24), channel_id=1, source_target_pairs={{0,16},{16,0},{32,48},{48,32},{64,80},{80,64},{96,112},{112,96},{1... | collective-permute-start | bytes 786440 | tf_op jit(solution)/shard_map/ppermute | solution.py:328
  188.8 5.9 %collective-permute-start.4 = (f32[128,1152]{1,0:T(8,128)S(1)}, f32[128,1152]{1,0:T(8,128)S(1)}, u32[]{:S(2)}, u32[]{:S(2)}) collective-permute-start(f32[128,1152]{1,0:T(8,128)S(1)} %bitcast.21), channel_id=1, source_target_pairs={{0,16},{16,0},{32,48},{48,32},{64,80},{80,64},{96,112},{112,96},{1... | collective-permute-start | bytes 1769480 | tf_op jit(solution)/shard_map/ppermute | solution.py:328
  203.0 16.4 %all-to-all-start.8 = ((f32[16,1,256]{2,1,0:T(1,128)}), f32[16,1,256]{2,1,0:T(1,128)S(1)}, u32[]{:S(2)}, u32[]{:S(2)}) async-start(f32[16,1,256]{2,1,0:T(1,128)} %get-tuple-element.41), calls=%async_computation.8 | async-start | bytes 32768 | tf_op jit(solution)/shard_map/all_to_all | solution.py:382
  208.0 11.4 %copy-start.1 = (bf16[256,896]{1,0:T(8,128)(2,1)S(1)}, bf16[256,896]{1,0:T(8,128)(2,1)}, u32[]{:S(2)}) copy-start(bf16[256,896]{1,0:T(8,128)(2,1)} %weight_ref.1) | copy-start | bytes 1376260
